TPU v7x, 32 devices: a whole 2x2x4 slice. The times are simulated.
32 devices in a mesh: ctx: 2 (over y), ep: 16 (over z, x, core).
Axes of the slice: x: 2, y: 2, z: 4, core: 2. Of those that a mesh axis runs over, the one named last changes fastest.
Arguments:
- queries: bfloat16 [256, 73728], P('ctx', 'ep'), may hold values from -12 to 12
- latent: bfloat16 [256, 576], P('ctx'), may hold values from -5 to 5
- doc_ids: int32 [256], replicated, may hold values from 0 to 3, never falling along the last dimension, each value on 1 to 128 neighbouring positions
- w_uv: bfloat16 [128, 512, 128], P('ep'), may hold values from -0.75 to 0.75
- w_out: bfloat16 [16384, 7168], P('ep', 'ctx'), may hold values from -0.046875 to 0.046875
- hidden_in: bfloat16 [256, 7168], P('ep', 'ctx'), may hold values from -24 to 24
- norm_gain: float32 [7168], P('ctx'), may hold values from 0.5 to 1.5
- route_ids: int32 [256, 8], P('ep'), may hold values from 0 to 15, all different within a row; in each aligned block of 16 rows (0 to 15, 16 to 31, ...) at most 9 rows name the same one
- route_weights: float32 [256, 8], P('ep'), may hold values from 0.1 to 1
- w_gate: bfloat16 [16, 7168, 1024], P('ep', 'ctx'), may hold values from -0.0625 to 0.0625
- w_up: bfloat16 [16, 7168, 1024], P('ep', 'ctx'), may hold values from -0.0625 to 0.0625
- w_down: bfloat16 [16, 1024, 7168], P('ep', None, 'ctx'), may hold values from -0.1875 to 0.1875
Outputs:
- layer_output: bfloat16 [256, 7168], P('ep', 'ctx')
Inputs may be any that keep to these rules, and one draw needn't show every extreme that they name: `doc_ids`: document numbers never fall along the sequence; a document has at most 128 tokens, and one has exactly that many. `route_ids`: each token names 8 different experts; among the 16 tokens of one index of ep no expert is named by more than 9 tokens, a bound that some block reaches.
All inputs are finite; a program needn't handle non-finite values.
Results may differ from a plain program's by a relative error of at most 0.014.
Values may be sent and summed in bfloat16 or wider, within the bound.
No kernel may reach another device: no remote copies, remote signals or barrier semaphores. Data moves between devices by JAX's collectives and lax.ppermute only.
A program may use at most 64 MiB of HBM per device.

v0:
```python
import math

import jax
import jax.numpy as jnp
from jax import lax
from jax.sharding import PartitionSpec as P

D = 7168
KVL = 512


score_scale = (1.0 + 0.1 * math.log(40.0)) ** 2 / math.sqrt(192.0)
masked_score = -1e30


def attend_group(state, query_block, query_first, keys, key_first, doc_ids):
    count = query_block.shape[0]
    key_count = keys.shape[0]
    running_max, running_total, running_sum = state

    def update(unused):
        scores = (
            jnp.einsum("nhc,kc->hnk", query_block, keys, preferred_element_type=jnp.float32)
            * score_scale
        )
        query_pos = query_first + jnp.arange(count, dtype=jnp.int32)
        key_pos = jnp.arange(key_count, dtype=jnp.int32)
        query_doc = lax.dynamic_slice_in_dim(doc_ids, query_first, count)
        allowed = (key_pos[None, :] <= query_pos[:, None]) & (
            doc_ids[None, :] == query_doc[:, None]
        )
        scores = jnp.where(allowed[None], scores, masked_score)
        new_max = jnp.maximum(running_max, jnp.max(scores, axis=2))
        probs = jnp.where(allowed[None], jnp.exp(scores - new_max[:, :, None]), 0.0)
        new_total = jnp.sum(probs, axis=2)
        values = keys[:, :KVL]
        new_sum = jnp.einsum(
            "hnk,kc->hnc", probs.astype(jnp.bfloat16), values, preferred_element_type=jnp.float32
        )
        return (new_max, new_total, new_sum)

    return lax.cond(key_first > query_first + count - 1, lambda unused: state, update, 0)


def shards(
    queries,
    latent,
    doc_ids,
    w_uv,
    w_out,
    hidden_in,
    norm_gain,
    route_ids,
    route_weights,
    w_gate,
    w_up,
    w_down,
):
    ctx_rank = lax.axis_index("ctx")
    block_rows = queries.shape[0]
    head_count = w_uv.shape[0]
    key_width = latent.shape[1]
    heads_local = queries.reshape(block_rows, head_count, key_width)
    own_first = ctx_rank * block_rows
    groups = ((heads_local, own_first),)

    def start_state(query_block):
        count = query_block.shape[0]
        return (
            jnp.full((head_count, count), masked_score, jnp.float32),
            jnp.zeros((head_count, count), jnp.float32),
            jnp.zeros((head_count, count, KVL), jnp.float32),
        )

    def add_keys(states, keys, key_first):
        return tuple(
            (
                attend_group(state, group[0], group[1], keys, key_first, doc_ids)
                for state, group in zip(states, groups)
            )
        )

    initial = tuple((start_state(group[0]) for group in groups))
    states = add_keys(initial, lax.all_gather(latent, "ctx", axis=0, tiled=True), jnp.int32(0))
    context = jnp.concatenate(
        [(state[2] / state[1][:, :, None]).astype(jnp.bfloat16) for state in states], axis=1
    )
    head_values = jnp.einsum("hnc,hcv->nhv", context, w_uv, preferred_element_type=jnp.float32)
    head_values = head_values.reshape(block_rows, -1).astype(jnp.bfloat16)
    partial_value = jnp.dot(
        lax.all_gather(head_values, "ctx", axis=0, tiled=True),
        w_out,
        preferred_element_type=jnp.float32,
    )
    attended = lax.psum_scatter(
        partial_value.astype(jnp.bfloat16), "ep", scatter_dimension=0, tiled=True
    ).astype(jnp.float32)
    residual = hidden_in.astype(jnp.float32) + attended
    squares = lax.psum(jnp.sum(residual * residual, axis=1), "ctx")
    normed = (residual * lax.rsqrt(squares / D + 1e-06)[:, None] * norm_gain).astype(jnp.bfloat16)
    expert_count = lax.axis_size("ep")
    token_count = hidden_in.shape[0]
    top_count = route_ids.shape[1]
    capacity = min(token_count, max(2, token_count * top_count * 9 // (8 * expert_count)))
    pair_count = token_count * top_count
    flat_ids = route_ids.reshape(pair_count)
    chosen = (flat_ids[:, None] == jnp.arange(expert_count, dtype=jnp.int32)[None, :]).astype(
        jnp.bfloat16
    )
    pair_index = jnp.arange(pair_count, dtype=jnp.int32)
    earlier = (pair_index[:, None] > pair_index[None, :]).astype(jnp.bfloat16)
    before = jnp.dot(earlier, chosen, preferred_element_type=jnp.float32)
    slot = jnp.sum(before * chosen.astype(jnp.float32), axis=1).astype(jnp.int32)
    target = flat_ids * capacity + slot
    placing = (
        jnp.arange(expert_count * capacity, dtype=jnp.int32)[:, None] == target[None, :]
    ).astype(jnp.bfloat16)
    repeated = jnp.repeat(normed, top_count, axis=0)
    outgoing = jnp.dot(placing, repeated, preferred_element_type=jnp.float32).astype(jnp.bfloat16)
    outgoing = outgoing.reshape(expert_count, capacity, -1)
    arrived = lax.all_to_all(outgoing, "ep", split_axis=0, concat_axis=0, tiled=True)
    source_count, item_count, width = arrived.shape
    flat_rows = arrived.reshape(source_count * item_count, width)
    gate_part = jnp.dot(flat_rows, w_gate[0], preferred_element_type=jnp.float32)
    up_part = jnp.dot(flat_rows, w_up[0], preferred_element_type=jnp.float32)
    both = jnp.stack([gate_part, up_part], axis=1)
    both = lax.psum(both.astype(jnp.bfloat16), "ctx").astype(jnp.float32)
    activated = (jax.nn.silu(both[:, 0]) * both[:, 1]).astype(jnp.bfloat16)
    produced = jnp.dot(activated, w_down[0], preferred_element_type=jnp.float32).astype(
        jnp.bfloat16
    )
    processed = produced.reshape(source_count, item_count, -1)
    incoming = lax.all_to_all(processed, "ep", split_axis=0, concat_axis=0, tiled=True)
    gathered_rows = lax.dot_general(
        placing,
        incoming.reshape(expert_count * capacity, -1),
        (((0,), (0,)), ((), ())),
        preferred_element_type=jnp.float32,
    )
    mixture = jnp.sum(
        gathered_rows.reshape(token_count, top_count, -1) * route_weights[:, :, None], axis=1
    )
    return (residual + mixture).astype(jnp.bfloat16)


def solution(mesh):
    return jax.shard_map(
        shards,
        mesh=mesh,
        in_specs=(
            P("ctx", "ep"),
            P("ctx", None),
            P(),
            P("ep", None, None),
            P("ep", "ctx"),
            P("ep", "ctx"),
            P("ctx"),
            P("ep", None),
            P("ep", None),
            P("ep", "ctx", None),
            P("ep", "ctx", None),
            P("ep", None, "ctx"),
        ),
        out_specs=P("ep", "ctx"),
        check_vma=False,
    )
```

profile of v0, /device:TPU:0, one launch (start us, length us, event | category | flops | bytes accessed | tf_op | source)
XLA Modules:
  0.0 254.5 jit_solution(7878341464850382552)
XLA Ops:
  6.5 1.1 copy.24
  7.7 7.8 %all_gather.6 = bf16[256,576]{1,0:T(8,128)(2,1)S(1)} all-gather(bf16[128,576]{1,0:T(8,128)(2,1)S(1)} %copy.24), channel_id=1, replica_groups=mesh['ctx'=2,'ep'=16] {'ctx'}, dimensions={0}, use_global_device_ids=true | all-gather | bytes 442368 | tf_op jit(solution)/shard_map/all_gather | solution.py:84
  15.5 4.5 %conditional.1 = (f32[8,128]{1,0:T(8,128)S(1)}, f32[8,128,512]{2,1,0:T(8,128)S(1)}) conditional(s32[]{:T(128)} %convert_element_type.65, (s32[]{:T(128)}, s32[256]{0:T(256)}, bf16[128,4608]{1,0:T(8,128)(2,1)}, bf16[256,576]{1,0:T(8,128)(2,1)S(1)}) %tuple.13, () %tuple.14), branch_computations={%region_0.3_spmd, %region_3.4_spmd} | conditional | flops 572882048 | bytes 9498170 | solution.py:42
  15.5 0.8 dynamic_slice.2
  16.3 0.8 fusion.12
  17.1 1.7 copy.25
  18.8 0.6 fusion.49
  19.4 0.5 fusion.4
  19.9 0.2 fusion.3
  20.1 0.6 convolution_convert_fusion.2
  20.7 8.2 %all_gather.7 = bf16[256,1024]{0,1:T(8,128)(2,1)S(1)} all-gather(bf16[128,1024]{0,1:T(8,128)(2,1)S(1)} %bitcast.56), channel_id=1, replica_groups=mesh['ctx'=2,'ep'=16] {'ctx'}, dimensions={0}, use_global_device_ids=true | all-gather | bytes 786432 | tf_op jit(solution)/shard_map/all_gather | solution.py:91
  28.9 6.5 %convolution_convert_fusion = bf16[256,3584]{1,0:T(8,128)(2,1)} fusion(bf16[256,1024]{0,1:T(8,128)(2,1)S(1)} %all_gather.7, bf16[1024,3584]{1,0:T(8,128)(2,1)} %param.18), kind=kOutput, calls=%fused_computation.24 | convolution fusion | flops 1879965696 | bytes 9699328 | tf_op jit(solution)/shard_map/dot_general | solution.py:90
  35.8 61.5 %reduce-scatter.2.cloned.1.call-done = bf16[16,3584]{1,0:T(8,128)(2,1)} async-done(((bf16[256,3584]{1,0:T(8,128)(2,1)}), bf16[16,3584]{1,0:T(8,128)(2,1)}) %reduce-scatter.2.cloned.1.call-update) | async-done | bytes 114704 | tf_op jit(solution)/shard_map/reduce_scatter | solution.py:95
  97.3 1.0 multiply_reduce_fusion
  98.4 4.9 %psum.14 = f32[16]{0:T(128)S(1)} all-reduce(f32[16]{0:T(128)S(1)} %multiply_reduce_fusion), channel_id=1, replica_groups=mesh['ctx'=2,'ep'=16] {'ctx'}, use_global_device_ids=true, to_apply=%region_7.8 | all-reduce | flops 16 | bytes 128 | tf_op jit(solution)/shard_map/psum | solution.py:99
  103.3 1.0 multiply_convert_fusion
  104.3 1.4 convolution_convert_fusion.1
  105.7 1.5 reshape.121
  107.2 46.4 %all_to_all.10 = bf16[16,9,3584]{2,1,0:T(8,128)(2,1)} all-to-all(bf16[16,9,3584]{2,1,0:T(8,128)(2,1)S(1)} %reshape.121), channel_id=1, replica_groups=mesh['ctx'=2,'ep'=16] {'ep'}, dimensions={0} | all-to-all | bytes 2064384 | tf_op jit(solution)/shard_map/all_to_all | solution.py:121
  153.6 1.7 reshape.122
  155.3 4.3 %fusion.30 = bf16[144,1,1024]{2,0,1:T(8,128)(2,1)S(1)} fusion(bf16[144,3584]{1,0:T(8,128)(2,1)S(1)} %reshape.122, bf16[1,3584,1024]{2,1,0:T(8,128)(2,1)} %param.24), kind=kOutput, calls=%fused_computation.33 | convolution fusion | flops 1057112064 | bytes 8667136 | tf_op jit(solution)/shard_map/dot_general | solution.py:125
  159.7 4.3 %fusion.33 = bf16[144,1,1024]{2,0,1:T(8,128)(2,1)S(1)} fusion(bf16[144,3584]{1,0:T(8,128)(2,1)S(1)} %reshape.122, bf16[1,3584,1024]{2,1,0:T(8,128)(2,1)} %param.23), kind=kOutput, calls=%fused_computation.34 | convolution fusion | flops 1057112064 | bytes 8667136 | tf_op jit(solution)/shard_map/dot_general | solution.py:124
  164.0 0.9 pad_maximum_fusion
  164.9 29.5 %all-reduce.2.cloned.1.call-done = bf16[144,2,1024]{2,0,1:T(8,128)(2,1)} async-done(((bf16[144,2,1024]{2,0,1:T(8,128)(2,1)}), bf16[144,2,1024]{2,0,1:T(8,128)(2,1)}) %all-reduce.2.cloned.1.call-update) | async-done | bytes 589840 | tf_op jit(solution)/shard_map/psum | solution.py:127
  194.4 1.2 convert_element_type.77
  195.6 4.4 %fusion.20 = bf16[144,3584]{1,0:T(8,128)(2,1)S(1)} fusion(bf16[1,1024,3584]{2,1,0:T(8,128)(2,1)} %param.25, f32[144,2,1024]{2,0,1:T(8,128)S(1)} %convert_element_type.77), kind=kOutput, calls=%fused_computation.26 | convolution fusion | flops 1058365440 | bytes 9551872 | tf_op jit(solution)/shard_map/dot_general | solution.py:129
  200.0 1.5 reshape.123
  201.5 5.8 %all-to-all-start.1 = ((bf16[16,9,3584]{2,1,0:T(8,128)(2,1)}), bf16[16,9,3584]{2,1,0:T(8,128)(2,1)S(1)}, u32[]{:S(2)}, u32[]{:S(2)}) async-start(bf16[16,9,3584]{2,1,0:T(8,128)(2,1)} %reshape.123), calls=%async_computation.2 | async-start | bytes 3670016 | tf_op jit(solution)/shard_map/all_to_all | solution.py:133
  207.3 36.5 %all-to-all-done.1 = bf16[16,9,3584]{2,1,0:T(8,128)(2,1)S(1)} async-done(((bf16[16,9,3584]{2,1,0:T(8,128)(2,1)}), bf16[16,9,3584]{2,1,0:T(8,128)(2,1)S(1)}, u32[]{:S(2)}, u32[]{:S(2)}) %all-to-all-start.1) | async-done | bytes 1032224 | tf_op jit(solution)/shard_map/all_to_all | solution.py:133
  243.8 1.3 reshape.127
  245.1 1.9 fusion.23
  247.0 0.7 add_convert_fusion
  (24 shorter events, 0.5 us)
Async XLA Ops:
  6.5 13.5 %copy-start = (bf16[8,512,128]{2,1,0:T(8,128)(2,1)S(1)}, bf16[8,512,128]{2,1,0:T(8,128)(2,1)}, u32[]{:S(2)}) copy-start(bf16[8,512,128]{2,1,0:T(8,128)(2,1)} %param.17) | copy-start | bytes 3145732
  6.5 90.8 %reduce-scatter.2.cloned.1.call-start = ((), (), s32[]{:S(2)}) async-start(), calls=%async_computation.3 | async-start | bytes 1949696 | tf_op jit(solution)/shard_map/reduce_scatter | solution.py:95
  28.9 6.5 %copy-start.4 = (s32[16,8]{0,1:T(8,128)S(1)}, s32[16,8]{0,1:T(8,128)}, u32[]{:S(2)}) copy-start(s32[16,8]{0,1:T(8,128)} %param.21) | copy-start | bytes 1540
  28.9 68.4 %copy-start.1 = (bf16[16,3584]{1,0:T(8,128)(2,1)S(1)}, bf16[16,3584]{1,0:T(8,128)(2,1)}, u32[]{:S(2)}) copy-start(bf16[16,3584]{1,0:T(8,128)(2,1)} %param.19) | copy-start | bytes 344068
  35.4 67.9 %copy-start.3 = (f32[3584]{0:T(1024)S(1)}, f32[3584]{0:T(1024)}, u32[]{:S(2)}) copy-start(f32[3584]{0:T(1024)} %param.20) | copy-start | bytes 43012
  35.4 159.0 %all-reduce.2.cloned.1.call-start = ((), (), s32[]{:S(2)}) async-start(), calls=%async_computation.4 | async-start | bytes 1179648 | tf_op jit(solution)/shard_map/psum | solution.py:127
  201.5 5.8 %copy-start.5 = (f32[16,8]{0,1:T(8,128)S(1)}, f32[16,8]{0,1:T(8,128)}, u32[]{:S(2)}) copy-start(f32[16,8]{0,1:T(8,128)} %param.22) | copy-start | bytes 1540
  201.5 42.3 %all-to-all-start.1 = ((bf16[16,9,3584]{2,1,0:T(8,128)(2,1)}), bf16[16,9,3584]{2,1,0:T(8,128)(2,1)S(1)}, u32[]{:S(2)}, u32[]{:S(2)}) async-start(bf16[16,9,3584]{2,1,0:T(8,128)(2,1)} %reshape.123), calls=%async_computation.2 | async-start | bytes 3670016 | tf_op jit(solution)/shard_map/all_to_all | solution.py:133
  207.3 39.7 %copy-start.2 = (bf16[16,3584]{1,0:T(8,128)(2,1)S(1)}, bf16[16,3584]{1,0:T(8,128)(2,1)}, u32[]{:S(2)}) copy-start(bf16[16,3584]{1,0:T(8,128)(2,1)} %reduce-scatter.2.cloned.1.call-done) | copy-start | bytes 344068
Sparse Core Ops, SparseCore 0:
  35.5 61.7 reduce-scatter.1
  165.0 29.3 all-reduce.1
where the time goes:
time: 260 us; the launch traced here: 255 us
  waiting for transfers between devices  128 us (49%)
  blocking collectives  67.3 us (26%)
  matrix products  24.8 us (10%)
  between operations  13.5 us (5%)
  local copies, waits for them, and re-layouts  9.8 us (4%)
  starting transfers between devices  5.8 us (2%)
  other arithmetic  5.76 us (2%)
    reduce_scatter x1, waiting for transfers between devices, shards(): lax.psum_scatter(partial_value.astype(jnp.bfloat16), 'ep', scatter_dimens...  61.5 us
    all_to_all x1, blocking collectives, shards(): lax.all_to_all(outgoing, 'ep', split_axis=0, concat_axis=0, tiled=True)  46.4 us
    all_to_all x1, waiting for transfers between devices, shards(): lax.all_to_all(processed, 'ep', split_axis=0, concat_axis=0, tiled=True)  36.5 us
    psum x1, waiting for transfers between devices, shards(): both = lax.psum(both.astype(jnp.bfloat16), 'ctx').astype(jnp.float32)  29.5 us
    all_gather x1, blocking collectives, shards(): lax.all_gather(head_values, 'ctx', axis=0, tiled=True)  8.2 us
    all_gather x1, blocking collectives, shards(): lax.all_gather(latent, 'ctx', axis=0, tiled=True)  7.82 us
    dot_general x1, matrix products, shards(): jnp.dot(lax.all_gather(head_values, 'ctx', axis=0, tiled=True), w_out, pr...  6.46 us
    all_to_all x1, starting transfers between devices, shards(): lax.all_to_all(processed, 'ep', split_axis=0, concat_axis=0, tiled=True)  5.75 us
  transfers between devices with their start and end apart: 3, of which 3 were waited for; matrix products, arithmetic and copies ran while one was open for 0% of the time, Pallas kernels for 0%

commit v1 on v0

v1 whole, which is shorter than its diff:
```python
import math

import jax
import jax.numpy as jnp
from jax import lax
from jax.sharding import PartitionSpec as P

D = 7168
KVL = 512


score_scale = (1.0 + 0.1 * math.log(40.0)) ** 2 / math.sqrt(192.0)
masked_score = -1e30
EXTRA = 128


def pairs(count, bit):
    return [(index, index ^ (1 << bit)) for index in range(count)]


def split_columns(array, parts):
    lanes = array.shape[-1] // 128
    edges = [lanes * part // parts * 128 for part in range(parts)] + [array.shape[-1]]
    return [array[..., low:high] for low, high in zip(edges[:-1], edges[1:]) if high > low]


def orders_of(bits):
    straight = list(range(bits))
    turned = [0] + straight[2:] + straight[1:2]
    return [straight, turned]


def opened(array, bits, bit):
    place = bits.index(bit)
    low, high = 1 << place, 1 << (len(bits) - 1 - place)
    return array.reshape((high, 2, low) + array.shape[1:])


def scatter_sum(parts, orders, count):
    bits = len(orders[0])
    states = [(part, list(range(bits))) for part in parts]
    for step in range(bits):
        following = []
        for (array, left), order in zip(states, orders):
            bit = order[step]
            both = opened(array, left, bit)
            shape = (-1,) + array.shape[1:]
            kept = both[:, 0].reshape(shape)
            got = lax.ppermute(both[:, 1].reshape(shape), "ep", pairs(count, bit))
            total = kept.astype(jnp.float32) + got.astype(jnp.float32)
            if step < bits - 1:
                total = total.astype(jnp.bfloat16)
            following.append((total, [other for other in left if other != bit]))
        states = following
    return jnp.concatenate([array[0] for array, left in states], axis=-1)


def gather_chunks(parts, orders, count):
    states = [(part[None], []) for part in parts]
    for step in range(len(orders[0])):
        following = []
        for (array, held), order in zip(states, orders):
            bit = order[-1 - step]
            got = lax.ppermute(array, "ep", pairs(count, bit))
            now = sorted(held + [bit])
            place = now.index(bit)
            low, high = 1 << place, 1 << (len(now) - 1 - place)
            shape = (high, low) + array.shape[1:]
            joined = jnp.stack([array.reshape(shape), got.reshape(shape)], axis=1)
            following.append((joined.reshape((-1,) + array.shape[1:]), now))
        states = following
    return [array for array, held in states]


def attend(heads_local, query_first, keys, key_first, doc_ids):
    count = heads_local.shape[0]
    key_count = keys.shape[0]
    scores = (
        jnp.einsum("nhc,kc->hnk", heads_local, keys, preferred_element_type=jnp.float32)
        * score_scale
    )
    query_pos = query_first + jnp.arange(count, dtype=jnp.int32)
    key_pos = key_first + jnp.arange(key_count, dtype=jnp.int32)
    query_doc = lax.dynamic_slice_in_dim(doc_ids, query_first, count)
    key_doc = jnp.sum(
        jnp.where(
            key_pos[:, None] == jnp.arange(doc_ids.shape[0], dtype=jnp.int32)[None, :],
            doc_ids[None, :] + 1,
            0,
        ),
        axis=1,
    )
    allowed = (key_pos[None, :] <= query_pos[:, None]) & (
        key_doc[None, :] == query_doc[:, None] + 1
    )
    scores = jnp.where(allowed[None], scores, masked_score)
    peak = jnp.max(scores, axis=2)
    probs = jnp.where(allowed[None], jnp.exp(scores - peak[:, :, None]), 0.0)
    total = jnp.sum(probs, axis=2)
    context = jnp.einsum(
        "hnk,kc->hnc",
        probs.astype(jnp.bfloat16),
        keys[:, :KVL],
        preferred_element_type=jnp.float32,
    )
    return (context / total[:, :, None]).astype(jnp.bfloat16)


def three_terms(values):
    first = values.astype(jnp.bfloat16)
    rest = values - first.astype(jnp.float32)
    second = rest.astype(jnp.bfloat16)
    third = (rest - second.astype(jnp.float32)).astype(jnp.bfloat16)
    return first, second, third


def shards(
    queries,
    latent,
    doc_ids,
    w_uv,
    w_out,
    hidden_in,
    norm_gain,
    route_ids,
    route_weights,
    w_gate,
    w_up,
    w_down,
):
    ctx_count = lax.axis_size("ctx")
    ep_count = lax.axis_size("ep")
    ctx_rank = lax.axis_index("ctx")
    ep_rank = lax.axis_index("ep")
    bits = ep_count.bit_length() - 1
    orders = orders_of(bits)
    block_rows = queries.shape[0]
    head_count = w_uv.shape[0]
    key_width = latent.shape[1]
    token_count = hidden_in.shape[0]
    top_count = route_ids.shape[1]
    all_tokens = ep_count * token_count
    heads_local = queries.reshape(block_rows, head_count, key_width)
    own_first = ctx_rank * block_rows
    swap = [(0, 1), (1, 0)]

    if ctx_count == 2:
        earlier_keys = lax.ppermute(latent, "ctx", [(0, 1)])
        keys = jnp.concatenate([earlier_keys, latent], axis=0)
        key_first = own_first - block_rows
    else:
        keys = lax.all_gather(latent, "ctx", axis=0, tiled=True)
        key_first = jnp.int32(0)
    context = attend(heads_local, own_first, keys, key_first, doc_ids)
    head_values = jnp.einsum("hnc,hcv->nhv", context, w_uv, preferred_element_type=jnp.float32)
    head_values = head_values.reshape(block_rows, -1).astype(jnp.bfloat16)

    chunk = jnp.arange(all_tokens, dtype=jnp.int32) // token_count
    source = ep_rank ^ chunk
    if ctx_count == 2:
        other = lax.ppermute(head_values, "ctx", swap)
        all_values = jnp.concatenate([head_values, other], axis=0)
        per_block = ep_count // 2
        source = source % per_block + per_block * (source // per_block != ctx_rank)
    else:
        all_values = lax.all_gather(head_values, "ctx", axis=0, tiled=True)
    row = source * token_count + jnp.arange(all_tokens, dtype=jnp.int32) % token_count
    ordering = (row[:, None] == jnp.arange(all_tokens, dtype=jnp.int32)[None, :]).astype(
        jnp.bfloat16
    )
    all_values = jnp.dot(ordering, all_values, preferred_element_type=jnp.float32).astype(
        jnp.bfloat16
    )
    partial_parts = [
        jnp.dot(all_values, part, preferred_element_type=jnp.float32)
        .astype(jnp.bfloat16)
        .reshape(ep_count, token_count, -1)
        for part in split_columns(w_out, len(orders))
    ]
    attended = scatter_sum(partial_parts, orders, ep_count)
    residual = hidden_in.astype(jnp.float32) + attended

    squares = jnp.sum(residual * residual, axis=1)
    gained = (residual * norm_gain).astype(jnp.bfloat16)
    experts = jnp.arange(ep_count, dtype=jnp.int32)
    named = route_ids[:, :, None] == experts[None, None, :]
    chosen = jnp.sum(named.astype(jnp.float32), axis=1)
    weights = jnp.sum(jnp.where(named, route_weights[:, :, None], 0.0), axis=1)
    token_index = jnp.arange(token_count, dtype=jnp.int32)
    before = (token_index[:, None] > token_index[None, :]).astype(jnp.float32)
    place = jnp.sum(before[:, :, None] * chosen[None, :, :], axis=1)
    place = jnp.where(chosen > 0, place, -1.0).astype(jnp.bfloat16)
    extra = [place, *three_terms(weights), *(term[:, None] for term in three_terms(squares))]
    extra_width = sum(part.shape[1] for part in extra)
    padded = -(-extra_width // EXTRA) * EXTRA
    extra.append(jnp.zeros((token_count, padded - extra_width), jnp.bfloat16))
    sent = split_columns(jnp.concatenate([gained, *extra], axis=1), len(orders))
    arrived = jnp.concatenate(gather_chunks(sent, orders, ep_count), axis=2)
    arrived = arrived.reshape(all_tokens, -1)
    width = gained.shape[1]
    features = arrived[:, :width]
    facts = arrived[:, width:].astype(jnp.float32)

    capacity = min(token_count, max(2, token_count * top_count * 9 // (8 * ep_count)))
    slots = ep_count * capacity
    mine = (experts == ep_rank).astype(jnp.float32)
    of_expert = [
        jnp.sum(facts[:, part * ep_count : (part + 1) * ep_count] * mine[None, :], axis=1)
        for part in range(4)
    ]
    token_place = of_expert[0].astype(jnp.int32)
    token_weight = of_expert[1] + of_expert[2] + of_expert[3]
    token_squares = jnp.sum(facts[:, 4 * ep_count : 4 * ep_count + 3], axis=1)
    if ctx_count == 2:
        token_squares = token_squares + lax.ppermute(token_squares, "ctx", swap)
    else:
        token_squares = lax.psum(token_squares, "ctx")
    token_scale = lax.rsqrt(token_squares / D + 1e-06)
    token_slot = jnp.where(token_place >= 0, chunk * capacity + token_place, -1)
    placing = jnp.arange(slots, dtype=jnp.int32)[:, None] == token_slot[None, :]
    slot_scale = jnp.sum(jnp.where(placing, token_scale[None, :], 0.0), axis=1)
    slot_weight = jnp.sum(jnp.where(placing, token_weight[None, :], 0.0), axis=1)
    placing = placing.astype(jnp.bfloat16)
    rows = jnp.dot(placing, features, preferred_element_type=jnp.float32).astype(jnp.bfloat16)
    both = jnp.concatenate(
        [
            jnp.dot(rows, w_gate[0], preferred_element_type=jnp.float32).astype(jnp.bfloat16),
            jnp.dot(rows, w_up[0], preferred_element_type=jnp.float32).astype(jnp.bfloat16),
        ],
        axis=1,
    )
    if ctx_count == 2:
        both = both.astype(jnp.float32) + lax.ppermute(both, "ctx", swap).astype(jnp.float32)
    else:
        both = lax.psum(both, "ctx").astype(jnp.float32)
    both = both * slot_scale[:, None]
    hidden = both.shape[1] // 2
    activated = (jax.nn.silu(both[:, :hidden]) * both[:, hidden:]).astype(jnp.bfloat16)
    returned = []
    for part in split_columns(w_down[0], len(orders)):
        produced = jnp.dot(activated, part, preferred_element_type=jnp.float32)
        produced = (produced * slot_weight[:, None]).astype(jnp.bfloat16)
        spread = lax.dot_general(
            placing, produced, (((0,), (0,)), ((), ())), preferred_element_type=jnp.float32
        )
        returned.append(spread.astype(jnp.bfloat16).reshape(ep_count, token_count, -1))
    mixture = scatter_sum(returned, orders, ep_count)
    return (residual + mixture).astype(jnp.bfloat16)


def solution(mesh):
    return jax.shard_map(
        shards,
        mesh=mesh,
        in_specs=(
            P("ctx", "ep"),
            P("ctx", None),
            P(),
            P("ep", None, None),
            P("ep", "ctx"),
            P("ep", "ctx"),
            P("ctx"),
            P("ep", None),
            P("ep", None),
            P("ep", "ctx", None),
            P("ep", "ctx", None),
            P("ep", None, "ctx"),
        ),
        out_specs=P("ep", "ctx"),
        check_vma=False,
    )
```

time: 260 us -> 129 us (0.50); the launches traced: 255 us -> 128 us
  waiting for transfers between devices: 128 us -> 58.8 us
  blocking collectives: 67.3 us -> 0 us
  starting transfers between devices: 5.8 us -> 38.9 us
  between operations: 13.5 us -> 0.61 us
  matrix products: 24.8 us -> 17.6 us
  local copies, waits for them, and re-layouts: 9.8 us -> 6.98 us
    reduce_scatter x1 -> x0, waiting for transfers between devices: 61.5 us -> none  [shards(): lax.psum_scatter(partial_value.astype(jnp.bfloat16), 'ep', scatter_dimens...]
    ppermute x0 -> x28, waiting for transfers between devices: none -> 58.8 us  [the longest x16 26.7 us: scatter_sum(): got = lax.ppermute(both[:, 1].reshape(shape), 'ep', pairs(count, bit))]
    all_to_all x1 -> x0, blocking collectives: 46.4 us -> none  [shards(): lax.all_to_all(outgoing, 'ep', split_axis=0, concat_axis=0, tiled=True)]
    ppermute x0 -> x28, starting transfers between devices: none -> 38.9 us  [the longest x16 21.5 us: scatter_sum(): got = lax.ppermute(both[:, 1].reshape(shape), 'ep', pairs(count, bit))]
    all_to_all x1 -> x0, waiting for transfers between devices: 36.5 us -> none  [shards(): lax.all_to_all(processed, 'ep', split_axis=0, concat_axis=0, tiled=True)]
    psum x1 -> x0, waiting for transfers between devices: 29.5 us -> none  [shards(): both = lax.psum(both.astype(jnp.bfloat16), 'ctx').astype(jnp.float32)]
    all_gather x2 -> x0, blocking collectives: 16 us -> none  [the longest x1 8.2 us: shards(): lax.all_gather(head_values, 'ctx', axis=0, tiled=True)]
    dot_general x9 -> x8, matrix products: 24.1 us -> 15.8 us  [the longest x2 6.35 us: shards(): jnp.dot(all_values, part, preferred_element_type=jnp.float32)]
  transfers between devices with their start and end apart: 3 -> 28, of which waited for: 3 -> 19; matrix products, arithmetic and copies ran while one was open for 0% -> 6% of each run, Pallas kernels for 0% -> 0%
where the time goes in v1:
time: 129 us; the launch traced here: 128 us
  waiting for transfers between devices  58.8 us (46%)
  starting transfers between devices  38.9 us (30%)
  matrix products  17.6 us (14%)
  local copies, waits for them, and re-layouts  6.98 us (5%)
  other arithmetic  5.29 us (4%)
    ppermute x16, waiting for transfers between devices, scatter_sum(): got = lax.ppermute(both[:, 1].reshape(shape), 'ep', pairs(count, bit))  26.7 us
    ppermute x16, starting transfers between devices, scatter_sum(): got = lax.ppermute(both[:, 1].reshape(shape), 'ep', pairs(count, bit))  21.5 us
    ppermute x1, waiting for transfers between devices, shards(): token_squares = token_squares + lax.ppermute(token_squares, 'ctx', swap)  13.2 us
    ppermute x8, waiting for transfers between devices, gather_chunks(): got = lax.ppermute(array, 'ep', pairs(count, bit))  11.6 us
    ppermute x8, starting transfers between devices, gather_chunks(): got = lax.ppermute(array, 'ep', pairs(count, bit))  9.77 us
    ppermute x1, waiting for transfers between devices, shards(): other = lax.ppermute(head_values, 'ctx', swap)  7.31 us
    dot_general x2, matrix products, shards(): jnp.dot(all_values, part, preferred_element_type=jnp.float32)  6.35 us
    dot_general x2, matrix products, shards(): lax.dot_general(placing, produced, (((0,), (0,)), ((), ())), preferred_el...  6.04 us
  transfers between devices with their start and end apart: 28, of which 19 were waited for; matrix products, arithmetic and copies ran while one was open for 6% of the time, Pallas kernels for 0%

profile of v1, /device:TPU:0, one launch (start us, length us, event | category | flops | bytes accessed | tf_op | source)
XLA Modules:
  0.0 128.2 jit_solution(16820495021905995612)
XLA Ops:
  0.0 5.0 %collective-permute-start = (bf16[128,576]{0,1:T(8,128)(2,1)}, bf16[128,576]{0,1:T(8,128)(2,1)S(1)}, u32[]{:S(2)}, u32[]{:S(2)}) collective-permute-start(bf16[128,576]{0,1:T(8,128)(2,1)} %param.13), channel_id=1, source_target_pairs={{0,16},{1,17},{2,18},{3,19},{4,20},{5,21},{6,22},{7,23},{8,24},{9,... | collective-permute-start | bytes 442376 | tf_op jit(solution)/shard_map/ppermute | solution.py:148
  6.5 1.8 %copy.100 = bf16[128,4608]{0,1:T(8,128)(2,1)S(1)} copy(bf16[128,4608]{1,0:T(8,128)(2,1)} %param.12) | data formatting | bytes 2359296 | tf_op args[0]
  13.8 7.3 %collective-permute-done.1 = bf16[128,1024]{0,1:T(8,128)(2,1)S(1)} collective-permute-done((bf16[128,1024]{0,1:T(8,128)(2,1)S(1)}, bf16[128,1024]{0,1:T(8,128)(2,1)S(1)}, u32[]{:S(2)}, u32[]{:S(2)}) %collective-permute-start.1) | collective-permute-done | bytes 262176 | tf_op jit(solution)/shard_map/ppermute | solution.py:161
  21.4 3.2 %fusion.13 = bf16[256,1792]{1,0:T(8,128)(2,1)S(1)} fusion(bf16[256,1024]{1,0:T(8,128)(2,1)S(1)} %convolution_convert_fusion.3, bf16[1024,3584]{1,0:T(8,128)(2,1)} %param.16), kind=kOutput, calls=%fused_computation.14 | convolution fusion | flops 939982848 | bytes 5111808 | tf_op jit(solution)/shard_map/dot_general | solution.py:175
  24.6 3.2 %fusion.16 = bf16[256,1792]{1,0:T(8,128)(2,1)S(1)} fusion(bf16[256,1024]{1,0:T(8,128)(2,1)S(1)} %convolution_convert_fusion.3, bf16[1024,3584]{1,0:T(8,128)(2,1)} %param.16), kind=kOutput, calls=%fused_computation.15 | convolution fusion | flops 939982848 | bytes 5111808 | tf_op jit(solution)/shard_map/dot_general | solution.py:175
  29.9 1.6 %collective-permute-start.7 = (bf16[4,16,1792]{2,1,0:T(8,128)(2,1)S(1)}, bf16[4,16,1792]{2,1,0:T(8,128)(2,1)S(1)}, u32[]{:S(2)}, u32[]{:S(2)}) collective-permute-start(bf16[4,16,1792]{2,1,0:T(8,128)(2,1)S(1)} %bitcast.290), channel_id=1, source_target_pairs={{0,4},{1,5},{2,6},{3,7},{4,0},{5,1},{6,2},{7,3},{8,12},{9,13},{10,... | collective-permute-start | bytes 688136 | tf_op jit(solution)/shard_map/ppermute | solution.py:49
  31.7 1.6 %collective-permute-start.3 = (bf16[4,16,1792]{2,1,0:T(8,128)(2,1)S(1)}, bf16[4,16,1792]{2,1,0:T(8,128)(2,1)S(1)}, u32[]{:S(2)}, u32[]{:S(2)}) collective-permute-start(bf16[4,16,1792]{2,1,0:T(8,128)(2,1)S(1)} %slice_bitcast_fusion.13), channel_id=1, source_target_pairs={{0,2},{1,3},{2,0},{3,1},{4,6},{5,7},{6,4},{7,5},{8,10},{9,11},{10,... | collective-permute-start | bytes 688136 | tf_op jit(solution)/shard_map/ppermute | solution.py:49
  33.2 4.4 %collective-permute-done.7 = bf16[4,16,1792]{2,1,0:T(8,128)(2,1)S(1)} collective-permute-done((bf16[4,16,1792]{2,1,0:T(8,128)(2,1)S(1)}, bf16[4,16,1792]{2,1,0:T(8,128)(2,1)S(1)}, u32[]{:S(2)}, u32[]{:S(2)}) %collective-permute-start.7) | collective-permute-done | bytes 229408 | tf_op jit(solution)/shard_map/ppermute | solution.py:49
  37.7 2.7 %collective-permute-start.8 = (bf16[2,16,1792]{2,1,0:T(8,128)(2,1)S(1)}, bf16[2,16,1792]{2,1,0:T(8,128)(2,1)S(1)}, u32[]{:S(2)}, u32[]{:S(2)}) collective-permute-start(bf16[2,16,1792]{2,1,0:T(8,128)(2,1)S(1)} %slice_bitcast_fusion.19), channel_id=1, source_target_pairs={{0,8},{1,9},{2,10},{3,11},{4,12},{5,13},{6,14},{7,15},{8,0},{9,1},... | collective-permute-start | bytes 344072 | tf_op jit(solution)/shard_map/ppermute | solution.py:49
  40.4 1.6 %collective-permute-start.4 = (bf16[2,16,1792]{2,1,0:T(8,128)(2,1)S(1)}, bf16[2,16,1792]{2,1,0:T(8,128)(2,1)S(1)}, u32[]{:S(2)}, u32[]{:S(2)}) collective-permute-start(bf16[2,16,1792]{2,1,0:T(8,128)(2,1)S(1)} %slice_bitcast_fusion.21), channel_id=1, source_target_pairs={{0,4},{1,5},{2,6},{3,7},{4,0},{5,1},{6,2},{7,3},{8,12},{9,13},{10,... | collective-permute-start | bytes 344072 | tf_op jit(solution)/shard_map/ppermute | solution.py:49
  42.0 3.4 %collective-permute-done.8 = bf16[2,16,1792]{2,1,0:T(8,128)(2,1)S(1)} collective-permute-done((bf16[2,16,1792]{2,1,0:T(8,128)(2,1)S(1)}, bf16[2,16,1792]{2,1,0:T(8,128)(2,1)S(1)}, u32[]{:S(2)}, u32[]{:S(2)}) %collective-permute-start.8) | collective-permute-done | bytes 114720 | tf_op jit(solution)/shard_map/ppermute | solution.py:49
  47.1 1.6 %collective-permute-start.5 = (bf16[1,16,1792]{2,1,0:T(8,128)(2,1)S(1)}, bf16[1,16,1792]{2,1,0:T(8,128)(2,1)S(1)}, u32[]{:S(2)}, u32[]{:S(2)}) collective-permute-start(bf16[1,16,1792]{2,1,0:T(8,128)(2,1)S(1)} %slice_bitcast_fusion.29), channel_id=1, source_target_pairs={{0,8},{1,9},{2,10},{3,11},{4,12},{5,13},{6,14},{7,15},{8,0},{9,1},... | collective-permute-start | bytes 172040 | tf_op jit(solution)/shard_map/ppermute | solution.py:49
  49.8 2.5 %collective-permute-done.5 = bf16[1,16,1792]{2,1,0:T(8,128)(2,1)S(1)} collective-permute-done((bf16[1,16,1792]{2,1,0:T(8,128)(2,1)S(1)}, bf16[1,16,1792]{2,1,0:T(8,128)(2,1)S(1)}, u32[]{:S(2)}, u32[]{:S(2)}) %collective-permute-start.5) | collective-permute-done | bytes 57376 | tf_op jit(solution)/shard_map/ppermute | solution.py:49
  52.8 1.7 %collective-permute-start.14 = (bf16[1,16,1792]{2,1,0:T(8,128)(2,1)S(1)}, bf16[1,16,1792]{2,1,0:T(8,128)(2,1)S(1)}, u32[]{:S(2)}, u32[]{:S(2)}) collective-permute-start(bf16[1,16,1792]{2,1,0:T(8,128)(2,1)S(1)} %get-tuple-element.30), channel_id=1, source_target_pairs={{0,8},{1,9},{2,10},{3,11},{4,12},{5,13},{6,14},{7,15},{8,0},{9,1},... | collective-permute-start | bytes 172040 | tf_op jit(solution)/shard_map/ppermute | solution.py:64
  55.1 2.9 %collective-permute-done.14 = bf16[1,16,1792]{2,1,0:T(8,128)(2,1)S(1)} collective-permute-done((bf16[1,16,1792]{2,1,0:T(8,128)(2,1)S(1)}, bf16[1,16,1792]{2,1,0:T(8,128)(2,1)S(1)}, u32[]{:S(2)}, u32[]{:S(2)}) %collective-permute-start.14) | collective-permute-done | bytes 57376 | tf_op jit(solution)/shard_map/ppermute | solution.py:64
  59.4 3.0 %collective-permute-start.11 = (bf16[2,16,1920]{2,1,0:T(8,128)(2,1)S(1)}, bf16[2,16,1920]{2,1,0:T(8,128)(2,1)S(1)}, u32[]{:S(2)}, u32[]{:S(2)}) collective-permute-start(bf16[2,16,1920]{2,1,0:T(8,128)(2,1)S(1)} %get-tuple-element.24), channel_id=1, source_target_pairs={{0,8},{1,9},{2,10},{3,11},{4,12},{5,13},{6,14},{7,15},{8,0},{9,1},... | collective-permute-start | bytes 368648 | tf_op jit(solution)/shard_map/ppermute | solution.py:64
  63.6 2.5 %collective-permute-done.11 = bf16[2,16,1920]{2,1,0:T(8,128)(2,1)S(1)} collective-permute-done((bf16[2,16,1920]{2,1,0:T(8,128)(2,1)S(1)}, bf16[2,16,1920]{2,1,0:T(8,128)(2,1)S(1)}, u32[]{:S(2)}, u32[]{:S(2)}) %collective-permute-start.11) | collective-permute-done | bytes 122912 | tf_op jit(solution)/shard_map/ppermute | solution.py:64
  66.1 2.5 %collective-permute-start.12 = (bf16[4,16,1920]{2,1,0:T(8,128)(2,1)S(1)}, bf16[4,16,1920]{2,1,0:T(8,128)(2,1)S(1)}, u32[]{:S(2)}, u32[]{:S(2)}) collective-permute-start(bf16[4,16,1920]{2,1,0:T(8,128)(2,1)S(1)} %bitcast.288), channel_id=1, source_target_pairs={{0,4},{1,5},{2,6},{3,7},{4,0},{5,1},{6,2},{7,3},{8,12},{9,13},{10,... | collective-permute-start | bytes 737288 | tf_op jit(solution)/shard_map/ppermute | solution.py:64
  69.2 3.6 %collective-permute-done.12 = bf16[4,16,1920]{2,1,0:T(8,128)(2,1)S(1)} collective-permute-done((bf16[4,16,1920]{2,1,0:T(8,128)(2,1)S(1)}, bf16[4,16,1920]{2,1,0:T(8,128)(2,1)S(1)}, u32[]{:S(2)}, u32[]{:S(2)}) %collective-permute-start.12) | collective-permute-done | bytes 245792 | tf_op jit(solution)/shard_map/ppermute | solution.py:64
  73.1 1.7 %collective-permute-done.13 = bf16[8,16,1920]{2,1,0:T(8,128)(2,1)S(1)} collective-permute-done((bf16[8,16,1920]{2,1,0:T(8,128)(2,1)S(1)}, bf16[8,16,1920]{2,1,0:T(8,128)(2,1)S(1)}, u32[]{:S(2)}, u32[]{:S(2)}) %collective-permute-start.13) | collective-permute-done | bytes 491552 | tf_op jit(solution)/shard_map/ppermute | solution.py:64
  80.8 1.8 %collective-permute-start.19 = (f32[256]{0:T(256)S(1)}, f32[256]{0:T(256)S(1)}, u32[]{:S(2)}, u32[]{:S(2)}) collective-permute-start(f32[256]{0:T(256)S(1)} %slice_reduce_fusion), channel_id=1, source_target_pairs={{0,16},{16,0},{1,17},{17,1},{2,18},{18,2},{3,19},{19,3},{4,20},{20... | collective-permute-start | bytes 3080 | tf_op jit(solution)/shard_map/ppermute | solution.py:215
  82.6 13.2 %collective-permute-done.19 = f32[256]{0:T(256)S(1)} collective-permute-done((f32[256]{0:T(256)S(1)}, f32[256]{0:T(256)S(1)}, u32[]{:S(2)}, u32[]{:S(2)}) %collective-permute-start.19) | collective-permute-done | bytes 1056 | tf_op jit(solution)/shard_map/ppermute | solution.py:215
  96.4 3.0 %convolution_convert_fusion.2 = bf16[256,1792]{1,0:T(8,128)(2,1)S(1)} fusion(bf16[144,1024]{1,0:T(8,128)(2,1)S(1)} %fusion.54, bf16[1024,3584]{1,0:T(8,128)(2,1)} %bitcast.297, f32[144]{0:T(256)S(1)} %get-tuple-element.11, s32[256]{0:T(256)S(1)} %compare_select_fusion), kind=kOutput, calls=%fused_computation.17 | convolution fusion | flops 661614592 | bytes 4884032 | tf_op jit(solution)/shard_map/dot_general | solution.py:243
  99.4 3.0 %convolution_convert_fusion.1 = bf16[256,1792]{1,0:T(8,128)(2,1)S(1)} fusion(bf16[144,1024]{1,0:T(8,128)(2,1)S(1)} %fusion.54, bf16[1024,3584]{1,0:T(8,128)(2,1)} %bitcast.298, f32[144]{0:T(256)S(1)} %get-tuple-element.11, s32[256]{0:T(256)S(1)} %compare_select_fusion), kind=kOutput, calls=%fused_computation.16 | convolution fusion | flops 661614592 | bytes 4884032 | tf_op jit(solution)/shard_map/dot_general | solution.py:243
  105.1 2.1 %collective-permute-start.25 = (bf16[4,16,1792]{2,1,0:T(8,128)(2,1)S(1)}, bf16[4,16,1792]{2,1,0:T(8,128)(2,1)S(1)}, u32[]{:S(2)}, u32[]{:S(2)}) collective-permute-start(bf16[4,16,1792]{2,1,0:T(8,128)(2,1)S(1)} %bitcast.292), channel_id=1, source_target_pairs={{0,4},{1,5},{2,6},{3,7},{4,0},{5,1},{6,2},{7,3},{8,12},{9,13},{10,... | collective-permute-start | bytes 688136 | tf_op jit(solution)/shard_map/ppermute | solution.py:49
  107.2 4.9 %collective-permute-done.21 = bf16[4,16,1792]{2,1,0:T(8,128)(2,1)S(1)} collective-permute-done((bf16[4,16,1792]{2,1,0:T(8,128)(2,1)S(1)}, bf16[4,16,1792]{2,1,0:T(8,128)(2,1)S(1)}, u32[]{:S(2)}, u32[]{:S(2)}) %collective-permute-start.21) | collective-permute-done | bytes 229408 | tf_op jit(solution)/shard_map/ppermute | solution.py:49
  112.2 2.1 %collective-permute-start.22 = (bf16[2,16,1792]{2,1,0:T(8,128)(2,1)S(1)}, bf16[2,16,1792]{2,1,0:T(8,128)(2,1)S(1)}, u32[]{:S(2)}, u32[]{:S(2)}) collective-permute-start(bf16[2,16,1792]{2,1,0:T(8,128)(2,1)S(1)} %slice_bitcast_fusion.17), channel_id=1, source_target_pairs={{0,4},{1,5},{2,6},{3,7},{4,0},{5,1},{6,2},{7,3},{8,12},{9,13},{10,... | collective-permute-start | bytes 344072 | tf_op jit(solution)/shard_map/ppermute | solution.py:49
  114.4 1.6 %collective-permute-start.26 = (bf16[2,16,1792]{2,1,0:T(8,128)(2,1)S(1)}, bf16[2,16,1792]{2,1,0:T(8,128)(2,1)S(1)}, u32[]{:S(2)}, u32[]{:S(2)}) collective-permute-start(bf16[2,16,1792]{2,1,0:T(8,128)(2,1)S(1)} %slice_bitcast_fusion.15), channel_id=1, source_target_pairs={{0,8},{1,9},{2,10},{3,11},{4,12},{5,13},{6,14},{7,15},{8,0},{9,1},... | collective-permute-start | bytes 344072 | tf_op jit(solution)/shard_map/ppermute | solution.py:49
  116.0 1.9 %collective-permute-done.22 = bf16[2,16,1792]{2,1,0:T(8,128)(2,1)S(1)} collective-permute-done((bf16[2,16,1792]{2,1,0:T(8,128)(2,1)S(1)}, bf16[2,16,1792]{2,1,0:T(8,128)(2,1)S(1)}, u32[]{:S(2)}, u32[]{:S(2)}) %collective-permute-start.22) | collective-permute-done | bytes 114720 | tf_op jit(solution)/shard_map/ppermute | solution.py:49
  117.9 3.1 %collective-permute-start.23 = (bf16[1,16,1792]{2,1,0:T(8,128)(2,1)S(1)}, bf16[1,16,1792]{2,1,0:T(8,128)(2,1)S(1)}, u32[]{:S(2)}, u32[]{:S(2)}) collective-permute-start(bf16[1,16,1792]{2,1,0:T(8,128)(2,1)S(1)} %slice_bitcast_fusion.25), channel_id=1, source_target_pairs={{0,8},{1,9},{2,10},{3,11},{4,12},{5,13},{6,14},{7,15},{8,0},{9,1},... | collective-permute-start | bytes 172040 | tf_op jit(solution)/shard_map/ppermute | solution.py:49
  121.0 2.2 %collective-permute-done.26 = bf16[2,16,1792]{2,1,0:T(8,128)(2,1)S(1)} collective-permute-done((bf16[2,16,1792]{2,1,0:T(8,128)(2,1)S(1)}, bf16[2,16,1792]{2,1,0:T(8,128)(2,1)S(1)}, u32[]{:S(2)}, u32[]{:S(2)}) %collective-permute-start.26) | collective-permute-done | bytes 114720 | tf_op jit(solution)/shard_map/ppermute | solution.py:49
  123.9 3.6 %collective-permute-done.27 = bf16[1,16,1792]{2,1,0:T(8,128)(2,1)S(1)} collective-permute-done((bf16[1,16,1792]{2,1,0:T(8,128)(2,1)S(1)}, bf16[1,16,1792]{2,1,0:T(8,128)(2,1)S(1)}, u32[]{:S(2)}, u32[]{:S(2)}) %collective-permute-start.27) | collective-permute-done | bytes 57376 | tf_op jit(solution)/shard_map/ppermute | solution.py:49
  (133 shorter events, 27.4 us)
Async XLA Ops:
  0.0 12.2 %copy-start = (bf16[8,512,128]{2,1,0:T(8,128)(2,1)S(1)}, bf16[8,512,128]{2,1,0:T(8,128)(2,1)}, u32[]{:S(2)}) copy-start(bf16[8,512,128]{2,1,0:T(8,128)(2,1)} %param.15) | copy-start | bytes 3145732
  0.0 10.3 %collective-permute-start = (bf16[128,576]{0,1:T(8,128)(2,1)}, bf16[128,576]{0,1:T(8,128)(2,1)S(1)}, u32[]{:S(2)}, u32[]{:S(2)}) collective-permute-start(bf16[128,576]{0,1:T(8,128)(2,1)} %param.13), channel_id=1, source_target_pairs={{0,16},{1,17},{2,18},{3,19},{4,20},{5,21},{6,22},{7,23},{8,24},{9,... | collective-permute-start | bytes 442376 | tf_op jit(solution)/shard_map/ppermute | solution.py:148
  13.2 7.8 %collective-permute-start.1 = (bf16[128,1024]{0,1:T(8,128)(2,1)S(1)}, bf16[128,1024]{0,1:T(8,128)(2,1)S(1)}, u32[]{:S(2)}, u32[]{:S(2)}) collective-permute-start(bf16[128,1024]{0,1:T(8,128)(2,1)S(1)} %bitcast.299), channel_id=1, source_target_pairs={{0,16},{16,0},{1,17},{17,1},{2,18},{18,2},{3,19},{19,3},{4,20},{20... | collective-permute-start | bytes 786440 | tf_op jit(solution)/shard_map/ppermute | solution.py:161
  27.8 1.9 %collective-permute-start.6 = (bf16[8,16,1792]{2,1,0:T(8,128)(2,1)S(1)}, bf16[8,16,1792]{2,1,0:T(8,128)(2,1)S(1)}, u32[]{:S(2)}, u32[]{:S(2)}) collective-permute-start(bf16[8,16,1792]{2,1,0:T(8,128)(2,1)S(1)} %slice_bitcast_fusion.4), channel_id=1, source_target_pairs={{0,1},{1,0},{2,3},{3,2},{4,5},{5,4},{6,7},{7,6},{8,9},{9,8},{10,11... | collective-permute-start | bytes 1376264 | tf_op jit(solution)/shard_map/ppermute | solution.py:49
  27.9 24.4 %copy-start.1 = (bf16[16,3584]{1,0:T(8,128)(2,1)S(1)}, bf16[16,3584]{1,0:T(8,128)(2,1)}, u32[]{:S(2)}) copy-start(bf16[16,3584]{1,0:T(8,128)(2,1)} %param.17) | copy-start | bytes 344068
  27.9 24.4 %copy-start.2 = (f32[3584]{0:T(1024)S(1)}, f32[3584]{0:T(1024)}, u32[]{:S(2)}) copy-start(f32[3584]{0:T(1024)} %param.18) | copy-start | bytes 43012
  28.0 3.5 %collective-permute-start.2 = (bf16[8,16,1792]{2,1,0:T(8,128)(2,1)S(1)}, bf16[8,16,1792]{2,1,0:T(8,128)(2,1)S(1)}, u32[]{:S(2)}, u32[]{:S(2)}) collective-permute-start(bf16[8,16,1792]{2,1,0:T(8,128)(2,1)S(1)} %slice_bitcast_fusion.6), channel_id=1, source_target_pairs={{0,1},{1,0},{2,3},{3,2},{4,5},{5,4},{6,7},{7,6},{8,9},{9,8},{10,11... | collective-permute-start | bytes 1376264 | tf_op jit(solution)/shard_map/ppermute | solution.py:49
  29.9 7.7 %collective-permute-start.7 = (bf16[4,16,1792]{2,1,0:T(8,128)(2,1)S(1)}, bf16[4,16,1792]{2,1,0:T(8,128)(2,1)S(1)}, u32[]{:S(2)}, u32[]{:S(2)}) collective-permute-start(bf16[4,16,1792]{2,1,0:T(8,128)(2,1)S(1)} %bitcast.290), channel_id=1, source_target_pairs={{0,4},{1,5},{2,6},{3,7},{4,0},{5,1},{6,2},{7,3},{8,12},{9,13},{10,... | collective-permute-start | bytes 688136 | tf_op jit(solution)/shard_map/ppermute | solution.py:49
  31.7 8.7 %collective-permute-start.3 = (bf16[4,16,1792]{2,1,0:T(8,128)(2,1)S(1)}, bf16[4,16,1792]{2,1,0:T(8,128)(2,1)S(1)}, u32[]{:S(2)}, u32[]{:S(2)}) collective-permute-start(bf16[4,16,1792]{2,1,0:T(8,128)(2,1)S(1)} %slice_bitcast_fusion.13), channel_id=1, source_target_pairs={{0,2},{1,3},{2,0},{3,1},{4,6},{5,7},{6,4},{7,5},{8,10},{9,11},{10,... | collective-permute-start | bytes 688136 | tf_op jit(solution)/shard_map/ppermute | solution.py:49
  37.7 7.8 %collective-permute-start.8 = (bf16[2,16,1792]{2,1,0:T(8,128)(2,1)S(1)}, bf16[2,16,1792]{2,1,0:T(8,128)(2,1)S(1)}, u32[]{:S(2)}, u32[]{:S(2)}) collective-permute-start(bf16[2,16,1792]{2,1,0:T(8,128)(2,1)S(1)} %slice_bitcast_fusion.19), channel_id=1, source_target_pairs={{0,8},{1,9},{2,10},{3,11},{4,12},{5,13},{6,14},{7,15},{8,0},{9,1},... | collective-permute-start | bytes 344072 | tf_op jit(solution)/shard_map/ppermute | solution.py:49
  40.4 6.7 %collective-permute-start.4 = (bf16[2,16,1792]{2,1,0:T(8,128)(2,1)S(1)}, bf16[2,16,1792]{2,1,0:T(8,128)(2,1)S(1)}, u32[]{:S(2)}, u32[]{:S(2)}) collective-permute-start(bf16[2,16,1792]{2,1,0:T(8,128)(2,1)S(1)} %slice_bitcast_fusion.21), channel_id=1, source_target_pairs={{0,4},{1,5},{2,6},{3,7},{4,0},{5,1},{6,2},{7,3},{8,12},{9,13},{10,... | collective-permute-start | bytes 344072 | tf_op jit(solution)/shard_map/ppermute | solution.py:49
  45.5 4.2 %collective-permute-start.9 = (bf16[1,16,1792]{2,1,0:T(8,128)(2,1)S(1)}, bf16[1,16,1792]{2,1,0:T(8,128)(2,1)S(1)}, u32[]{:S(2)}, u32[]{:S(2)}) collective-permute-start(bf16[1,16,1792]{2,1,0:T(8,128)(2,1)S(1)} %slice_bitcast_fusion.27), channel_id=1, source_target_pairs={{0,2},{1,3},{2,0},{3,1},{4,6},{5,7},{6,4},{7,5},{8,10},{9,11},{10,... | collective-permute-start | bytes 172040 | tf_op jit(solution)/shard_map/ppermute | solution.py:49
  47.1 5.2 %collective-permute-start.5 = (bf16[1,16,1792]{2,1,0:T(8,128)(2,1)S(1)}, bf16[1,16,1792]{2,1,0:T(8,128)(2,1)S(1)}, u32[]{:S(2)}, u32[]{:S(2)}) collective-permute-start(bf16[1,16,1792]{2,1,0:T(8,128)(2,1)S(1)} %slice_bitcast_fusion.29), channel_id=1, source_target_pairs={{0,8},{1,9},{2,10},{3,11},{4,12},{5,13},{6,14},{7,15},{8,0},{9,1},... | collective-permute-start | bytes 172040 | tf_op jit(solution)/shard_map/ppermute | solution.py:49
  52.8 5.2 %collective-permute-start.14 = (bf16[1,16,1792]{2,1,0:T(8,128)(2,1)S(1)}, bf16[1,16,1792]{2,1,0:T(8,128)(2,1)S(1)}, u32[]{:S(2)}, u32[]{:S(2)}) collective-permute-start(bf16[1,16,1792]{2,1,0:T(8,128)(2,1)S(1)} %get-tuple-element.30), channel_id=1, source_target_pairs={{0,8},{1,9},{2,10},{3,11},{4,12},{5,13},{6,14},{7,15},{8,0},{9,1},... | collective-permute-start | bytes 172040 | tf_op jit(solution)/shard_map/ppermute | solution.py:64
  54.6 4.7 %collective-permute-start.10 = (bf16[1,16,1920]{2,1,0:T(8,128)(2,1)S(1)}, bf16[1,16,1920]{2,1,0:T(8,128)(2,1)S(1)}, u32[]{:S(2)}, u32[]{:S(2)}) collective-permute-start(bf16[1,16,1920]{2,1,0:T(8,128)(2,1)S(1)} %get-tuple-element.26), channel_id=1, source_target_pairs={{0,2},{1,3},{2,0},{3,1},{4,6},{5,7},{6,4},{7,5},{8,10},{9,11},{10,... | collective-permute-start | bytes 184328 | tf_op jit(solution)/shard_map/ppermute | solution.py:64
  58.1 4.9 %collective-permute-start.15 = (bf16[2,16,1792]{2,1,0:T(8,128)(2,1)S(1)}, bf16[2,16,1792]{2,1,0:T(8,128)(2,1)S(1)}, u32[]{:S(2)}, u32[]{:S(2)}) collective-permute-start(bf16[2,16,1792]{2,1,0:T(8,128)(2,1)S(1)} %get-tuple-element.28), channel_id=1, source_target_pairs={{0,4},{1,5},{2,6},{3,7},{4,0},{5,1},{6,2},{7,3},{8,12},{9,13},{10,... | collective-permute-start | bytes 344072 | tf_op jit(solution)/shard_map/ppermute | solution.py:64
  59.4 6.7 %collective-permute-start.11 = (bf16[2,16,1920]{2,1,0:T(8,128)(2,1)S(1)}, bf16[2,16,1920]{2,1,0:T(8,128)(2,1)S(1)}, u32[]{:S(2)}, u32[]{:S(2)}) collective-permute-start(bf16[2,16,1920]{2,1,0:T(8,128)(2,1)S(1)} %get-tuple-element.24), channel_id=1, source_target_pairs={{0,8},{1,9},{2,10},{3,11},{4,12},{5,13},{6,14},{7,15},{8,0},{9,1},... | collective-permute-start | bytes 368648 | tf_op jit(solution)/shard_map/ppermute | solution.py:64
  63.0 6.1 %collective-permute-start.16 = (bf16[4,16,1792]{2,1,0:T(8,128)(2,1)S(1)}, bf16[4,16,1792]{2,1,0:T(8,128)(2,1)S(1)}, u32[]{:S(2)}, u32[]{:S(2)}) collective-permute-start(bf16[4,16,1792]{2,1,0:T(8,128)(2,1)S(1)} %bitcast.267), channel_id=1, source_target_pairs={{0,2},{1,3},{2,0},{3,1},{4,6},{5,7},{6,4},{7,5},{8,10},{9,11},{10,... | collective-permute-start | bytes 688136 | tf_op jit(solution)/shard_map/ppermute | solution.py:64
  66.1 6.7 %collective-permute-start.12 = (bf16[4,16,1920]{2,1,0:T(8,128)(2,1)S(1)}, bf16[4,16,1920]{2,1,0:T(8,128)(2,1)S(1)}, u32[]{:S(2)}, u32[]{:S(2)}) collective-permute-start(bf16[4,16,1920]{2,1,0:T(8,128)(2,1)S(1)} %bitcast.288), channel_id=1, source_target_pairs={{0,4},{1,5},{2,6},{3,7},{4,0},{5,1},{6,2},{7,3},{8,12},{9,13},{10,... | collective-permute-start | bytes 737288 | tf_op jit(solution)/shard_map/ppermute | solution.py:64
  69.1 3.8 %collective-permute-start.17 = (bf16[8,16,1792]{2,1,0:T(8,128)(2,1)S(1)}, bf16[8,16,1792]{2,1,0:T(8,128)(2,1)S(1)}, u32[]{:S(2)}, u32[]{:S(2)}) collective-permute-start(bf16[8,16,1792]{2,1,0:T(8,128)(2,1)S(1)} %bitcast.256), channel_id=1, source_target_pairs={{0,1},{1,0},{2,3},{3,2},{4,5},{5,4},{6,7},{7,6},{8,9},{9,8},{10,11... | collective-permute-start | bytes 1376264 | tf_op jit(solution)/shard_map/ppermute | solution.py:64
  72.8 3.1 %slice-start = ((s8[7340032]{0:T(1024)(128)(4,1)}), s8[4194304]{0:T(1024)(128)(4,1)S(1)}, s32[]{:S(2)}) async-start(s8[7340032]{0:T(1024)(128)(4,1)} %bitcast.250), calls=%async_computation | async-start | bytes 8388608
  72.9 1.9 %collective-permute-start.13 = (bf16[8,16,1920]{2,1,0:T(8,128)(2,1)S(1)}, bf16[8,16,1920]{2,1,0:T(8,128)(2,1)S(1)}, u32[]{:S(2)}, u32[]{:S(2)}) collective-permute-start(bf16[8,16,1920]{2,1,0:T(8,128)(2,1)S(1)} %bitcast.254), channel_id=1, source_target_pairs={{0,1},{1,0},{2,3},{3,2},{4,5},{5,4},{6,7},{7,6},{8,9},{9,8},{10,11... | collective-permute-start | bytes 1474568 | tf_op jit(solution)/shard_map/ppermute | solution.py:64
  80.3 15.7 %collective-permute-start.18 = (bf16[144,2048]{1,0:T(8,128)(2,1)S(1)}, bf16[144,2048]{1,0:T(8,128)(2,1)S(1)}, u32[]{:S(2)}, u32[]{:S(2)}) collective-permute-start(bf16[144,2048]{1,0:T(8,128)(2,1)S(1)} %pad_maximum_fusion.4), channel_id=1, source_target_pairs={{0,16},{16,0},{1,17},{17,1},{2,18},{18,2},{3,19},{19,3},{4,20},{20... | collective-permute-start | bytes 1769480 | tf_op jit(solution)/shard_map/ppermute | solution.py:233
  80.8 15.0 %collective-permute-start.19 = (f32[256]{0:T(256)S(1)}, f32[256]{0:T(256)S(1)}, u32[]{:S(2)}, u32[]{:S(2)}) collective-permute-start(f32[256]{0:T(256)S(1)} %slice_reduce_fusion), channel_id=1, source_target_pairs={{0,16},{16,0},{1,17},{17,1},{2,18},{18,2},{3,19},{19,3},{4,20},{20... | collective-permute-start | bytes 3080 | tf_op jit(solution)/shard_map/ppermute | solution.py:215
  102.4 1.9 %collective-permute-start.20 = (bf16[8,16,1792]{2,1,0:T(8,128)(2,1)S(1)}, bf16[8,16,1792]{2,1,0:T(8,128)(2,1)S(1)}, u32[]{:S(2)}, u32[]{:S(2)}) collective-permute-start(bf16[8,16,1792]{2,1,0:T(8,128)(2,1)S(1)} %slice_bitcast_fusion.2), channel_id=1, source_target_pairs={{0,1},{1,0},{2,3},{3,2},{4,5},{5,4},{6,7},{7,6},{8,9},{9,8},{10,11... | collective-permute-start | bytes 1376264 | tf_op jit(solution)/shard_map/ppermute | solution.py:49
  102.6 2.4 %collective-permute-start.24 = (bf16[8,16,1792]{2,1,0:T(8,128)(2,1)S(1)}, bf16[8,16,1792]{2,1,0:T(8,128)(2,1)S(1)}, u32[]{:S(2)}, u32[]{:S(2)}) collective-permute-start(bf16[8,16,1792]{2,1,0:T(8,128)(2,1)S(1)} %slice_bitcast_fusion), channel_id=1, source_target_pairs={{0,1},{1,0},{2,3},{3,2},{4,5},{5,4},{6,7},{7,6},{8,9},{9,8},{10,11... | collective-permute-start | bytes 1376264 | tf_op jit(solution)/shard_map/ppermute | solution.py:49
  104.5 7.7 %collective-permute-start.21 = (bf16[4,16,1792]{2,1,0:T(8,128)(2,1)S(1)}, bf16[4,16,1792]{2,1,0:T(8,128)(2,1)S(1)}, u32[]{:S(2)}, u32[]{:S(2)}) collective-permute-start(bf16[4,16,1792]{2,1,0:T(8,128)(2,1)S(1)} %slice_bitcast_fusion.11), channel_id=1, source_target_pairs={{0,2},{1,3},{2,0},{3,1},{4,6},{5,7},{6,4},{7,5},{8,10},{9,11},{10,... | collective-permute-start | bytes 688136 | tf_op jit(solution)/shard_map/ppermute | solution.py:49
  105.1 9.2 %collective-permute-start.25 = (bf16[4,16,1792]{2,1,0:T(8,128)(2,1)S(1)}, bf16[4,16,1792]{2,1,0:T(8,128)(2,1)S(1)}, u32[]{:S(2)}, u32[]{:S(2)}) collective-permute-start(bf16[4,16,1792]{2,1,0:T(8,128)(2,1)S(1)} %bitcast.292), channel_id=1, source_target_pairs={{0,4},{1,5},{2,6},{3,7},{4,0},{5,1},{6,2},{7,3},{8,12},{9,13},{10,... | collective-permute-start | bytes 688136 | tf_op jit(solution)/shard_map/ppermute | solution.py:49
  112.2 5.6 %collective-permute-start.22 = (bf16[2,16,1792]{2,1,0:T(8,128)(2,1)S(1)}, bf16[2,16,1792]{2,1,0:T(8,128)(2,1)S(1)}, u32[]{:S(2)}, u32[]{:S(2)}) collective-permute-start(bf16[2,16,1792]{2,1,0:T(8,128)(2,1)S(1)} %slice_bitcast_fusion.17), channel_id=1, source_target_pairs={{0,4},{1,5},{2,6},{3,7},{4,0},{5,1},{6,2},{7,3},{8,12},{9,13},{10,... | collective-permute-start | bytes 344072 | tf_op jit(solution)/shard_map/ppermute | solution.py:49
  114.4 8.7 %collective-permute-start.26 = (bf16[2,16,1792]{2,1,0:T(8,128)(2,1)S(1)}, bf16[2,16,1792]{2,1,0:T(8,128)(2,1)S(1)}, u32[]{:S(2)}, u32[]{:S(2)}) collective-permute-start(bf16[2,16,1792]{2,1,0:T(8,128)(2,1)S(1)} %slice_bitcast_fusion.15), channel_id=1, source_target_pairs={{0,8},{1,9},{2,10},{3,11},{4,12},{5,13},{6,14},{7,15},{8,0},{9,1},... | collective-permute-start | bytes 344072 | tf_op jit(solution)/shard_map/ppermute | solution.py:49
  117.9 6.0 %collective-permute-start.23 = (bf16[1,16,1792]{2,1,0:T(8,128)(2,1)S(1)}, bf16[1,16,1792]{2,1,0:T(8,128)(2,1)S(1)}, u32[]{:S(2)}, u32[]{:S(2)}) collective-permute-start(bf16[1,16,1792]{2,1,0:T(8,128)(2,1)S(1)} %slice_bitcast_fusion.25), channel_id=1, source_target_pairs={{0,8},{1,9},{2,10},{3,11},{4,12},{5,13},{6,14},{7,15},{8,0},{9,1},... | collective-permute-start | bytes 172040 | tf_op jit(solution)/shard_map/ppermute | solution.py:49
  123.2 4.2 %collective-permute-start.27 = (bf16[1,16,1792]{2,1,0:T(8,128)(2,1)S(1)}, bf16[1,16,1792]{2,1,0:T(8,128)(2,1)S(1)}, u32[]{:S(2)}, u32[]{:S(2)}) collective-permute-start(bf16[1,16,1792]{2,1,0:T(8,128)(2,1)S(1)} %slice_bitcast_fusion.23), channel_id=1, source_target_pairs={{0,2},{1,3},{2,0},{3,1},{4,6},{5,7},{6,4},{7,5},{8,10},{9,11},{10,... | collective-permute-start | bytes 172040 | tf_op jit(solution)/shard_map/ppermute | solution.py:49
  (3 other events, 6.9 us)

commit v2 on v1

v2 whole, which is shorter than its diff:
```python
import functools
import math

import jax
import jax.numpy as jnp
from jax import lax
from jax.experimental import pallas as pl
from jax.experimental.pallas import tpu as pltpu
from jax.sharding import PartitionSpec as P

D = 7168
KVL = 512


score_scale = (1.0 + 0.1 * math.log(40.0)) ** 2 / math.sqrt(192.0)
masked_score = -1e30
PARTS = 2


def split_edges(width, parts):
    lanes = width // 128
    edges = [lanes * part // parts * 128 for part in range(parts)] + [width]
    return [(low, high) for low, high in zip(edges[:-1], edges[1:]) if high > low]


def split_columns(array, parts):
    return [array[..., low:high] for low, high in split_edges(array.shape[-1], parts)]


def step_bits(bits, lane):
    middle = list(range(1, bits - 1))
    if lane:
        middle = middle[1:] + middle[:1]
    return [0] + middle + [bits - 1]


def crossing(count, step):
    bits = count.bit_length() - 1
    return [(index, index ^ (1 << step_bits(bits, index & 1)[step])) for index in range(count)]


def chunk_owners(count, rank):
    bits = count.bit_length() - 1
    number = jnp.arange(count, dtype=jnp.int32)
    flip = number >> (bits - 1)
    distances = []
    for lane in range(2):
        order = step_bits(bits, lane)
        distance = jnp.zeros((count,), jnp.int32)
        for step in range(1, bits):
            distance = distance | ((number >> (bits - 1 - step)) & 1) << order[step]
        distances.append(distance)
    other_lane = ((rank & 1) ^ flip) == 1
    return rank ^ flip ^ jnp.where(other_lane, distances[1], distances[0])


def halved(array, step, count):
    half = array.shape[0] // 2
    got = lax.ppermute(array[half:], "ep", crossing(count, step))
    return array[:half].astype(jnp.float32) + got.astype(jnp.float32)


def doubled(array, step, count):
    return jnp.concatenate([array, lax.ppermute(array, "ep", crossing(count, step))], axis=0)


def scores_kernel(pair_count, query_ref, keys_ref, heads_ref, scores_ref):
    rows = query_ref.shape[0]
    pair_width = query_ref.shape[1] // pair_count
    width = heads_ref.shape[1]
    half = pair_count * rows
    for side in range(2):
        first = side * (pair_width - width)
        for pair in range(pair_count):
            at = side * half + pair * rows
            low = pair * pair_width + first
            heads_ref[at : at + rows, :] = query_ref[:, low : low + width]
        part = slice(side * half, (side + 1) * half)
        scores_ref[part, :] = jnp.dot(
            heads_ref[part, :], padded_keys(keys_ref, width, side), preferred_element_type=jnp.float32
        )


def padded_keys(keys_ref, width, side):
    zeros = jnp.zeros((width - keys_ref.shape[0], keys_ref.shape[1]), jnp.bfloat16)
    parts = [zeros, keys_ref[...]] if side else [keys_ref[...], zeros]
    return jnp.concatenate(parts, axis=0)


def attend_kernel(pair_count, doc_ref, heads_ref, scores_ref, up_ref, *refs):
    blocks, out_ref = refs[:-1], refs[-1]
    rows = out_ref.shape[0]
    half = pair_count * rows
    width = heads_ref.shape[1]
    value_width = up_ref.shape[2]
    rank = lax.axis_index("ctx")

    def docs_of(first, count):
        return doc_ref[:, pl.ds(pl.multiple_of(first, 128), count)]

    own_first = rank * rows
    query_doc = jnp.broadcast_to(docs_of(own_first, rows), (rows, rows)).T[:, 0:1]
    firsts = [jnp.int32(0)] if len(blocks) == 1 else [own_first, (1 - rank) * rows]
    scores, masks = [], []
    for first, block in zip(firsts, blocks):
        count = block.shape[1]
        key_pos = first + lax.broadcasted_iota(jnp.int32, (rows, count), 1)
        query_pos = own_first + lax.broadcasted_iota(jnp.int32, (rows, count), 0)
        allowed = (key_pos <= query_pos) & (docs_of(first, count) == query_doc)
        masks.append(jnp.where(allowed, 1.0, 0.0))
        if block is blocks[0]:
            scores.append(scores_ref[...])
        else:
            sides = [
                jnp.dot(
                    heads_ref[side * half : (side + 1) * half, :],
                    padded_keys(block, width, side),
                    preferred_element_type=jnp.float32,
                )
                for side in range(2)
            ]
            scores.append(jnp.concatenate(sides, axis=0))
    allowed = jnp.concatenate([jnp.concatenate(masks, axis=1)] * (2 * pair_count), axis=0) > 0
    scores = jnp.where(allowed, jnp.concatenate(scores, axis=1) * score_scale, masked_score)
    peak = jnp.max(scores, axis=1, keepdims=True)
    probs = jnp.where(allowed, jnp.exp(scores - peak), 0.0)
    total = jnp.sum(probs, axis=1, keepdims=True)
    context = lax.dot_general(
        probs.astype(jnp.bfloat16),
        jnp.concatenate([block[:KVL, :] for block in blocks], axis=1),
        (((1,), (1,)), ((), ())),
        preferred_element_type=jnp.float32,
    )
    context = (context / total).astype(jnp.bfloat16)
    for pair in range(pair_count):
        for side in range(2):
            at = side * half + pair * rows
            head = 2 * pair + side
            out_ref[:, head * value_width : (head + 1) * value_width] = jnp.dot(
                context[at : at + rows], up_ref[head], preferred_element_type=jnp.float32
            ).astype(jnp.bfloat16)


def whole_block(shape):
    return pl.BlockSpec(shape, lambda step: (0,) * len(shape))


def attend(queries, blocks, doc_ids, w_uv):
    rows = queries.shape[0]
    head_count, value_in, value_width = w_uv.shape
    query_width = queries.shape[1] // head_count
    key_count = doc_ids.shape[0]
    width = -(-query_width // 128) * 128
    pair_count = 2 if head_count % 4 == 0 and key_count <= 512 else 1
    heads = 2 * pair_count
    grid = (head_count // heads,)
    first_keys = blocks[0].shape[1]
    params = pltpu.CompilerParams(
        vmem_limit_bytes=(8 << 20) + 8 * heads * rows * (key_count + KVL) * 4
    )
    stacked = lambda columns: pl.BlockSpec((heads * rows, columns), lambda step: (step, 0))
    arranged, scores = pl.pallas_call(
        functools.partial(scores_kernel, pair_count),
        out_shape=(
            jax.ShapeDtypeStruct((head_count * rows, width), jnp.bfloat16),
            jax.ShapeDtypeStruct((head_count * rows, first_keys), jnp.float32),
        ),
        grid=grid,
        in_specs=[
            pl.BlockSpec((rows, heads * query_width), lambda step: (0, step)),
            whole_block(blocks[0].shape),
        ],
        out_specs=(stacked(width), stacked(first_keys)),
        compiler_params=params,
        cost_estimate=pl.CostEstimate(
            flops=2 * rows * head_count * first_keys * width,
            bytes_accessed=2 * queries.size,
            transcendentals=0,
        ),
        name="first_scores",
    )(queries, blocks[0])
    return pl.pallas_call(
        functools.partial(attend_kernel, pair_count),
        out_shape=jax.ShapeDtypeStruct((rows, head_count * value_width), jnp.bfloat16),
        grid=grid,
        in_specs=[
            whole_block((1, key_count)),
            stacked(width),
            stacked(first_keys),
            pl.BlockSpec((heads, value_in, value_width), lambda step: (step, 0, 0)),
            *(whole_block(block.shape) for block in blocks),
        ],
        out_specs=pl.BlockSpec((rows, heads * value_width), lambda step: (0, step)),
        compiler_params=params,
        cost_estimate=pl.CostEstimate(
            flops=2 * rows * head_count * key_count * (query_width + value_in),
            bytes_accessed=2 * (queries.size + w_uv.size),
            transcendentals=rows * head_count * key_count,
        ),
        name="attention",
    )(doc_ids[None], arranged, scores, w_uv, *blocks)


def fetch_kernel(pieces, first, from_ref, after_ref, to_ref, sems):
    rows = from_ref.shape[0] // pieces
    columns = pl.ds(first, to_ref.shape[1])
    copies = []
    for piece in range(pieces):
        part = pl.ds(piece * rows, rows)
        copies.append(
            pltpu.make_async_copy(
                from_ref.at[part, columns], to_ref.at[part], sems.at[piece]
            )
        )
    for copy in copies:
        copy.start()
    for copy in copies:
        copy.wait()


def fetched(weights, after, edges=None):
    pieces = 4
    low, high = edges or (0, weights.shape[1])
    return pl.pallas_call(
        functools.partial(fetch_kernel, pieces, low),
        out_shape=pltpu.VMEM((weights.shape[0], high - low), weights.dtype),
        in_specs=[
            pl.BlockSpec(memory_space=pltpu.HBM),
            pl.BlockSpec(memory_space=pl.ANY),
        ],
        out_specs=pl.BlockSpec(memory_space=pltpu.VMEM),
        scratch_shapes=[pltpu.SemaphoreType.DMA((pieces,))],
        compiler_params=pltpu.CompilerParams(vmem_limit_bytes=1 << 20),
        cost_estimate=pl.CostEstimate(
            flops=0, bytes_accessed=2 * weights.shape[0] * (high - low) * weights.dtype.itemsize, transcendentals=0
        ),
        name="fetch_weights",
    )(weights, after)


def norm_part(own_ref, got_ref, gain_ref, kept_ref, sent_ref):
    width = own_ref.shape[2]
    squares = []
    for chunk in range(2):
        residual = own_ref[chunk] + got_ref[1 - chunk, :, :width].astype(jnp.float32)
        if chunk == 0:
            kept_ref[...] = residual
        sent_ref[chunk, :, :width] = (residual * gain_ref[...]).astype(jnp.bfloat16)
        squares.append(jnp.sum(residual * residual, axis=1, keepdims=True))
    return squares


def first_norm_kernel(own_ref, got_ref, gain_ref, kept_ref, sent_ref, squares_ref):
    for chunk, squares in enumerate(norm_part(own_ref, got_ref, gain_ref, kept_ref, sent_ref)):
        squares_ref[chunk] = squares


def last_norm_kernel(
    facts_width, own_ref, got_ref, gain_ref, squares_ref, facts_ref, kept_ref, sent_ref
):
    width = own_ref.shape[2]
    for chunk, squares in enumerate(norm_part(own_ref, got_ref, gain_ref, kept_ref, sent_ref)):
        facts = facts_ref[...] if chunk == 0 else got_ref[0, :, width:]
        facts = facts.astype(jnp.float32)
        lane = lax.broadcasted_iota(jnp.int32, facts.shape, 1)
        for place, term in enumerate(three_terms(squares + squares_ref[chunk])):
            facts = jnp.where(lane == facts_width + place, term.astype(jnp.float32), facts)
        sent_ref[chunk, :, width:] = facts.astype(jnp.bfloat16)


def normalised(facts_width, own, got, gain, squares=None, facts=None):
    rows, width = own.shape[1:]
    vmem = pl.BlockSpec(memory_space=pltpu.VMEM)
    if squares is None:
        return pl.pallas_call(
            first_norm_kernel,
            out_shape=(
                jax.ShapeDtypeStruct((rows, width), jnp.float32),
                jax.ShapeDtypeStruct((2, rows, width), jnp.bfloat16),
                jax.ShapeDtypeStruct((2, rows, 1), jnp.float32),
            ),
            in_specs=[vmem] * 3,
            out_specs=(vmem,) * 3,
            compiler_params=pltpu.CompilerParams(vmem_limit_bytes=4 << 20),
            name="norm",
        )(own, got, gain[None])
    return pl.pallas_call(
        functools.partial(last_norm_kernel, facts_width),
        out_shape=(
            jax.ShapeDtypeStruct((rows, width), jnp.float32),
            jax.ShapeDtypeStruct((2, rows, width + facts.shape[1]), jnp.bfloat16),
        ),
        in_specs=[vmem] * 5,
        out_specs=(vmem,) * 2,
        compiler_params=pltpu.CompilerParams(vmem_limit_bytes=4 << 20),
        name="norm_last",
    )(own, got, gain[None], squares, facts)


def three_terms(values):
    first = values.astype(jnp.bfloat16)
    rest = values - first.astype(jnp.float32)
    second = rest.astype(jnp.bfloat16)
    third = (rest - second.astype(jnp.float32)).astype(jnp.bfloat16)
    return first, second, third


def shards(
    queries,
    latent,
    doc_ids,
    w_uv,
    w_out,
    hidden_in,
    norm_gain,
    route_ids,
    route_weights,
    w_gate,
    w_up,
    w_down,
):
    ctx_count = lax.axis_size("ctx")
    ep_count = lax.axis_size("ep")
    ctx_rank = lax.axis_index("ctx")
    ep_rank = lax.axis_index("ep")
    bits = ep_count.bit_length() - 1
    block_rows = queries.shape[0]
    token_count = hidden_in.shape[0]
    top_count = route_ids.shape[1]
    all_tokens = ep_count * token_count
    swap = [(0, 1), (1, 0)]

    key_columns = latent.T
    if ctx_count == 2:
        blocks = [key_columns, lax.ppermute(key_columns, "ctx", [(0, 1)])]
    else:
        blocks = [lax.all_gather(key_columns, "ctx", axis=1, tiled=True)]
    head_values = attend(queries, blocks, doc_ids, w_uv)
    route_ids, route_weights, head_values = lax.optimization_barrier(
        (route_ids, route_weights, head_values)
    )

    owner = jnp.repeat(chunk_owners(ep_count, ep_rank), token_count)
    chunk = jnp.arange(all_tokens, dtype=jnp.int32) // token_count
    if ctx_count == 2:
        other = lax.ppermute(head_values, "ctx", swap)
        w_out = fetched(w_out, head_values)
        all_values = jnp.concatenate([head_values, other], axis=0)
        per_block = ep_count // 2
        owner = owner % per_block + per_block * (owner // per_block != ctx_rank)
    else:
        all_values = lax.all_gather(head_values, "ctx", axis=0, tiled=True)
    row = owner * token_count + jnp.arange(all_tokens, dtype=jnp.int32) % token_count
    ordering = (row[:, None] == jnp.arange(all_tokens, dtype=jnp.int32)[None, :]).astype(
        jnp.bfloat16
    )
    all_values = jnp.dot(ordering, all_values, preferred_element_type=jnp.float32).astype(
        jnp.bfloat16
    )

    experts = jnp.arange(ep_count, dtype=jnp.int32)
    named = route_ids[:, :, None] == experts[None, None, :]
    chosen = jnp.sum(named.astype(jnp.float32), axis=1)
    weights = jnp.sum(jnp.where(named, route_weights[:, :, None], 0.0), axis=1)
    token_index = jnp.arange(token_count, dtype=jnp.int32)
    before = (token_index[:, None] > token_index[None, :]).astype(jnp.float32)
    place = jnp.sum(before[:, :, None] * chosen[None, :, :], axis=1)
    place = jnp.where(chosen > 0, place, -1.0).astype(jnp.bfloat16)
    facts = jnp.concatenate([place, *three_terms(weights)], axis=1)
    facts_width = facts.shape[1]
    padded = -(-(facts_width + 3) // 128) * 128
    facts = jnp.pad(facts, ((0, 0), (0, padded - facts_width)))

    edges = split_edges(w_out.shape[1], PARTS)
    residuals, arrived = [], []
    squares = jnp.zeros((2, token_count, 1), jnp.float32)
    for part, (low, high) in enumerate(edges):
        array = (
            jnp.dot(all_values, w_out[:, low:high], preferred_element_type=jnp.float32)
            .astype(jnp.bfloat16)
            .reshape(ep_count, token_count, -1)
        )
        for step in range(bits - 1):
            total = halved(array, step, ep_count)
            array = total.astype(jnp.bfloat16)
        own = total[0] + hidden_in[:, low:high].astype(jnp.float32)
        total = jnp.stack([own, total[1]])
        sent = total.astype(jnp.bfloat16)
        last = part == len(edges) - 1
        if last:
            sent = jnp.concatenate([sent, jnp.stack([facts, jnp.zeros_like(facts)])], axis=2)
        got = lax.ppermute(sent, "ep", crossing(ep_count, bits - 1))
        if part == 0:
            gate_weights = fetched(w_gate[0], sent)
            up_weights = fetched(w_up[0], sent)
        width = high - low
        if last:
            kept, array = normalised(facts_width, total, got, norm_gain[low:high], squares, facts)
        else:
            kept, array, more = normalised(facts_width, total, got, norm_gain[low:high])
            squares = squares + more
        residuals.append(kept)
        for step in range(bits - 2, -1, -1):
            array = doubled(array, step, ep_count)
        arrived.append(array.reshape(all_tokens, -1))
    facts = arrived[-1][:, width:].astype(jnp.float32)
    arrived[-1] = arrived[-1][:, :width]

    capacity = min(token_count, max(2, token_count * top_count * 9 // (8 * ep_count)))
    slots = ep_count * capacity
    mine = (experts == ep_rank).astype(jnp.float32)
    of_expert = [
        jnp.sum(facts[:, part * ep_count : (part + 1) * ep_count] * mine[None, :], axis=1)
        for part in range(4)
    ]
    token_place = of_expert[0].astype(jnp.int32)
    token_weight = of_expert[1] + of_expert[2] + of_expert[3]
    token_squares = jnp.sum(facts[:, 4 * ep_count : 4 * ep_count + 3], axis=1)
    if ctx_count == 2:
        token_squares = token_squares + lax.ppermute(token_squares, "ctx", swap)
    else:
        token_squares = lax.psum(token_squares, "ctx")
    token_scale = lax.rsqrt(token_squares / D + 1e-06)
    token_slot = jnp.where(token_place >= 0, chunk * capacity + token_place, -1)
    placing = jnp.arange(slots, dtype=jnp.int32)[:, None] == token_slot[None, :]
    slot_scale = jnp.sum(jnp.where(placing, token_scale[None, :], 0.0), axis=1)
    slot_weight = jnp.sum(jnp.where(placing, token_weight[None, :], 0.0), axis=1)
    placing = placing.astype(jnp.bfloat16)
    both = 0.0
    for (low, high), features in zip(edges, arrived):
        rows = jnp.dot(placing, features, preferred_element_type=jnp.float32).astype(jnp.bfloat16)
        both = both + jnp.concatenate(
            [
                jnp.dot(rows, gate_weights[low:high], preferred_element_type=jnp.float32),
                jnp.dot(rows, up_weights[low:high], preferred_element_type=jnp.float32),
            ],
            axis=1,
        )
    both = both.astype(jnp.bfloat16)
    if ctx_count == 2:
        down_weights = fetched(w_down[0], both)
        other_both = lax.ppermute(both, "ctx", swap)
        both = both.astype(jnp.float32) + other_both.astype(jnp.float32)
    else:
        down_weights = w_down[0]
        both = lax.psum(both, "ctx").astype(jnp.float32)
    both = both * slot_scale[:, None]
    hidden = both.shape[1] // 2
    activated = (jax.nn.silu(both[:, :hidden]) * both[:, hidden:]).astype(jnp.bfloat16)
    spread = placing.T
    outputs = []
    for (low, high), residual in zip(edges, residuals):
        produced = jnp.dot(activated, down_weights[:, low:high], preferred_element_type=jnp.float32)
        produced = (produced * slot_weight[:, None]).astype(jnp.bfloat16)
        produced = lax.optimization_barrier(produced)
        array = (
            jnp.dot(spread, produced, preferred_element_type=jnp.float32)
            .astype(jnp.bfloat16)
            .reshape(ep_count, token_count, -1)
        )
        for step in range(bits):
            total = halved(array, step, ep_count)
            array = total.astype(jnp.bfloat16)
        outputs.append((residual + total[0]).astype(jnp.bfloat16))
    return jnp.concatenate(outputs, axis=1)


def solution(mesh):
    return jax.shard_map(
        shards,
        mesh=mesh,
        in_specs=(
            P("ctx", "ep"),
            P("ctx", None),
            P(),
            P("ep", None, None),
            P("ep", "ctx"),
            P("ep", "ctx"),
            P("ctx"),
            P("ep", None),
            P("ep", None),
            P("ep", "ctx", None),
            P("ep", "ctx", None),
            P("ep", None, "ctx"),
        ),
        out_specs=P("ep", "ctx"),
        check_vma=False,
    )
```

time: 129 us -> 114 us (0.88)
  starting transfers between devices: 38.9 us -> 28 us
  matrix products: 17.6 us -> 8.56 us
  Pallas kernels: 0 us -> 5.17 us
  local copies, waits for them, and re-layouts: 6.98 us -> 12.1 us
  waiting for transfers between devices: 58.8 us -> 56 us
  other arithmetic: 5.29 us -> 3.53 us
    ppermute x26 -> x24, starting transfers between devices: 36.6 us -> 25.3 us  [the longest x14 11.5 us: halved(): got = lax.ppermute(array[half:], 'ep', crossing(count, step))]
    dot_general x7 -> x10, matrix products: 16 us -> 7.62 us  [the longest x2 2.27 us: shards(): jnp.dot(all_values, w_out[:, low:high], preferred_element_type=jnp.float32)]
    unnamed x18 -> x30, local copies, waits for them, and re-layouts: 5.12 us -> 10.6 us
    pallas_call x0 -> x8, Pallas kernels: none -> 5.17 us  [the longest x4 2.31 us: fetched(): pl.pallas_call(functools.partial(fetch_kernel, pieces, low), out_shape=pl...]
    ppermute x1, waiting for transfers between devices: 7.31 us -> 2.14 us  [shards(): other = lax.ppermute(head_values, 'ctx', swap)]
    ppermute x26 -> x24, waiting for transfers between devices: 38.3 us -> 42.3 us  [the longest x14 25 us: halved(): got = lax.ppermute(array[half:], 'ep', crossing(count, step))]
    ppermute x1, waiting for transfers between devices: 13.2 us -> 11.6 us  [shards(): token_squares = token_squares + lax.ppermute(token_squares, 'ctx', swap)]
    add x4 -> x3, other arithmetic: 1.46 us -> 0.07 us  [the longest x2 0.05 us: halved(): return array[:half].astype(jnp.float32) + got.astype(jnp.float32)]
  transfers between devices with their start and end apart: 28 -> 26, of which waited for: 19 -> 20; matrix products, arithmetic and copies ran while one was open for 6% -> 3% of each run, Pallas kernels for 0% -> 3%
where the time goes in v2:
time: 114 us
  waiting for transfers between devices  56 us (49%)
  starting transfers between devices  28 us (25%)
  local copies, waits for them, and re-layouts  12.1 us (11%)
  matrix products  8.56 us (8%)
  Pallas kernels  5.17 us (5%)
  other arithmetic  3.53 us (3%)
    ppermute x14, waiting for transfers between devices, halved(): got = lax.ppermute(array[half:], 'ep', crossing(count, step))  25 us
    ppermute x1, waiting for transfers between devices, shards(): token_squares = token_squares + lax.ppermute(token_squares, 'ctx', swap)  11.6 us
    ppermute x14, starting transfers between devices, halved(): got = lax.ppermute(array[half:], 'ep', crossing(count, step))  11.5 us
    unnamed x30, local copies, waits for them, and re-layouts  10.6 us
    ppermute x6, waiting for transfers between devices, doubled(): lax.ppermute(array, 'ep', crossing(count, step))  9.14 us
    ppermute x2, waiting for transfers between devices, shards(): got = lax.ppermute(sent, 'ep', crossing(ep_count, bits - 1))  8.11 us
    ppermute x1, starting transfers between devices, shards(): blocks = [key_columns, lax.ppermute(key_columns, 'ctx', [(0, 1)])]  5 us
    ppermute x6, starting transfers between devices, doubled(): lax.ppermute(array, 'ep', crossing(count, step))  4.46 us
  transfers between devices with their start and end apart: 26, of which 20 were waited for; matrix products, arithmetic and copies ran while one was open for 3% of the time, Pallas kernels for 3%

profile of v2, /device:TPU:0, one launch (start us, length us, event | category | flops | bytes accessed | tf_op | source)
XLA Modules:
  0.0 114.1 jit_solution(10017953153163888853)
XLA Ops:
  0.0 5.0 %collective-permute-start = (bf16[576,128]{1,0:T(8,128)(2,1)}, bf16[576,128]{1,0:T(8,128)(2,1)S(1)}, u32[]{:S(2)}, u32[]{:S(2)}) collective-permute-start(bf16[576,128]{1,0:T(8,128)(2,1)} %bitcast.64), channel_id=1, source_target_pairs={{0,16},{1,17},{2,18},{3,19},{4,20},{5,21},{6,22},{7,23},{8,24},{9,... | collective-permute-start | bytes 442376 | tf_op jit(solution)/shard_map/ppermute | solution.py:335
  6.0 1.3 %copy-done.1 = bf16[128,4608]{1,0:T(8,128)(2,1)S(1)} copy-done((bf16[128,4608]{1,0:T(8,128)(2,1)S(1)}, bf16[128,4608]{1,0:T(8,128)(2,1)}, u32[]{:S(2)}) %copy-start.1) | copy-done | bytes 1179672
  9.0 1.2 %copy-done.2 = bf16[8,512,128]{2,1,0:T(8,128)(2,1)S(1)} copy-done((bf16[8,512,128]{2,1,0:T(8,128)(2,1)S(1)}, bf16[8,512,128]{2,1,0:T(8,128)(2,1)}, u32[]{:S(2)}) %copy-start.2) | copy-done | bytes 1048600
  11.8 1.7 %attention.1.after_ref = bf16[128,1024]{1,0:T(8,128)(2,1)S(1)} custom-call(s32[1,256]{1,0:T(1,128)S(1)} %bitcast.68, bf16[1024,640]{1,0:T(8,128)(2,1)S(1)} %get-tuple-element.15.heads_ref, f32[1024,128]{1,0:T(8,128)S(1)} %get-tuple-element.16.scores_ref, bf16[8,512,128]{2,1,0:T(8,128)(2,1)S(1)} %copy-done.2, bf16[576,128]{1,0:T(8,128)(2,1)S(1)} %bitcast.66, ...), custom_call_target="tpu_custom_call" | custom-call | flops 570425344 | bytes 2228224 | tf_op jit(solution)/shard_map/attention/pallas_call | solution.py:182
  13.9 1.8 %collective-permute-start.1 = (bf16[128,1024]{1,0:T(8,128)(2,1)S(1)}, bf16[128,1024]{1,0:T(8,128)(2,1)S(1)}, u32[]{:S(2)}, u32[]{:S(2)}) collective-permute-start(bf16[128,1024]{1,0:T(8,128)(2,1)S(1)} %attention.1.after_ref), channel_id=1, source_target_pairs={{0,16},{16,0},{1,17},{17,1},{2,18},{18,2},{3,19},{19,3},{4,20},{20... | collective-permute-start | bytes 786440 | tf_op jit(solution)/shard_map/ppermute | solution.py:346
  15.7 3.1 %copy-done = bf16[1024,3584]{1,0:T(8,128)(2,1)S(1)} copy-done((bf16[1024,3584]{1,0:T(8,128)(2,1)S(1)}, bf16[1024,3584]{1,0:T(8,128)(2,1)}, u32[]{:S(2)}) %copy-start) | copy-done | bytes 7340056
  19.5 2.1 %collective-permute-done.1 = bf16[128,1024]{1,0:T(8,128)(2,1)S(1)} collective-permute-done((bf16[128,1024]{1,0:T(8,128)(2,1)S(1)}, bf16[128,1024]{1,0:T(8,128)(2,1)S(1)}, u32[]{:S(2)}, u32[]{:S(2)}) %collective-permute-start.1) | collective-permute-done | bytes 262176 | tf_op jit(solution)/shard_map/ppermute | solution.py:346
  25.1 1.2 %collective-permute-done.6 = bf16[8,16,1792]{2,1,0:T(8,128)(2,1)S(1)} collective-permute-done((bf16[8,16,1792]{2,1,0:T(8,128)(2,1)S(1)}, bf16[8,16,1792]{2,1,0:T(8,128)(2,1)S(1)}, u32[]{:S(2)}, u32[]{:S(2)}) %collective-permute-start.6) | collective-permute-done | bytes 458784 | tf_op jit(solution)/shard_map/ppermute | solution.py:59
  26.4 1.6 %collective-permute-start.7 = (bf16[4,16,1792]{2,1,0:T(8,128)(2,1)S(1)}, bf16[4,16,1792]{2,1,0:T(8,128)(2,1)S(1)}, u32[]{:S(2)}, u32[]{:S(2)}) collective-permute-start(bf16[4,16,1792]{2,1,0:T(8,128)(2,1)S(1)} %slice.245), channel_id=1, source_target_pairs={{0,2},{1,5},{2,0},{3,7},{4,6},{5,1},{6,4},{7,3},{8,10},{9,13},{10,... | collective-permute-start | bytes 688136 | tf_op jit(solution)/shard_map/ppermute | solution.py:59
  28.7 3.8 %collective-permute-done.7 = bf16[4,16,1792]{2,1,0:T(8,128)(2,1)S(1)} collective-permute-done((bf16[4,16,1792]{2,1,0:T(8,128)(2,1)S(1)}, bf16[4,16,1792]{2,1,0:T(8,128)(2,1)S(1)}, u32[]{:S(2)}, u32[]{:S(2)}) %collective-permute-start.7) | collective-permute-done | bytes 229408 | tf_op jit(solution)/shard_map/ppermute | solution.py:59
  32.6 1.6 %collective-permute-start.8 = (bf16[2,16,1792]{2,1,0:T(8,128)(2,1)S(1)}, bf16[2,16,1792]{2,1,0:T(8,128)(2,1)S(1)}, u32[]{:S(2)}, u32[]{:S(2)}) collective-permute-start(bf16[2,16,1792]{2,1,0:T(8,128)(2,1)S(1)} %slice.247), channel_id=1, source_target_pairs={{0,4},{1,3},{2,6},{3,1},{4,0},{5,7},{6,2},{7,5},{8,12},{9,11},{10,... | collective-permute-start | bytes 344072 | tf_op jit(solution)/shard_map/ppermute | solution.py:59
  35.4 1.6 %collective-permute-start.4 = (bf16[2,16,1792]{2,1,0:T(8,128)(2,1)S(1)}, bf16[2,16,1792]{2,1,0:T(8,128)(2,1)S(1)}, u32[]{:S(2)}, u32[]{:S(2)}) collective-permute-start(bf16[2,16,1792]{2,1,0:T(8,128)(2,1)S(1)} %slice.238), channel_id=1, source_target_pairs={{0,4},{1,3},{2,6},{3,1},{4,0},{5,7},{6,2},{7,5},{8,12},{9,11},{10,... | collective-permute-start | bytes 344072 | tf_op jit(solution)/shard_map/ppermute | solution.py:59
  37.5 2.8 %collective-permute-done.4 = bf16[2,16,1792]{2,1,0:T(8,128)(2,1)S(1)} collective-permute-done((bf16[2,16,1792]{2,1,0:T(8,128)(2,1)S(1)}, bf16[2,16,1792]{2,1,0:T(8,128)(2,1)S(1)}, u32[]{:S(2)}, u32[]{:S(2)}) %collective-permute-start.4) | collective-permute-done | bytes 114720 | tf_op jit(solution)/shard_map/ppermute | solution.py:59
  40.4 2.6 %collective-permute-start.5 = (bf16[2,16,1792]{2,1,0:T(8,128)(2,1)S(1)}, bf16[2,16,1792]{2,1,0:T(8,128)(2,1)S(1)}, u32[]{:S(2)}, u32[]{:S(2)}) collective-permute-start(bf16[2,16,1792]{2,1,0:T(8,128)(2,1)S(1)} %fusion.82.after_ref), channel_id=1, source_target_pairs={{0,8},{1,9},{2,10},{3,11},{4,12},{5,13},{6,14},{7,15},{8,0},{9,1},... | collective-permute-start | bytes 344072 | tf_op jit(solution)/shard_map/ppermute | solution.py:392
  43.5 7.1 %collective-permute-done.5.got_ref = bf16[2,16,1792]{2,1,0:T(8,128)(2,1)S(1)} collective-permute-done((bf16[2,16,1792]{2,1,0:T(8,128)(2,1)S(1)}, bf16[2,16,1792]{2,1,0:T(8,128)(2,1)S(1)}, u32[]{:S(2)}, u32[]{:S(2)}) %collective-permute-start.5) | collective-permute-done | bytes 114720 | tf_op jit(solution)/shard_map/ppermute | solution.py:392
  53.1 3.6 %collective-permute-done.13 = bf16[2,16,1792]{2,1,0:T(8,128)(2,1)S(1)} collective-permute-done((bf16[2,16,1792]{2,1,0:T(8,128)(2,1)S(1)}, bf16[2,16,1792]{2,1,0:T(8,128)(2,1)S(1)}, u32[]{:S(2)}, u32[]{:S(2)}) %collective-permute-start.13) | collective-permute-done | bytes 114720 | tf_op jit(solution)/shard_map/ppermute | solution.py:64
  56.7 1.6 %collective-permute-start.14 = (bf16[4,16,1792]{2,1,0:T(8,128)(2,1)S(1)}, bf16[4,16,1792]{2,1,0:T(8,128)(2,1)S(1)}, u32[]{:S(2)}, u32[]{:S(2)}) collective-permute-start(bf16[4,16,1792]{2,1,0:T(8,128)(2,1)S(1)} %pad_maximum_fusion.7), channel_id=1, source_target_pairs={{0,2},{1,5},{2,0},{3,7},{4,6},{5,1},{6,4},{7,3},{8,10},{9,13},{10,... | collective-permute-start | bytes 688136 | tf_op jit(solution)/shard_map/ppermute | solution.py:64
  59.4 1.6 %collective-permute-start.11 = (bf16[4,16,1920]{2,1,0:T(8,128)(2,1)S(1)}, bf16[4,16,1920]{2,1,0:T(8,128)(2,1)S(1)}, u32[]{:S(2)}, u32[]{:S(2)}) collective-permute-start(bf16[4,16,1920]{2,1,0:T(8,128)(2,1)S(1)} %pad_maximum_fusion.4), channel_id=1, source_target_pairs={{0,2},{1,5},{2,0},{3,7},{4,6},{5,1},{6,4},{7,3},{8,10},{9,13},{10,... | collective-permute-start | bytes 737288 | tf_op jit(solution)/shard_map/ppermute | solution.py:64
  61.0 1.8 %collective-permute-done.14 = bf16[4,16,1792]{2,1,0:T(8,128)(2,1)S(1)} collective-permute-done((bf16[4,16,1792]{2,1,0:T(8,128)(2,1)S(1)}, bf16[4,16,1792]{2,1,0:T(8,128)(2,1)S(1)}, u32[]{:S(2)}, u32[]{:S(2)}) %collective-permute-start.14) | collective-permute-done | bytes 229408 | tf_op jit(solution)/shard_map/ppermute | solution.py:64
  62.9 2.7 %collective-permute-done.11 = bf16[4,16,1920]{2,1,0:T(8,128)(2,1)S(1)} collective-permute-done((bf16[4,16,1920]{2,1,0:T(8,128)(2,1)S(1)}, bf16[4,16,1920]{2,1,0:T(8,128)(2,1)S(1)}, u32[]{:S(2)}, u32[]{:S(2)}) %collective-permute-start.11) | collective-permute-done | bytes 245792 | tf_op jit(solution)/shard_map/ppermute | solution.py:64
  66.4 1.4 %slice-done.2 = s8[4194304]{0:T(1024)(128)(4,1)S(1)} async-done(((s8[7340032]{0:T(1024)(128)(4,1)}), s8[4194304]{0:T(1024)(128)(4,1)S(1)}, s32[]{:S(2)}) %slice-start.2) | async-done | bytes 4194328
  73.8 1.3 %collective-permute-start.16 = (bf16[144,2048]{1,0:T(8,128)(2,1)S(1)}, bf16[144,2048]{1,0:T(8,128)(2,1)S(1)}, u32[]{:S(2)}, u32[]{:S(2)}) collective-permute-start(bf16[144,2048]{1,0:T(8,128)(2,1)S(1)} %fusion.34.after_ref), channel_id=1, source_target_pairs={{0,16},{16,0},{1,17},{17,1},{2,18},{18,2},{3,19},{19,3},{4,20},{20... | collective-permute-start | bytes 1769480 | tf_op jit(solution)/shard_map/ppermute | solution.py:442
  76.8 11.6 %collective-permute-done.17 = f32[256]{0:T(256)S(1)} collective-permute-done((f32[256]{0:T(256)S(1)}, f32[256]{0:T(256)S(1)}, u32[]{:S(2)}, u32[]{:S(2)}) %collective-permute-start.17) | collective-permute-done | bytes 1056 | tf_op jit(solution)/shard_map/ppermute | solution.py:420
  92.2 1.2 %collective-permute-done.18 = bf16[8,16,1792]{2,1,0:T(8,128)(2,1)S(1)} collective-permute-done((bf16[8,16,1792]{2,1,0:T(8,128)(2,1)S(1)}, bf16[8,16,1792]{2,1,0:T(8,128)(2,1)S(1)}, u32[]{:S(2)}, u32[]{:S(2)}) %collective-permute-start.18) | collective-permute-done | bytes 458784 | tf_op jit(solution)/shard_map/ppermute | solution.py:59
  93.5 1.6 %collective-permute-start.19 = (bf16[4,16,1792]{2,1,0:T(8,128)(2,1)S(1)}, bf16[4,16,1792]{2,1,0:T(8,128)(2,1)S(1)}, u32[]{:S(2)}, u32[]{:S(2)}) collective-permute-start(bf16[4,16,1792]{2,1,0:T(8,128)(2,1)S(1)} %slice.267), channel_id=1, source_target_pairs={{0,2},{1,5},{2,0},{3,7},{4,6},{5,1},{6,4},{7,3},{8,10},{9,13},{10,... | collective-permute-start | bytes 688136 | tf_op jit(solution)/shard_map/ppermute | solution.py:59
  95.8 3.8 %collective-permute-done.19 = bf16[4,16,1792]{2,1,0:T(8,128)(2,1)S(1)} collective-permute-done((bf16[4,16,1792]{2,1,0:T(8,128)(2,1)S(1)}, bf16[4,16,1792]{2,1,0:T(8,128)(2,1)S(1)}, u32[]{:S(2)}, u32[]{:S(2)}) %collective-permute-start.19) | collective-permute-done | bytes 229408 | tf_op jit(solution)/shard_map/ppermute | solution.py:59
  99.8 2.7 %collective-permute-done.23 = bf16[4,16,1792]{2,1,0:T(8,128)(2,1)S(1)} collective-permute-done((bf16[4,16,1792]{2,1,0:T(8,128)(2,1)S(1)}, bf16[4,16,1792]{2,1,0:T(8,128)(2,1)S(1)}, u32[]{:S(2)}, u32[]{:S(2)}) %collective-permute-start.23) | collective-permute-done | bytes 229408 | tf_op jit(solution)/shard_map/ppermute | solution.py:59
  102.6 1.9 %collective-permute-done.20 = bf16[2,16,1792]{2,1,0:T(8,128)(2,1)S(1)} collective-permute-done((bf16[2,16,1792]{2,1,0:T(8,128)(2,1)S(1)}, bf16[2,16,1792]{2,1,0:T(8,128)(2,1)S(1)}, u32[]{:S(2)}, u32[]{:S(2)}) %collective-permute-start.20) | collective-permute-done | bytes 114720 | tf_op jit(solution)/shard_map/ppermute | solution.py:59
  104.6 1.4 %collective-permute-start.21 = (bf16[1,16,1792]{2,1,0:T(8,128)(2,1)S(1)}, bf16[1,16,1792]{2,1,0:T(8,128)(2,1)S(1)}, u32[]{:S(2)}, u32[]{:S(2)}) collective-permute-start(bf16[1,16,1792]{2,1,0:T(8,128)(2,1)S(1)} %slice.271), channel_id=1, source_target_pairs={{0,8},{1,9},{2,10},{3,11},{4,12},{5,13},{6,14},{7,15},{8,0},{9,1},... | collective-permute-start | bytes 172040 | tf_op jit(solution)/shard_map/ppermute | solution.py:59
  106.0 2.0 %collective-permute-done.24 = bf16[2,16,1792]{2,1,0:T(8,128)(2,1)S(1)} collective-permute-done((bf16[2,16,1792]{2,1,0:T(8,128)(2,1)S(1)}, bf16[2,16,1792]{2,1,0:T(8,128)(2,1)S(1)}, u32[]{:S(2)}, u32[]{:S(2)}) %collective-permute-start.24) | collective-permute-done | bytes 114720 | tf_op jit(solution)/shard_map/ppermute | solution.py:59
  109.2 2.1 %collective-permute-done.21 = bf16[1,16,1792]{2,1,0:T(8,128)(2,1)S(1)} collective-permute-done((bf16[1,16,1792]{2,1,0:T(8,128)(2,1)S(1)}, bf16[1,16,1792]{2,1,0:T(8,128)(2,1)S(1)}, u32[]{:S(2)}, u32[]{:S(2)}) %collective-permute-start.21) | collective-permute-done | bytes 57376 | tf_op jit(solution)/shard_map/ppermute | solution.py:59
  111.2 2.2 %collective-permute-done.25 = bf16[1,16,1792]{2,1,0:T(8,128)(2,1)S(1)} collective-permute-done((bf16[1,16,1792]{2,1,0:T(8,128)(2,1)S(1)}, bf16[1,16,1792]{2,1,0:T(8,128)(2,1)S(1)}, u32[]{:S(2)}, u32[]{:S(2)}) %collective-permute-start.25) | collective-permute-done | bytes 57376 | tf_op jit(solution)/shard_map/ppermute | solution.py:59
  (143 shorter events, 30.3 us)
Async XLA Ops:
  0.0 13.7 %copy-start.8 = (f32[16,8]{0,1:T(8,128)S(1)}, f32[16,8]{0,1:T(8,128)}, u32[]{:S(2)}) copy-start(f32[16,8]{0,1:T(8,128)} %param.20) | copy-start | bytes 1540
  0.0 13.6 %copy-start.7 = (s32[16,8]{0,1:T(8,128)S(1)}, s32[16,8]{0,1:T(8,128)}, u32[]{:S(2)}) copy-start(s32[16,8]{0,1:T(8,128)} %param.19) | copy-start | bytes 1540
  0.0 9.0 %collective-permute-start = (bf16[576,128]{1,0:T(8,128)(2,1)}, bf16[576,128]{1,0:T(8,128)(2,1)S(1)}, u32[]{:S(2)}, u32[]{:S(2)}) collective-permute-start(bf16[576,128]{1,0:T(8,128)(2,1)} %bitcast.64), channel_id=1, source_target_pairs={{0,16},{1,17},{2,18},{3,19},{4,20},{5,21},{6,22},{7,23},{8,24},{9,... | collective-permute-start | bytes 442376 | tf_op jit(solution)/shard_map/ppermute | solution.py:335
  13.9 7.8 %collective-permute-start.1 = (bf16[128,1024]{1,0:T(8,128)(2,1)S(1)}, bf16[128,1024]{1,0:T(8,128)(2,1)S(1)}, u32[]{:S(2)}, u32[]{:S(2)}) collective-permute-start(bf16[128,1024]{1,0:T(8,128)(2,1)S(1)} %attention.1.after_ref), channel_id=1, source_target_pairs={{0,16},{16,0},{1,17},{17,1},{2,18},{18,2},{3,19},{19,3},{4,20},{20... | collective-permute-start | bytes 786440 | tf_op jit(solution)/shard_map/ppermute | solution.py:346
  24.3 41.5 %slice-start = ((s8[7340032]{0:T(1024)(128)(4,1)}), s8[4194304]{0:T(1024)(128)(4,1)S(1)}, s32[]{:S(2)}) async-start(s8[7340032]{0:T(1024)(128)(4,1)} %bitcast.55), calls=%async_computation | async-start | bytes 8388608
  24.4 1.9 %collective-permute-start.6 = (bf16[8,16,1792]{2,1,0:T(8,128)(2,1)S(1)}, bf16[8,16,1792]{2,1,0:T(8,128)(2,1)S(1)}, u32[]{:S(2)}, u32[]{:S(2)}) collective-permute-start(bf16[8,16,1792]{2,1,0:T(8,128)(2,1)S(1)} %bitcast.78), channel_id=1, source_target_pairs={{0,1},{1,0},{2,3},{3,2},{4,5},{5,4},{6,7},{7,6},{8,9},{9,8},{10,11... | collective-permute-start | bytes 1376264 | tf_op jit(solution)/shard_map/ppermute | solution.py:59
  24.6 15.8 %copy-start.6 = (bf16[16,3584]{1,0:T(8,128)(2,1)S(1)}, bf16[16,3584]{1,0:T(8,128)(2,1)}, u32[]{:S(2)}) copy-start(bf16[16,3584]{1,0:T(8,128)(2,1)} %param.17) | copy-start | bytes 344068
  24.6 3.4 %collective-permute-start.2 = (bf16[8,16,1792]{2,1,0:T(8,128)(2,1)S(1)}, bf16[8,16,1792]{2,1,0:T(8,128)(2,1)S(1)}, u32[]{:S(2)}, u32[]{:S(2)}) collective-permute-start(bf16[8,16,1792]{2,1,0:T(8,128)(2,1)S(1)} %bitcast.76), channel_id=1, source_target_pairs={{0,1},{1,0},{2,3},{3,2},{4,5},{5,4},{6,7},{7,6},{8,9},{9,8},{10,11... | collective-permute-start | bytes 1376264 | tf_op jit(solution)/shard_map/ppermute | solution.py:59
  26.4 6.1 %collective-permute-start.7 = (bf16[4,16,1792]{2,1,0:T(8,128)(2,1)S(1)}, bf16[4,16,1792]{2,1,0:T(8,128)(2,1)S(1)}, u32[]{:S(2)}, u32[]{:S(2)}) collective-permute-start(bf16[4,16,1792]{2,1,0:T(8,128)(2,1)S(1)} %slice.245), channel_id=1, source_target_pairs={{0,2},{1,5},{2,0},{3,7},{4,6},{5,1},{6,4},{7,3},{8,10},{9,13},{10,... | collective-permute-start | bytes 688136 | tf_op jit(solution)/shard_map/ppermute | solution.py:59
  28.1 7.2 %collective-permute-start.3 = (bf16[4,16,1792]{2,1,0:T(8,128)(2,1)S(1)}, bf16[4,16,1792]{2,1,0:T(8,128)(2,1)S(1)}, u32[]{:S(2)}, u32[]{:S(2)}) collective-permute-start(bf16[4,16,1792]{2,1,0:T(8,128)(2,1)S(1)} %slice.236), channel_id=1, source_target_pairs={{0,2},{1,5},{2,0},{3,7},{4,6},{5,1},{6,4},{7,3},{8,10},{9,13},{10,... | collective-permute-start | bytes 688136 | tf_op jit(solution)/shard_map/ppermute | solution.py:59
  32.6 33.2 %slice-start.1 = ((s8[7340032]{0:T(1024)(128)(4,1)}), s8[3145728]{0:T(1024)(128)(4,1)S(1)}, s32[]{:S(2)}) async-start(s8[7340032]{0:T(1024)(128)(4,1)} %bitcast.55), calls=%async_computation.1 | async-start | bytes 6291456
  32.6 4.9 %collective-permute-start.8 = (bf16[2,16,1792]{2,1,0:T(8,128)(2,1)S(1)}, bf16[2,16,1792]{2,1,0:T(8,128)(2,1)S(1)}, u32[]{:S(2)}, u32[]{:S(2)}) collective-permute-start(bf16[2,16,1792]{2,1,0:T(8,128)(2,1)S(1)} %slice.247), channel_id=1, source_target_pairs={{0,4},{1,3},{2,6},{3,1},{4,0},{5,7},{6,2},{7,5},{8,12},{9,11},{10,... | collective-permute-start | bytes 344072 | tf_op jit(solution)/shard_map/ppermute | solution.py:59
  35.4 4.9 %collective-permute-start.4 = (bf16[2,16,1792]{2,1,0:T(8,128)(2,1)S(1)}, bf16[2,16,1792]{2,1,0:T(8,128)(2,1)S(1)}, u32[]{:S(2)}, u32[]{:S(2)}) collective-permute-start(bf16[2,16,1792]{2,1,0:T(8,128)(2,1)S(1)} %slice.238), channel_id=1, source_target_pairs={{0,4},{1,3},{2,6},{3,1},{4,0},{5,7},{6,2},{7,5},{8,12},{9,11},{10,... | collective-permute-start | bytes 344072 | tf_op jit(solution)/shard_map/ppermute | solution.py:59
  40.4 10.2 %collective-permute-start.5 = (bf16[2,16,1792]{2,1,0:T(8,128)(2,1)S(1)}, bf16[2,16,1792]{2,1,0:T(8,128)(2,1)S(1)}, u32[]{:S(2)}, u32[]{:S(2)}) collective-permute-start(bf16[2,16,1792]{2,1,0:T(8,128)(2,1)S(1)} %fusion.82.after_ref), channel_id=1, source_target_pairs={{0,8},{1,9},{2,10},{3,11},{4,12},{5,13},{6,14},{7,15},{8,0},{9,1},... | collective-permute-start | bytes 344072 | tf_op jit(solution)/shard_map/ppermute | solution.py:392
  43.1 8.8 %collective-permute-start.9 = (bf16[2,16,1920]{2,1,0:T(8,128)(2,1)S(1)}, bf16[2,16,1920]{2,1,0:T(8,128)(2,1)S(1)}, u32[]{:S(2)}, u32[]{:S(2)}) collective-permute-start(bf16[2,16,1920]{2,1,0:T(8,128)(2,1)S(1)} %fusion.50), channel_id=1, source_target_pairs={{0,8},{1,9},{2,10},{3,11},{4,12},{5,13},{6,14},{7,15},{8,0},{9,1},... | collective-permute-start | bytes 368648 | tf_op jit(solution)/shard_map/ppermute | solution.py:392
  50.7 6.0 %collective-permute-start.13 = (bf16[2,16,1792]{2,1,0:T(8,128)(2,1)S(1)}, bf16[2,16,1792]{2,1,0:T(8,128)(2,1)S(1)}, u32[]{:S(2)}, u32[]{:S(2)}) collective-permute-start(bf16[2,16,1792]{2,1,0:T(8,128)(2,1)S(1)} %get-tuple-element.23), channel_id=1, source_target_pairs={{0,4},{1,3},{2,6},{3,1},{4,0},{5,7},{6,2},{7,5},{8,12},{9,11},{10,... | collective-permute-start | bytes 344072 | tf_op jit(solution)/shard_map/ppermute | solution.py:64
  52.1 7.2 %collective-permute-start.10 = (bf16[2,16,1920]{2,1,0:T(8,128)(2,1)S(1)}, bf16[2,16,1920]{2,1,0:T(8,128)(2,1)S(1)}, u32[]{:S(2)}, u32[]{:S(2)}) collective-permute-start(bf16[2,16,1920]{2,1,0:T(8,128)(2,1)S(1)} %get-tuple-element.22), channel_id=1, source_target_pairs={{0,4},{1,3},{2,6},{3,1},{4,0},{5,7},{6,2},{7,5},{8,12},{9,11},{10,... | collective-permute-start | bytes 368648 | tf_op jit(solution)/shard_map/ppermute | solution.py:64
  56.7 6.1 %collective-permute-start.14 = (bf16[4,16,1792]{2,1,0:T(8,128)(2,1)S(1)}, bf16[4,16,1792]{2,1,0:T(8,128)(2,1)S(1)}, u32[]{:S(2)}, u32[]{:S(2)}) collective-permute-start(bf16[4,16,1792]{2,1,0:T(8,128)(2,1)S(1)} %pad_maximum_fusion.7), channel_id=1, source_target_pairs={{0,2},{1,5},{2,0},{3,7},{4,6},{5,1},{6,4},{7,3},{8,10},{9,13},{10,... | collective-permute-start | bytes 688136 | tf_op jit(solution)/shard_map/ppermute | solution.py:64
  59.4 6.3 %collective-permute-start.11 = (bf16[4,16,1920]{2,1,0:T(8,128)(2,1)S(1)}, bf16[4,16,1920]{2,1,0:T(8,128)(2,1)S(1)}, u32[]{:S(2)}, u32[]{:S(2)}) collective-permute-start(bf16[4,16,1920]{2,1,0:T(8,128)(2,1)S(1)} %pad_maximum_fusion.4), channel_id=1, source_target_pairs={{0,2},{1,5},{2,0},{3,7},{4,6},{5,1},{6,4},{7,3},{8,10},{9,13},{10,... | collective-permute-start | bytes 737288 | tf_op jit(solution)/shard_map/ppermute | solution.py:64
  62.9 6.5 %collective-permute-start.15 = (bf16[8,16,1792]{2,1,0:T(8,128)(2,1)S(1)}, bf16[8,16,1792]{2,1,0:T(8,128)(2,1)S(1)}, u32[]{:S(2)}, u32[]{:S(2)}) collective-permute-start(bf16[8,16,1792]{2,1,0:T(8,128)(2,1)S(1)} %pad_maximum_fusion.3), channel_id=1, source_target_pairs={{0,1},{1,0},{2,3},{3,2},{4,5},{5,4},{6,7},{7,6},{8,9},{9,8},{10,11... | collective-permute-start | bytes 1376264 | tf_op jit(solution)/shard_map/ppermute | solution.py:64
  65.7 3.8 %collective-permute-start.12 = (bf16[8,16,1920]{2,1,0:T(8,128)(2,1)S(1)}, bf16[8,16,1920]{2,1,0:T(8,128)(2,1)S(1)}, u32[]{:S(2)}, u32[]{:S(2)}) collective-permute-start(bf16[8,16,1920]{2,1,0:T(8,128)(2,1)S(1)} %pad_maximum_fusion.2), channel_id=1, source_target_pairs={{0,1},{1,0},{2,3},{3,2},{4,5},{5,4},{6,7},{7,6},{8,9},{9,8},{10,11... | collective-permute-start | bytes 1474568 | tf_op jit(solution)/shard_map/ppermute | solution.py:64
  72.1 4.0 %slice-start.4 = ((s8[7340032]{0:T(1024)(128)(4,1)}), s8[4194304]{0:T(1024)(128)(4,1)S(1)}, s32[]{:S(2)}) async-start(s8[7340032]{0:T(1024)(128)(4,1)} %bitcast.61), calls=%async_computation.4 | async-start | bytes 8388608
  73.8 14.9 %collective-permute-start.16 = (bf16[144,2048]{1,0:T(8,128)(2,1)S(1)}, bf16[144,2048]{1,0:T(8,128)(2,1)S(1)}, u32[]{:S(2)}, u32[]{:S(2)}) collective-permute-start(bf16[144,2048]{1,0:T(8,128)(2,1)S(1)} %fusion.34.after_ref), channel_id=1, source_target_pairs={{0,16},{16,0},{1,17},{17,1},{2,18},{18,2},{3,19},{19,3},{4,20},{20... | collective-permute-start | bytes 1769480 | tf_op jit(solution)/shard_map/ppermute | solution.py:442
  75.2 13.3 %collective-permute-start.17 = (f32[256]{0:T(256)S(1)}, f32[256]{0:T(256)S(1)}, u32[]{:S(2)}, u32[]{:S(2)}) collective-permute-start(f32[256]{0:T(256)S(1)} %slice_reduce_fusion), channel_id=1, source_target_pairs={{0,16},{16,0},{1,17},{17,1},{2,18},{18,2},{3,19},{19,3},{4,20},{20... | collective-permute-start | bytes 3080 | tf_op jit(solution)/shard_map/ppermute | solution.py:420
  91.5 1.9 %collective-permute-start.18 = (bf16[8,16,1792]{2,1,0:T(8,128)(2,1)S(1)}, bf16[8,16,1792]{2,1,0:T(8,128)(2,1)S(1)}, u32[]{:S(2)}, u32[]{:S(2)}) collective-permute-start(bf16[8,16,1792]{2,1,0:T(8,128)(2,1)S(1)} %bitcast.79), channel_id=1, source_target_pairs={{0,1},{1,0},{2,3},{3,2},{4,5},{5,4},{6,7},{7,6},{8,9},{9,8},{10,11... | collective-permute-start | bytes 1376264 | tf_op jit(solution)/shard_map/ppermute | solution.py:59
  91.7 3.5 %collective-permute-start.22 = (bf16[8,16,1792]{2,1,0:T(8,128)(2,1)S(1)}, bf16[8,16,1792]{2,1,0:T(8,128)(2,1)S(1)}, u32[]{:S(2)}, u32[]{:S(2)}) collective-permute-start(bf16[8,16,1792]{2,1,0:T(8,128)(2,1)S(1)} %bitcast.77), channel_id=1, source_target_pairs={{0,1},{1,0},{2,3},{3,2},{4,5},{5,4},{6,7},{7,6},{8,9},{9,8},{10,11... | collective-permute-start | bytes 1376264 | tf_op jit(solution)/shard_map/ppermute | solution.py:59
  93.5 6.1 %collective-permute-start.19 = (bf16[4,16,1792]{2,1,0:T(8,128)(2,1)S(1)}, bf16[4,16,1792]{2,1,0:T(8,128)(2,1)S(1)}, u32[]{:S(2)}, u32[]{:S(2)}) collective-permute-start(bf16[4,16,1792]{2,1,0:T(8,128)(2,1)S(1)} %slice.267), channel_id=1, source_target_pairs={{0,2},{1,5},{2,0},{3,7},{4,6},{5,1},{6,4},{7,3},{8,10},{9,13},{10,... | collective-permute-start | bytes 688136 | tf_op jit(solution)/shard_map/ppermute | solution.py:59
  95.3 7.2 %collective-permute-start.23 = (bf16[4,16,1792]{2,1,0:T(8,128)(2,1)S(1)}, bf16[4,16,1792]{2,1,0:T(8,128)(2,1)S(1)}, u32[]{:S(2)}, u32[]{:S(2)}) collective-permute-start(bf16[4,16,1792]{2,1,0:T(8,128)(2,1)S(1)} %slice.276), channel_id=1, source_target_pairs={{0,2},{1,5},{2,0},{3,7},{4,6},{5,1},{6,4},{7,3},{8,10},{9,13},{10,... | collective-permute-start | bytes 688136 | tf_op jit(solution)/shard_map/ppermute | solution.py:59
  99.7 4.9 %collective-permute-start.20 = (bf16[2,16,1792]{2,1,0:T(8,128)(2,1)S(1)}, bf16[2,16,1792]{2,1,0:T(8,128)(2,1)S(1)}, u32[]{:S(2)}, u32[]{:S(2)}) collective-permute-start(bf16[2,16,1792]{2,1,0:T(8,128)(2,1)S(1)} %slice.269), channel_id=1, source_target_pairs={{0,4},{1,3},{2,6},{3,1},{4,0},{5,7},{6,2},{7,5},{8,12},{9,11},{10,... | collective-permute-start | bytes 344072 | tf_op jit(solution)/shard_map/ppermute | solution.py:59
  102.5 5.5 %collective-permute-start.24 = (bf16[2,16,1792]{2,1,0:T(8,128)(2,1)S(1)}, bf16[2,16,1792]{2,1,0:T(8,128)(2,1)S(1)}, u32[]{:S(2)}, u32[]{:S(2)}) collective-permute-start(bf16[2,16,1792]{2,1,0:T(8,128)(2,1)S(1)} %slice.278), channel_id=1, source_target_pairs={{0,4},{1,3},{2,6},{3,1},{4,0},{5,7},{6,2},{7,5},{8,12},{9,11},{10,... | collective-permute-start | bytes 344072 | tf_op jit(solution)/shard_map/ppermute | solution.py:59
  104.6 6.6 %collective-permute-start.21 = (bf16[1,16,1792]{2,1,0:T(8,128)(2,1)S(1)}, bf16[1,16,1792]{2,1,0:T(8,128)(2,1)S(1)}, u32[]{:S(2)}, u32[]{:S(2)}) collective-permute-start(bf16[1,16,1792]{2,1,0:T(8,128)(2,1)S(1)} %slice.271), channel_id=1, source_target_pairs={{0,8},{1,9},{2,10},{3,11},{4,12},{5,13},{6,14},{7,15},{8,0},{9,1},... | collective-permute-start | bytes 172040 | tf_op jit(solution)/shard_map/ppermute | solution.py:59
  108.1 5.4 %collective-permute-start.25 = (bf16[1,16,1792]{2,1,0:T(8,128)(2,1)S(1)}, bf16[1,16,1792]{2,1,0:T(8,128)(2,1)S(1)}, u32[]{:S(2)}, u32[]{:S(2)}) collective-permute-start(bf16[1,16,1792]{2,1,0:T(8,128)(2,1)S(1)} %slice.280), channel_id=1, source_target_pairs={{0,8},{1,9},{2,10},{3,11},{4,12},{5,13},{6,14},{7,15},{8,0},{9,1},... | collective-permute-start | bytes 172040 | tf_op jit(solution)/shard_map/ppermute | solution.py:59
  (9 other events, 16.5 us)

commit v3 on v2

--- a/solution.py
+++ b/solution.py
@@ -15,6 +15,7 @@
 score_scale = (1.0 + 0.1 * math.log(40.0)) ** 2 / math.sqrt(192.0)
 masked_score = -1e30
 PARTS = 2
+HIDDEN_PARTS = 2
 
 
 def split_edges(width, parts):
@@ -39,18 +40,17 @@
     return [(index, index ^ (1 << step_bits(bits, index & 1)[step])) for index in range(count)]
 
 
-def chunk_owners(count, rank):
+def chunk_owners(count, rank, lane, number):
     bits = count.bit_length() - 1
-    number = jnp.arange(count, dtype=jnp.int32)
     flip = number >> (bits - 1)
     distances = []
-    for lane in range(2):
-        order = step_bits(bits, lane)
-        distance = jnp.zeros((count,), jnp.int32)
+    for side in range(2):
+        order = step_bits(bits, side)
+        distance = jnp.zeros_like(number)
         for step in range(1, bits):
             distance = distance | ((number >> (bits - 1 - step)) & 1) << order[step]
         distances.append(distance)
-    other_lane = ((rank & 1) ^ flip) == 1
+    other_lane = (lane ^ flip) == 1
     return rank ^ flip ^ jnp.where(other_lane, distances[1], distances[0])
 
 
@@ -64,7 +64,21 @@
     return jnp.concatenate([array, lax.ppermute(array, "ep", crossing(count, step))], axis=0)
 
 
-def scores_kernel(pair_count, query_ref, keys_ref, heads_ref, scores_ref):
+def scores_kernel(
+    pair_count,
+    query_ref,
+    keys_ref,
+    up_ref,
+    doc_ref,
+    heads_ref,
+    scores_ref,
+    own_ref,
+    up_out_ref,
+    doc_out_ref,
+):
+    own_ref[...] = keys_ref[...]
+    up_out_ref[...] = up_ref[...]
+    doc_out_ref[...] = doc_ref[...]
     rows = query_ref.shape[0]
     pair_width = query_ref.shape[1] // pair_count
     width = heads_ref.shape[1]
@@ -159,18 +173,30 @@
         vmem_limit_bytes=(8 << 20) + 8 * heads * rows * (key_count + KVL) * 4
     )
     stacked = lambda columns: pl.BlockSpec((heads * rows, columns), lambda step: (step, 0))
-    arranged, scores = pl.pallas_call(
+    up_block = pl.BlockSpec((heads, value_in, value_width), lambda step: (step, 0, 0))
+    arranged, scores, own, w_uv, docs = pl.pallas_call(
         functools.partial(scores_kernel, pair_count),
         out_shape=(
             jax.ShapeDtypeStruct((head_count * rows, width), jnp.bfloat16),
             jax.ShapeDtypeStruct((head_count * rows, first_keys), jnp.float32),
+            jax.ShapeDtypeStruct(blocks[0].shape, jnp.bfloat16),
+            jax.ShapeDtypeStruct(w_uv.shape, jnp.bfloat16),
+            jax.ShapeDtypeStruct((1, key_count), jnp.int32),
         ),
         grid=grid,
         in_specs=[
             pl.BlockSpec((rows, heads * query_width), lambda step: (0, step)),
             whole_block(blocks[0].shape),
+            up_block,
+            whole_block((1, key_count)),
         ],
-        out_specs=(stacked(width), stacked(first_keys)),
+        out_specs=(
+            stacked(width),
+            stacked(first_keys),
+            whole_block(blocks[0].shape),
+            up_block,
+            whole_block((1, key_count)),
+        ),
         compiler_params=params,
         cost_estimate=pl.CostEstimate(
             flops=2 * rows * head_count * first_keys * width,
@@ -178,7 +204,7 @@
             transcendentals=0,
         ),
         name="first_scores",
-    )(queries, blocks[0])
+    )(queries, blocks[0], w_uv, doc_ids[None])
     return pl.pallas_call(
         functools.partial(attend_kernel, pair_count),
         out_shape=jax.ShapeDtypeStruct((rows, head_count * value_width), jnp.bfloat16),
@@ -187,7 +213,7 @@
             whole_block((1, key_count)),
             stacked(width),
             stacked(first_keys),
-            pl.BlockSpec((heads, value_in, value_width), lambda step: (step, 0, 0)),
+            up_block,
             *(whole_block(block.shape) for block in blocks),
         ],
         out_specs=pl.BlockSpec((rows, heads * value_width), lambda step: (0, step)),
@@ -198,7 +224,7 @@
             transcendentals=rows * head_count * key_count,
         ),
         name="attention",
-    )(doc_ids[None], arranged, scores, w_uv, *blocks)
+    )(docs, arranged, scores, w_uv, own, *blocks[1:])
 
 
 def fetch_kernel(pieces, first, from_ref, after_ref, to_ref, sems):
@@ -330,18 +356,20 @@
     all_tokens = ep_count * token_count
     swap = [(0, 1), (1, 0)]
 
-    key_columns = latent.T
+    key_columns, ctx_rank, ep_rank, lane = lax.optimization_barrier(
+        (latent.T, ctx_rank, ep_rank, ep_rank & 1)
+    )
     if ctx_count == 2:
         blocks = [key_columns, lax.ppermute(key_columns, "ctx", [(0, 1)])]
     else:
         blocks = [lax.all_gather(key_columns, "ctx", axis=1, tiled=True)]
     head_values = attend(queries, blocks, doc_ids, w_uv)
-    route_ids, route_weights, head_values = lax.optimization_barrier(
-        (route_ids, route_weights, head_values)
-    )
-
-    owner = jnp.repeat(chunk_owners(ep_count, ep_rank), token_count)
+    route_ids, route_weights, norm_gain, head_values = lax.optimization_barrier(
+        (route_ids, route_weights, norm_gain, head_values)
+    )
+
     chunk = jnp.arange(all_tokens, dtype=jnp.int32) // token_count
+    owner = chunk_owners(ep_count, ep_rank, lane, chunk)
     if ctx_count == 2:
         other = lax.ppermute(head_values, "ctx", swap)
         w_out = fetched(w_out, head_values)
@@ -359,9 +387,9 @@
     )
 
     experts = jnp.arange(ep_count, dtype=jnp.int32)
-    named = route_ids[:, :, None] == experts[None, None, :]
-    chosen = jnp.sum(named.astype(jnp.float32), axis=1)
-    weights = jnp.sum(jnp.where(named, route_weights[:, :, None], 0.0), axis=1)
+    named = route_ids.T[:, :, None] == experts[None, None, :]
+    chosen = jnp.sum(named.astype(jnp.float32), axis=0)
+    weights = jnp.sum(jnp.where(named, route_weights.T[:, :, None], 0.0), axis=0)
     token_index = jnp.arange(token_count, dtype=jnp.int32)
     before = (token_index[:, None] > token_index[None, :]).astype(jnp.float32)
     place = jnp.sum(before[:, :, None] * chosen[None, :, :], axis=1)
@@ -393,6 +421,9 @@
         if part == 0:
             gate_weights = fetched(w_gate[0], sent)
             up_weights = fetched(w_up[0], sent)
+            got, gate_weights, up_weights = lax.optimization_barrier(
+                (got, gate_weights, up_weights)
+            )
         width = high - low
         if last:
             kept, array = normalised(facts_width, total, got, norm_gain[low:high], squares, facts)
@@ -426,31 +457,47 @@
     slot_scale = jnp.sum(jnp.where(placing, token_scale[None, :], 0.0), axis=1)
     slot_weight = jnp.sum(jnp.where(placing, token_weight[None, :], 0.0), axis=1)
     placing = placing.astype(jnp.bfloat16)
-    both = 0.0
-    for (low, high), features in zip(edges, arrived):
-        rows = jnp.dot(placing, features, preferred_element_type=jnp.float32).astype(jnp.bfloat16)
-        both = both + jnp.concatenate(
-            [
-                jnp.dot(rows, gate_weights[low:high], preferred_element_type=jnp.float32),
-                jnp.dot(rows, up_weights[low:high], preferred_element_type=jnp.float32),
-            ],
-            axis=1,
-        )
-    both = both.astype(jnp.bfloat16)
+    rows = [
+        jnp.dot(placing, features, preferred_element_type=jnp.float32).astype(jnp.bfloat16)
+        for features in arrived
+    ]
+    hidden = gate_weights.shape[1]
+    ranges = split_edges(hidden, HIDDEN_PARTS)
+    sums = []
+    for start, stop in ranges:
+        both = []
+        for weights in (gate_weights, up_weights):
+            total = 0.0
+            for (low, high), part_rows in zip(edges, rows):
+                total = total + jnp.dot(
+                    part_rows, weights[low:high, start:stop], preferred_element_type=jnp.float32
+                )
+            both.append(total.astype(jnp.bfloat16))
+        sums.append(jnp.concatenate(both, axis=1))
     if ctx_count == 2:
-        down_weights = fetched(w_down[0], both)
-        other_both = lax.ppermute(both, "ctx", swap)
-        both = both.astype(jnp.float32) + other_both.astype(jnp.float32)
+        others = [lax.ppermute(both, "ctx", swap) for both in sums]
+        down_weights = fetched(w_down[0], sums[-1])
+        others[0], down_weights = lax.optimization_barrier((others[0], down_weights))
+        sums = [
+            both.astype(jnp.float32) + other.astype(jnp.float32)
+            for both, other in zip(sums, others)
+        ]
     else:
         down_weights = w_down[0]
-        both = lax.psum(both, "ctx").astype(jnp.float32)
-    both = both * slot_scale[:, None]
-    hidden = both.shape[1] // 2
-    activated = (jax.nn.silu(both[:, :hidden]) * both[:, hidden:]).astype(jnp.bfloat16)
+        sums = [lax.psum(both, "ctx").astype(jnp.float32) for both in sums]
+    activated = []
+    for both in sums:
+        both = both * slot_scale[:, None]
+        half = both.shape[1] // 2
+        activated.append((jax.nn.silu(both[:, :half]) * both[:, half:]).astype(jnp.bfloat16))
     spread = placing.T
     outputs = []
     for (low, high), residual in zip(edges, residuals):
-        produced = jnp.dot(activated, down_weights[:, low:high], preferred_element_type=jnp.float32)
+        produced = 0.0
+        for (start, stop), part_rows in zip(ranges, activated):
+            produced = produced + jnp.dot(
+                part_rows, down_weights[start:stop, low:high], preferred_element_type=jnp.float32
+            )
         produced = (produced * slot_weight[:, None]).astype(jnp.bfloat16)
         produced = lax.optimization_barrier(produced)
         array = (

time: 114 us -> 110 us (0.965)
  local copies, waits for them, and re-layouts: 12.1 us -> 9.1 us
  waiting for transfers between devices: 56 us -> 54.1 us
    ppermute x1, waiting for transfers between devices: 11.6 us -> 5.75 us  [shards(): token_squares = token_squares + lax.ppermute(token_squares, 'ctx', swap)]
    ppermute x1 -> x2, waiting for transfers between devices: 0.01 us -> 5.31 us  [shards(): others = [lax.ppermute(both, 'ctx', swap) for both in sums]]
    ppermute x2, waiting for transfers between devices: 8.11 us -> 5.63 us  [shards(): got = lax.ppermute(sent, 'ep', crossing(ep_count, bits - 1))]
    unnamed x30, local copies, waits for them, and re-layouts: 10.6 us -> 8.7 us
    ppermute x6, waiting for transfers between devices: 9.14 us -> 10.9 us  [doubled(): lax.ppermute(array, 'ep', crossing(count, step))]
    ppermute x14, waiting for transfers between devices: 25 us -> 23.6 us  [halved(): got = lax.ppermute(array[half:], 'ep', crossing(count, step))]
    dot_general x6 -> x12, matrix products: 4.38 us -> 5.37 us  [the longest x8 3.58 us: shards(): jnp.dot(part_rows, weights[low:high, start:stop], preferred_element_type=...]
  transfers between devices with their start and end apart: 26 -> 27, of which waited for: 20 -> 22; matrix products, arithmetic and copies ran while one was open for 3% -> 3% of each run, Pallas kernels for 3% -> 3%
where the time goes in v3:
time: 110 us
  waiting for transfers between devices  54.1 us (49%)
  starting transfers between devices  27.6 us (25%)
  matrix products  9.55 us (9%)
  local copies, waits for them, and re-layouts  9.1 us (8%)
  Pallas kernels  5.27 us (5%)
  other arithmetic  3.46 us (3%)
    ppermute x14, waiting for transfers between devices, halved(): got = lax.ppermute(array[half:], 'ep', crossing(count, step))  23.6 us
    ppermute x14, starting transfers between devices, halved(): got = lax.ppermute(array[half:], 'ep', crossing(count, step))  11.9 us
    ppermute x6, waiting for transfers between devices, doubled(): lax.ppermute(array, 'ep', crossing(count, step))  10.9 us
    unnamed x30, local copies, waits for them, and re-layouts  8.7 us
    ppermute x1, waiting for transfers between devices, shards(): token_squares = token_squares + lax.ppermute(token_squares, 'ctx', swap)  5.75 us
    ppermute x2, waiting for transfers between devices, shards(): got = lax.ppermute(sent, 'ep', crossing(ep_count, bits - 1))  5.63 us
    ppermute x2, waiting for transfers between devices, shards(): others = [lax.ppermute(both, 'ctx', swap) for both in sums]  5.31 us
    ppermute x1, starting transfers between devices, shards(): blocks = [key_columns, lax.ppermute(key_columns, 'ctx', [(0, 1)])]  4.87 us
  transfers between devices with their start and end apart: 27, of which 22 were waited for; matrix products, arithmetic and copies ran while one was open for 3% of the time, Pallas kernels for 3%

profile of v3, /device:TPU:0, one launch (start us, length us, event | category | flops | bytes accessed | tf_op | source)
XLA Modules:
  0.0 109.8 jit_solution(9075139068625332551)
XLA Ops:
  0.0 4.9 %collective-permute-start = (bf16[576,128]{1,0:T(8,128)(2,1)}, bf16[576,128]{1,0:T(8,128)(2,1)S(1)}, u32[]{:S(2)}, u32[]{:S(2)}) collective-permute-start(bf16[576,128]{1,0:T(8,128)(2,1)} %bitcast.72), channel_id=1, source_target_pairs={{0,16},{1,17},{2,18},{3,19},{4,20},{5,21},{6,22},{7,23},{8,24},{9,... | collective-permute-start | bytes 442376 | tf_op jit(solution)/shard_map/ppermute | solution.py:363
  4.9 1.3 %copy-done.1 = bf16[128,4608]{1,0:T(8,128)(2,1)S(1)} copy-done((bf16[128,4608]{1,0:T(8,128)(2,1)S(1)}, bf16[128,4608]{1,0:T(8,128)(2,1)}, u32[]{:S(2)}) %copy-start.1) | copy-done | bytes 1179672
  6.2 1.2 %copy-done.2 = bf16[8,512,128]{2,1,0:T(8,128)(2,1)S(1)} copy-done((bf16[8,512,128]{2,1,0:T(8,128)(2,1)S(1)}, bf16[8,512,128]{2,1,0:T(8,128)(2,1)}, u32[]{:S(2)}) %copy-start.2) | copy-done | bytes 1048600
  9.9 1.8 %attention.1.after_ref = bf16[128,1024]{1,0:T(8,128)(2,1)S(1)} custom-call(s32[1,256]{1,0:T(1,128)S(1)} %get-tuple-element.32.doc_ref, bf16[1024,640]{1,0:T(8,128)(2,1)S(1)} %get-tuple-element.33.heads_ref, f32[1024,128]{1,0:T(8,128)S(1)} %get-tuple-element.34.scores_ref, bf16[8,512,128]{2,1,0:T(8,128)(2,1)S(1)} %get-tuple-element.35.up_ref, ...), custom_call_target="tpu_custom_call" | custom-call | flops 570425344 | bytes 2228224 | tf_op jit(solution)/shard_map/attention/pallas_call | solution.py:208
  12.5 3.1 %copy-done = bf16[1024,3584]{1,0:T(8,128)(2,1)S(1)} copy-done((bf16[1024,3584]{1,0:T(8,128)(2,1)S(1)}, bf16[1024,3584]{1,0:T(8,128)(2,1)}, u32[]{:S(2)}) %copy-start) | copy-done | bytes 7340056
  16.6 2.8 %collective-permute-done.1 = bf16[128,1024]{1,0:T(8,128)(2,1)S(1)} collective-permute-done((bf16[128,1024]{1,0:T(8,128)(2,1)S(1)}, bf16[128,1024]{1,0:T(8,128)(2,1)S(1)}, u32[]{:S(2)}, u32[]{:S(2)}) %collective-permute-start.1) | collective-permute-done | bytes 262176 | tf_op jit(solution)/shard_map/ppermute | solution.py:374
  22.9 1.2 %collective-permute-done.6 = bf16[8,16,1792]{2,1,0:T(8,128)(2,1)S(1)} collective-permute-done((bf16[8,16,1792]{2,1,0:T(8,128)(2,1)S(1)}, bf16[8,16,1792]{2,1,0:T(8,128)(2,1)S(1)}, u32[]{:S(2)}, u32[]{:S(2)}) %collective-permute-start.6) | collective-permute-done | bytes 458784 | tf_op jit(solution)/shard_map/ppermute | solution.py:59
  24.2 1.5 %collective-permute-start.7 = (bf16[4,16,1792]{2,1,0:T(8,128)(2,1)S(1)}, bf16[4,16,1792]{2,1,0:T(8,128)(2,1)S(1)}, u32[]{:S(2)}, u32[]{:S(2)}) collective-permute-start(bf16[4,16,1792]{2,1,0:T(8,128)(2,1)S(1)} %slice.277), channel_id=1, source_target_pairs={{0,2},{1,5},{2,0},{3,7},{4,6},{5,1},{6,4},{7,3},{8,10},{9,13},{10,... | collective-permute-start | bytes 688136 | tf_op jit(solution)/shard_map/ppermute | solution.py:59
  26.5 3.8 %collective-permute-done.7 = bf16[4,16,1792]{2,1,0:T(8,128)(2,1)S(1)} collective-permute-done((bf16[4,16,1792]{2,1,0:T(8,128)(2,1)S(1)}, bf16[4,16,1792]{2,1,0:T(8,128)(2,1)S(1)}, u32[]{:S(2)}, u32[]{:S(2)}) %collective-permute-start.7) | collective-permute-done | bytes 229408 | tf_op jit(solution)/shard_map/ppermute | solution.py:59
  30.4 1.6 %collective-permute-start.8 = (bf16[2,16,1792]{2,1,0:T(8,128)(2,1)S(1)}, bf16[2,16,1792]{2,1,0:T(8,128)(2,1)S(1)}, u32[]{:S(2)}, u32[]{:S(2)}) collective-permute-start(bf16[2,16,1792]{2,1,0:T(8,128)(2,1)S(1)} %slice.279), channel_id=1, source_target_pairs={{0,4},{1,3},{2,6},{3,1},{4,0},{5,7},{6,2},{7,5},{8,12},{9,11},{10,... | collective-permute-start | bytes 344072 | tf_op jit(solution)/shard_map/ppermute | solution.py:59
  33.2 1.6 %collective-permute-start.4 = (bf16[2,16,1792]{2,1,0:T(8,128)(2,1)S(1)}, bf16[2,16,1792]{2,1,0:T(8,128)(2,1)S(1)}, u32[]{:S(2)}, u32[]{:S(2)}) collective-permute-start(bf16[2,16,1792]{2,1,0:T(8,128)(2,1)S(1)} %slice.270), channel_id=1, source_target_pairs={{0,4},{1,3},{2,6},{3,1},{4,0},{5,7},{6,2},{7,5},{8,12},{9,11},{10,... | collective-permute-start | bytes 344072 | tf_op jit(solution)/shard_map/ppermute | solution.py:59
  35.3 2.8 %collective-permute-done.4 = bf16[2,16,1792]{2,1,0:T(8,128)(2,1)S(1)} collective-permute-done((bf16[2,16,1792]{2,1,0:T(8,128)(2,1)S(1)}, bf16[2,16,1792]{2,1,0:T(8,128)(2,1)S(1)}, u32[]{:S(2)}, u32[]{:S(2)}) %collective-permute-start.4) | collective-permute-done | bytes 114720 | tf_op jit(solution)/shard_map/ppermute | solution.py:59
  38.2 2.7 %collective-permute-start.5 = (bf16[2,16,1792]{2,1,0:T(8,128)(2,1)S(1)}, bf16[2,16,1792]{2,1,0:T(8,128)(2,1)S(1)}, u32[]{:S(2)}, u32[]{:S(2)}) collective-permute-start(bf16[2,16,1792]{2,1,0:T(8,128)(2,1)S(1)} %fusion.103.after_ref), channel_id=1, source_target_pairs={{0,8},{1,9},{2,10},{3,11},{4,12},{5,13},{6,14},{7,15},{8,0},{9,1},... | collective-permute-start | bytes 344072 | tf_op jit(solution)/shard_map/ppermute | solution.py:420
  41.9 1.3 %slice-done.5 = s8[3145728]{0:T(1024)(128)(4,1)S(1)} async-done(((s8[7340032]{0:T(1024)(128)(4,1)}), s8[3145728]{0:T(1024)(128)(4,1)S(1)}, s32[]{:S(2)}) %slice-start.5) | async-done | bytes 3145752
  43.8 4.7 %collective-permute-done.5.got_ref = bf16[2,16,1792]{2,1,0:T(8,128)(2,1)S(1)} collective-permute-done((bf16[2,16,1792]{2,1,0:T(8,128)(2,1)S(1)}, bf16[2,16,1792]{2,1,0:T(8,128)(2,1)S(1)}, u32[]{:S(2)}, u32[]{:S(2)}) %collective-permute-start.5) | collective-permute-done | bytes 114720 | tf_op jit(solution)/shard_map/ppermute | solution.py:420
  50.9 3.6 %collective-permute-done.13 = bf16[2,16,1792]{2,1,0:T(8,128)(2,1)S(1)} collective-permute-done((bf16[2,16,1792]{2,1,0:T(8,128)(2,1)S(1)}, bf16[2,16,1792]{2,1,0:T(8,128)(2,1)S(1)}, u32[]{:S(2)}, u32[]{:S(2)}) %collective-permute-start.13) | collective-permute-done | bytes 114720 | tf_op jit(solution)/shard_map/ppermute | solution.py:64
  54.6 1.6 %collective-permute-start.14 = (bf16[4,16,1792]{2,1,0:T(8,128)(2,1)S(1)}, bf16[4,16,1792]{2,1,0:T(8,128)(2,1)S(1)}, u32[]{:S(2)}, u32[]{:S(2)}) collective-permute-start(bf16[4,16,1792]{2,1,0:T(8,128)(2,1)S(1)} %pad_maximum_fusion.9), channel_id=1, source_target_pairs={{0,2},{1,5},{2,0},{3,7},{4,6},{5,1},{6,4},{7,3},{8,10},{9,13},{10,... | collective-permute-start | bytes 688136 | tf_op jit(solution)/shard_map/ppermute | solution.py:64
  57.2 1.6 %collective-permute-start.11 = (bf16[4,16,1920]{2,1,0:T(8,128)(2,1)S(1)}, bf16[4,16,1920]{2,1,0:T(8,128)(2,1)S(1)}, u32[]{:S(2)}, u32[]{:S(2)}) collective-permute-start(bf16[4,16,1920]{2,1,0:T(8,128)(2,1)S(1)} %pad_maximum_fusion.6), channel_id=1, source_target_pairs={{0,2},{1,5},{2,0},{3,7},{4,6},{5,1},{6,4},{7,3},{8,10},{9,13},{10,... | collective-permute-start | bytes 737288 | tf_op jit(solution)/shard_map/ppermute | solution.py:64
  58.8 1.9 %collective-permute-done.14 = bf16[4,16,1792]{2,1,0:T(8,128)(2,1)S(1)} collective-permute-done((bf16[4,16,1792]{2,1,0:T(8,128)(2,1)S(1)}, bf16[4,16,1792]{2,1,0:T(8,128)(2,1)S(1)}, u32[]{:S(2)}, u32[]{:S(2)}) %collective-permute-start.14) | collective-permute-done | bytes 229408 | tf_op jit(solution)/shard_map/ppermute | solution.py:64
  60.8 2.7 %collective-permute-done.11 = bf16[4,16,1920]{2,1,0:T(8,128)(2,1)S(1)} collective-permute-done((bf16[4,16,1920]{2,1,0:T(8,128)(2,1)S(1)}, bf16[4,16,1920]{2,1,0:T(8,128)(2,1)S(1)}, u32[]{:S(2)}, u32[]{:S(2)}) %collective-permute-start.11) | collective-permute-done | bytes 245792 | tf_op jit(solution)/shard_map/ppermute | solution.py:64
  63.7 1.7 %collective-permute-done.12 = bf16[8,16,1920]{2,1,0:T(8,128)(2,1)S(1)} collective-permute-done((bf16[8,16,1920]{2,1,0:T(8,128)(2,1)S(1)}, bf16[8,16,1920]{2,1,0:T(8,128)(2,1)S(1)}, u32[]{:S(2)}, u32[]{:S(2)}) %collective-permute-start.12) | collective-permute-done | bytes 491552 | tf_op jit(solution)/shard_map/ppermute | solution.py:64
  70.8 1.8 %collective-permute-start.17 = (f32[256]{0:T(256)S(1)}, f32[256]{0:T(256)S(1)}, u32[]{:S(2)}, u32[]{:S(2)}) collective-permute-start(f32[256]{0:T(256)S(1)} %slice_reduce_fusion), channel_id=1, source_target_pairs={{0,16},{16,0},{1,17},{17,1},{2,18},{18,2},{3,19},{19,3},{4,20},{20... | collective-permute-start | bytes 3080 | tf_op jit(solution)/shard_map/ppermute | solution.py:451
  73.8 5.7 %collective-permute-done.17 = f32[256]{0:T(256)S(1)} collective-permute-done((f32[256]{0:T(256)S(1)}, f32[256]{0:T(256)S(1)}, u32[]{:S(2)}, u32[]{:S(2)}) %collective-permute-start.17) | collective-permute-done | bytes 1056 | tf_op jit(solution)/shard_map/ppermute | solution.py:451
  79.7 5.3 %collective-permute-done.18 = bf16[144,1024]{1,0:T(8,128)(2,1)S(1)} collective-permute-done((bf16[144,1024]{1,0:T(8,128)(2,1)S(1)}, bf16[144,1024]{1,0:T(8,128)(2,1)S(1)}, u32[]{:S(2)}, u32[]{:S(2)}) %collective-permute-start.18) | collective-permute-done | bytes 294944 | tf_op jit(solution)/shard_map/ppermute | solution.py:478
  89.3 1.6 %collective-permute-start.24 = (bf16[4,16,1792]{2,1,0:T(8,128)(2,1)S(1)}, bf16[4,16,1792]{2,1,0:T(8,128)(2,1)S(1)}, u32[]{:S(2)}, u32[]{:S(2)}) collective-permute-start(bf16[4,16,1792]{2,1,0:T(8,128)(2,1)S(1)} %slice.304), channel_id=1, source_target_pairs={{0,2},{1,5},{2,0},{3,7},{4,6},{5,1},{6,4},{7,3},{8,10},{9,13},{10,... | collective-permute-start | bytes 688136 | tf_op jit(solution)/shard_map/ppermute | solution.py:59
  92.1 3.3 %collective-permute-done.24 = bf16[4,16,1792]{2,1,0:T(8,128)(2,1)S(1)} collective-permute-done((bf16[4,16,1792]{2,1,0:T(8,128)(2,1)S(1)}, bf16[4,16,1792]{2,1,0:T(8,128)(2,1)S(1)}, u32[]{:S(2)}, u32[]{:S(2)}) %collective-permute-start.24) | collective-permute-done | bytes 229408 | tf_op jit(solution)/shard_map/ppermute | solution.py:59
  95.6 2.7 %collective-permute-done.20 = bf16[4,16,1792]{2,1,0:T(8,128)(2,1)S(1)} collective-permute-done((bf16[4,16,1792]{2,1,0:T(8,128)(2,1)S(1)}, bf16[4,16,1792]{2,1,0:T(8,128)(2,1)S(1)}, u32[]{:S(2)}, u32[]{:S(2)}) %collective-permute-start.20) | collective-permute-done | bytes 229408 | tf_op jit(solution)/shard_map/ppermute | solution.py:59
  98.4 1.9 %collective-permute-done.25 = bf16[2,16,1792]{2,1,0:T(8,128)(2,1)S(1)} collective-permute-done((bf16[2,16,1792]{2,1,0:T(8,128)(2,1)S(1)}, bf16[2,16,1792]{2,1,0:T(8,128)(2,1)S(1)}, u32[]{:S(2)}, u32[]{:S(2)}) %collective-permute-start.25) | collective-permute-done | bytes 114720 | tf_op jit(solution)/shard_map/ppermute | solution.py:59
  100.4 1.5 %collective-permute-start.26 = (bf16[1,16,1792]{2,1,0:T(8,128)(2,1)S(1)}, bf16[1,16,1792]{2,1,0:T(8,128)(2,1)S(1)}, u32[]{:S(2)}, u32[]{:S(2)}) collective-permute-start(bf16[1,16,1792]{2,1,0:T(8,128)(2,1)S(1)} %slice.308), channel_id=1, source_target_pairs={{0,8},{1,9},{2,10},{3,11},{4,12},{5,13},{6,14},{7,15},{8,0},{9,1},... | collective-permute-start | bytes 172040 | tf_op jit(solution)/shard_map/ppermute | solution.py:59
  101.8 1.9 %collective-permute-done.21 = bf16[2,16,1792]{2,1,0:T(8,128)(2,1)S(1)} collective-permute-done((bf16[2,16,1792]{2,1,0:T(8,128)(2,1)S(1)}, bf16[2,16,1792]{2,1,0:T(8,128)(2,1)S(1)}, u32[]{:S(2)}, u32[]{:S(2)}) %collective-permute-start.21) | collective-permute-done | bytes 114720 | tf_op jit(solution)/shard_map/ppermute | solution.py:59
  104.8 2.1 %collective-permute-done.26 = bf16[1,16,1792]{2,1,0:T(8,128)(2,1)S(1)} collective-permute-done((bf16[1,16,1792]{2,1,0:T(8,128)(2,1)S(1)}, bf16[1,16,1792]{2,1,0:T(8,128)(2,1)S(1)}, u32[]{:S(2)}, u32[]{:S(2)}) %collective-permute-start.26) | collective-permute-done | bytes 57376 | tf_op jit(solution)/shard_map/ppermute | solution.py:59
  106.9 2.2 %collective-permute-done.22 = bf16[1,16,1792]{2,1,0:T(8,128)(2,1)S(1)} collective-permute-done((bf16[1,16,1792]{2,1,0:T(8,128)(2,1)S(1)}, bf16[1,16,1792]{2,1,0:T(8,128)(2,1)S(1)}, u32[]{:S(2)}, u32[]{:S(2)}) %collective-permute-start.22) | collective-permute-done | bytes 57376 | tf_op jit(solution)/shard_map/ppermute | solution.py:59
  (147 shorter events, 29.8 us)
Async XLA Ops:
  0.0 9.9 %collective-permute-start = (bf16[576,128]{1,0:T(8,128)(2,1)}, bf16[576,128]{1,0:T(8,128)(2,1)S(1)}, u32[]{:S(2)}, u32[]{:S(2)}) collective-permute-start(bf16[576,128]{1,0:T(8,128)(2,1)} %bitcast.72), channel_id=1, source_target_pairs={{0,16},{1,17},{2,18},{3,19},{4,20},{5,21},{6,22},{7,23},{8,24},{9,... | collective-permute-start | bytes 442376 | tf_op jit(solution)/shard_map/ppermute | solution.py:363
  11.6 7.8 %collective-permute-start.1 = (bf16[128,1024]{1,0:T(8,128)(2,1)S(1)}, bf16[128,1024]{1,0:T(8,128)(2,1)S(1)}, u32[]{:S(2)}, u32[]{:S(2)}) collective-permute-start(bf16[128,1024]{1,0:T(8,128)(2,1)S(1)} %attention.1.after_ref), channel_id=1, source_target_pairs={{0,16},{16,0},{1,17},{17,1},{2,18},{18,2},{3,19},{19,3},{4,20},{20... | collective-permute-start | bytes 786440 | tf_op jit(solution)/shard_map/ppermute | solution.py:374
  21.0 17.2 %copy-start.5 = (bf16[16,3584]{1,0:T(8,128)(2,1)S(1)}, bf16[16,3584]{1,0:T(8,128)(2,1)}, u32[]{:S(2)}) copy-start(bf16[16,3584]{1,0:T(8,128)(2,1)} %param.17) | copy-start | bytes 344068
  21.0 20.3 %slice-start.2 = ((s8[7340032]{0:T(1024)(128)(4,1)}), s8[3145728]{0:T(1024)(128)(4,1)S(1)}, s32[]{:S(2)}) async-start(s8[7340032]{0:T(1024)(128)(4,1)} %bitcast.66), calls=%async_computation.2 | async-start | bytes 6291456
  22.2 19.1 %slice-start.3 = ((s8[7340032]{0:T(1024)(128)(4,1)}), s8[4194304]{0:T(1024)(128)(4,1)S(1)}, s32[]{:S(2)}) async-start(s8[7340032]{0:T(1024)(128)(4,1)} %bitcast.66), calls=%async_computation.3 | async-start | bytes 8388608
  22.2 1.9 %collective-permute-start.6 = (bf16[8,16,1792]{2,1,0:T(8,128)(2,1)S(1)}, bf16[8,16,1792]{2,1,0:T(8,128)(2,1)S(1)}, u32[]{:S(2)}, u32[]{:S(2)}) collective-permute-start(bf16[8,16,1792]{2,1,0:T(8,128)(2,1)S(1)} %bitcast.86), channel_id=1, source_target_pairs={{0,1},{1,0},{2,3},{3,2},{4,5},{5,4},{6,7},{7,6},{8,9},{9,8},{10,11... | collective-permute-start | bytes 1376264 | tf_op jit(solution)/shard_map/ppermute | solution.py:59
  22.4 3.4 %collective-permute-start.2 = (bf16[8,16,1792]{2,1,0:T(8,128)(2,1)S(1)}, bf16[8,16,1792]{2,1,0:T(8,128)(2,1)S(1)}, u32[]{:S(2)}, u32[]{:S(2)}) collective-permute-start(bf16[8,16,1792]{2,1,0:T(8,128)(2,1)S(1)} %bitcast.84), channel_id=1, source_target_pairs={{0,1},{1,0},{2,3},{3,2},{4,5},{5,4},{6,7},{7,6},{8,9},{9,8},{10,11... | collective-permute-start | bytes 1376264 | tf_op jit(solution)/shard_map/ppermute | solution.py:59
  24.2 6.1 %collective-permute-start.7 = (bf16[4,16,1792]{2,1,0:T(8,128)(2,1)S(1)}, bf16[4,16,1792]{2,1,0:T(8,128)(2,1)S(1)}, u32[]{:S(2)}, u32[]{:S(2)}) collective-permute-start(bf16[4,16,1792]{2,1,0:T(8,128)(2,1)S(1)} %slice.277), channel_id=1, source_target_pairs={{0,2},{1,5},{2,0},{3,7},{4,6},{5,1},{6,4},{7,3},{8,10},{9,13},{10,... | collective-permute-start | bytes 688136 | tf_op jit(solution)/shard_map/ppermute | solution.py:59
  25.9 7.2 %collective-permute-start.3 = (bf16[4,16,1792]{2,1,0:T(8,128)(2,1)S(1)}, bf16[4,16,1792]{2,1,0:T(8,128)(2,1)S(1)}, u32[]{:S(2)}, u32[]{:S(2)}) collective-permute-start(bf16[4,16,1792]{2,1,0:T(8,128)(2,1)S(1)} %slice.268), channel_id=1, source_target_pairs={{0,2},{1,5},{2,0},{3,7},{4,6},{5,1},{6,4},{7,3},{8,10},{9,13},{10,... | collective-permute-start | bytes 688136 | tf_op jit(solution)/shard_map/ppermute | solution.py:59
  30.4 4.9 %collective-permute-start.8 = (bf16[2,16,1792]{2,1,0:T(8,128)(2,1)S(1)}, bf16[2,16,1792]{2,1,0:T(8,128)(2,1)S(1)}, u32[]{:S(2)}, u32[]{:S(2)}) collective-permute-start(bf16[2,16,1792]{2,1,0:T(8,128)(2,1)S(1)} %slice.279), channel_id=1, source_target_pairs={{0,4},{1,3},{2,6},{3,1},{4,0},{5,7},{6,2},{7,5},{8,12},{9,11},{10,... | collective-permute-start | bytes 344072 | tf_op jit(solution)/shard_map/ppermute | solution.py:59
  33.2 4.9 %collective-permute-start.4 = (bf16[2,16,1792]{2,1,0:T(8,128)(2,1)S(1)}, bf16[2,16,1792]{2,1,0:T(8,128)(2,1)S(1)}, u32[]{:S(2)}, u32[]{:S(2)}) collective-permute-start(bf16[2,16,1792]{2,1,0:T(8,128)(2,1)S(1)} %slice.270), channel_id=1, source_target_pairs={{0,4},{1,3},{2,6},{3,1},{4,0},{5,7},{6,2},{7,5},{8,12},{9,11},{10,... | collective-permute-start | bytes 344072 | tf_op jit(solution)/shard_map/ppermute | solution.py:59
  38.2 10.2 %collective-permute-start.5 = (bf16[2,16,1792]{2,1,0:T(8,128)(2,1)S(1)}, bf16[2,16,1792]{2,1,0:T(8,128)(2,1)S(1)}, u32[]{:S(2)}, u32[]{:S(2)}) collective-permute-start(bf16[2,16,1792]{2,1,0:T(8,128)(2,1)S(1)} %fusion.103.after_ref), channel_id=1, source_target_pairs={{0,8},{1,9},{2,10},{3,11},{4,12},{5,13},{6,14},{7,15},{8,0},{9,1},... | collective-permute-start | bytes 344072 | tf_op jit(solution)/shard_map/ppermute | solution.py:420
  40.9 8.8 %collective-permute-start.9 = (bf16[2,16,1920]{2,1,0:T(8,128)(2,1)S(1)}, bf16[2,16,1920]{2,1,0:T(8,128)(2,1)S(1)}, u32[]{:S(2)}, u32[]{:S(2)}) collective-permute-start(bf16[2,16,1920]{2,1,0:T(8,128)(2,1)S(1)} %fusion.76), channel_id=1, source_target_pairs={{0,8},{1,9},{2,10},{3,11},{4,12},{5,13},{6,14},{7,15},{8,0},{9,1},... | collective-permute-start | bytes 368648 | tf_op jit(solution)/shard_map/ppermute | solution.py:420
  48.5 6.0 %collective-permute-start.13 = (bf16[2,16,1792]{2,1,0:T(8,128)(2,1)S(1)}, bf16[2,16,1792]{2,1,0:T(8,128)(2,1)S(1)}, u32[]{:S(2)}, u32[]{:S(2)}) collective-permute-start(bf16[2,16,1792]{2,1,0:T(8,128)(2,1)S(1)} %get-tuple-element.45), channel_id=1, source_target_pairs={{0,4},{1,3},{2,6},{3,1},{4,0},{5,7},{6,2},{7,5},{8,12},{9,11},{10,... | collective-permute-start | bytes 344072 | tf_op jit(solution)/shard_map/ppermute | solution.py:64
  50.0 7.2 %collective-permute-start.10 = (bf16[2,16,1920]{2,1,0:T(8,128)(2,1)S(1)}, bf16[2,16,1920]{2,1,0:T(8,128)(2,1)S(1)}, u32[]{:S(2)}, u32[]{:S(2)}) collective-permute-start(bf16[2,16,1920]{2,1,0:T(8,128)(2,1)S(1)} %get-tuple-element.44), channel_id=1, source_target_pairs={{0,4},{1,3},{2,6},{3,1},{4,0},{5,7},{6,2},{7,5},{8,12},{9,11},{10,... | collective-permute-start | bytes 368648 | tf_op jit(solution)/shard_map/ppermute | solution.py:64
  54.6 6.1 %collective-permute-start.14 = (bf16[4,16,1792]{2,1,0:T(8,128)(2,1)S(1)}, bf16[4,16,1792]{2,1,0:T(8,128)(2,1)S(1)}, u32[]{:S(2)}, u32[]{:S(2)}) collective-permute-start(bf16[4,16,1792]{2,1,0:T(8,128)(2,1)S(1)} %pad_maximum_fusion.9), channel_id=1, source_target_pairs={{0,2},{1,5},{2,0},{3,7},{4,6},{5,1},{6,4},{7,3},{8,10},{9,13},{10,... | collective-permute-start | bytes 688136 | tf_op jit(solution)/shard_map/ppermute | solution.py:64
  57.2 6.3 %collective-permute-start.11 = (bf16[4,16,1920]{2,1,0:T(8,128)(2,1)S(1)}, bf16[4,16,1920]{2,1,0:T(8,128)(2,1)S(1)}, u32[]{:S(2)}, u32[]{:S(2)}) collective-permute-start(bf16[4,16,1920]{2,1,0:T(8,128)(2,1)S(1)} %pad_maximum_fusion.6), channel_id=1, source_target_pairs={{0,2},{1,5},{2,0},{3,7},{4,6},{5,1},{6,4},{7,3},{8,10},{9,13},{10,... | collective-permute-start | bytes 737288 | tf_op jit(solution)/shard_map/ppermute | solution.py:64
  60.7 2.9 %collective-permute-start.15 = (bf16[8,16,1792]{2,1,0:T(8,128)(2,1)S(1)}, bf16[8,16,1792]{2,1,0:T(8,128)(2,1)S(1)}, u32[]{:S(2)}, u32[]{:S(2)}) collective-permute-start(bf16[8,16,1792]{2,1,0:T(8,128)(2,1)S(1)} %pad_maximum_fusion.3), channel_id=1, source_target_pairs={{0,1},{1,0},{2,3},{3,2},{4,5},{5,4},{6,7},{7,6},{8,9},{9,8},{10,11... | collective-permute-start | bytes 1376264 | tf_op jit(solution)/shard_map/ppermute | solution.py:64
  63.5 1.9 %collective-permute-start.12 = (bf16[8,16,1920]{2,1,0:T(8,128)(2,1)S(1)}, bf16[8,16,1920]{2,1,0:T(8,128)(2,1)S(1)}, u32[]{:S(2)}, u32[]{:S(2)}) collective-permute-start(bf16[8,16,1920]{2,1,0:T(8,128)(2,1)S(1)} %pad_maximum_fusion.2), channel_id=1, source_target_pairs={{0,1},{1,0},{2,3},{3,2},{4,5},{5,4},{6,7},{7,6},{8,9},{9,8},{10,11... | collective-permute-start | bytes 1474568 | tf_op jit(solution)/shard_map/ppermute | solution.py:64
  68.2 4.8 %slice-start = ((s8[7340032]{0:T(1024)(128)(4,1)}), s8[4194304]{0:T(1024)(128)(4,1)S(1)}, s32[]{:S(2)}) async-start(s8[7340032]{0:T(1024)(128)(4,1)} %bitcast.63), calls=%async_computation | async-start | bytes 8388608
  69.0 4.0 %slice-start.1 = ((s8[7340032]{0:T(1024)(128)(4,1)}), s8[3145728]{0:T(1024)(128)(4,1)S(1)}, s32[]{:S(2)}) async-start(s8[7340032]{0:T(1024)(128)(4,1)} %bitcast.63), calls=%async_computation.1 | async-start | bytes 6291456
  69.5 10.1 %collective-permute-start.16 = (bf16[144,1024]{1,0:T(8,128)(2,1)S(1)}, bf16[144,1024]{1,0:T(8,128)(2,1)S(1)}, u32[]{:S(2)}, u32[]{:S(2)}) collective-permute-start(bf16[144,1024]{1,0:T(8,128)(2,1)S(1)} %pad_maximum_fusion.4), channel_id=1, source_target_pairs={{0,16},{16,0},{1,17},{17,1},{2,18},{18,2},{3,19},{19,3},{4,20},{20... | collective-permute-start | bytes 884744 | tf_op jit(solution)/shard_map/ppermute | solution.py:478
  70.8 8.7 %collective-permute-start.17 = (f32[256]{0:T(256)S(1)}, f32[256]{0:T(256)S(1)}, u32[]{:S(2)}, u32[]{:S(2)}) collective-permute-start(f32[256]{0:T(256)S(1)} %slice_reduce_fusion), channel_id=1, source_target_pairs={{0,16},{16,0},{1,17},{17,1},{2,18},{18,2},{3,19},{19,3},{4,20},{20... | collective-permute-start | bytes 3080 | tf_op jit(solution)/shard_map/ppermute | solution.py:451
  72.7 12.3 %collective-permute-start.18 = (bf16[144,1024]{1,0:T(8,128)(2,1)S(1)}, bf16[144,1024]{1,0:T(8,128)(2,1)S(1)}, u32[]{:S(2)}, u32[]{:S(2)}) collective-permute-start(bf16[144,1024]{1,0:T(8,128)(2,1)S(1)} %pad_maximum_fusion.5.after_ref), channel_id=1, source_target_pairs={{0,16},{16,0},{1,17},{17,1},{2,18},{18,2},{3,19},{19,3},{4,20},{20... | collective-permute-start | bytes 884744 | tf_op jit(solution)/shard_map/ppermute | solution.py:478
  87.3 1.9 %collective-permute-start.23 = (bf16[8,16,1792]{2,1,0:T(8,128)(2,1)S(1)}, bf16[8,16,1792]{2,1,0:T(8,128)(2,1)S(1)}, u32[]{:S(2)}, u32[]{:S(2)}) collective-permute-start(bf16[8,16,1792]{2,1,0:T(8,128)(2,1)S(1)} %bitcast.83), channel_id=1, source_target_pairs={{0,1},{1,0},{2,3},{3,2},{4,5},{5,4},{6,7},{7,6},{8,9},{9,8},{10,11... | collective-permute-start | bytes 1376264 | tf_op jit(solution)/shard_map/ppermute | solution.py:59
  88.4 2.5 %collective-permute-start.19 = (bf16[8,16,1792]{2,1,0:T(8,128)(2,1)S(1)}, bf16[8,16,1792]{2,1,0:T(8,128)(2,1)S(1)}, u32[]{:S(2)}, u32[]{:S(2)}) collective-permute-start(bf16[8,16,1792]{2,1,0:T(8,128)(2,1)S(1)} %bitcast.85), channel_id=1, source_target_pairs={{0,1},{1,0},{2,3},{3,2},{4,5},{5,4},{6,7},{7,6},{8,9},{9,8},{10,11... | collective-permute-start | bytes 1376264 | tf_op jit(solution)/shard_map/ppermute | solution.py:59
  89.3 6.1 %collective-permute-start.24 = (bf16[4,16,1792]{2,1,0:T(8,128)(2,1)S(1)}, bf16[4,16,1792]{2,1,0:T(8,128)(2,1)S(1)}, u32[]{:S(2)}, u32[]{:S(2)}) collective-permute-start(bf16[4,16,1792]{2,1,0:T(8,128)(2,1)S(1)} %slice.304), channel_id=1, source_target_pairs={{0,2},{1,5},{2,0},{3,7},{4,6},{5,1},{6,4},{7,3},{8,10},{9,13},{10,... | collective-permute-start | bytes 688136 | tf_op jit(solution)/shard_map/ppermute | solution.py:59
  91.0 7.2 %collective-permute-start.20 = (bf16[4,16,1792]{2,1,0:T(8,128)(2,1)S(1)}, bf16[4,16,1792]{2,1,0:T(8,128)(2,1)S(1)}, u32[]{:S(2)}, u32[]{:S(2)}) collective-permute-start(bf16[4,16,1792]{2,1,0:T(8,128)(2,1)S(1)} %slice.296), channel_id=1, source_target_pairs={{0,2},{1,5},{2,0},{3,7},{4,6},{5,1},{6,4},{7,3},{8,10},{9,13},{10,... | collective-permute-start | bytes 688136 | tf_op jit(solution)/shard_map/ppermute | solution.py:59
  95.5 4.9 %collective-permute-start.25 = (bf16[2,16,1792]{2,1,0:T(8,128)(2,1)S(1)}, bf16[2,16,1792]{2,1,0:T(8,128)(2,1)S(1)}, u32[]{:S(2)}, u32[]{:S(2)}) collective-permute-start(bf16[2,16,1792]{2,1,0:T(8,128)(2,1)S(1)} %slice.306), channel_id=1, source_target_pairs={{0,4},{1,3},{2,6},{3,1},{4,0},{5,7},{6,2},{7,5},{8,12},{9,11},{10,... | collective-permute-start | bytes 344072 | tf_op jit(solution)/shard_map/ppermute | solution.py:59
  98.3 5.5 %collective-permute-start.21 = (bf16[2,16,1792]{2,1,0:T(8,128)(2,1)S(1)}, bf16[2,16,1792]{2,1,0:T(8,128)(2,1)S(1)}, u32[]{:S(2)}, u32[]{:S(2)}) collective-permute-start(bf16[2,16,1792]{2,1,0:T(8,128)(2,1)S(1)} %slice.298), channel_id=1, source_target_pairs={{0,4},{1,3},{2,6},{3,1},{4,0},{5,7},{6,2},{7,5},{8,12},{9,11},{10,... | collective-permute-start | bytes 344072 | tf_op jit(solution)/shard_map/ppermute | solution.py:59
  100.4 6.5 %collective-permute-start.26 = (bf16[1,16,1792]{2,1,0:T(8,128)(2,1)S(1)}, bf16[1,16,1792]{2,1,0:T(8,128)(2,1)S(1)}, u32[]{:S(2)}, u32[]{:S(2)}) collective-permute-start(bf16[1,16,1792]{2,1,0:T(8,128)(2,1)S(1)} %slice.308), channel_id=1, source_target_pairs={{0,8},{1,9},{2,10},{3,11},{4,12},{5,13},{6,14},{7,15},{8,0},{9,1},... | collective-permute-start | bytes 172040 | tf_op jit(solution)/shard_map/ppermute | solution.py:59
  103.8 5.3 %collective-permute-start.22 = (bf16[1,16,1792]{2,1,0:T(8,128)(2,1)S(1)}, bf16[1,16,1792]{2,1,0:T(8,128)(2,1)S(1)}, u32[]{:S(2)}, u32[]{:S(2)}) collective-permute-start(bf16[1,16,1792]{2,1,0:T(8,128)(2,1)S(1)} %slice.300), channel_id=1, source_target_pairs={{0,8},{1,9},{2,10},{3,11},{4,12},{5,13},{6,14},{7,15},{8,0},{9,1},... | collective-permute-start | bytes 172040 | tf_op jit(solution)/shard_map/ppermute | solution.py:59
  (10 other events, 15.0 us)

commit v4 on v3

--- a/solution.py
+++ b/solution.py
@@ -30,7 +30,7 @@
 
 def step_bits(bits, lane):
     middle = list(range(1, bits - 1))
-    if lane:
+    if not lane:
         middle = middle[1:] + middle[:1]
     return [0] + middle + [bits - 1]
 
@@ -399,7 +399,8 @@
     padded = -(-(facts_width + 3) // 128) * 128
     facts = jnp.pad(facts, ((0, 0), (0, padded - facts_width)))
 
-    edges = split_edges(w_out.shape[1], PARTS)
+    first_width = w_out.shape[1] // 128 * 15 // 28 * 128
+    edges = [(0, first_width), (first_width, w_out.shape[1])]
     residuals, arrived = [], []
     squares = jnp.zeros((2, token_count, 1), jnp.float32)
     for part, (low, high) in enumerate(edges):
@@ -492,7 +493,9 @@
         activated.append((jax.nn.silu(both[:, :half]) * both[:, half:]).astype(jnp.bfloat16))
     spread = placing.T
     outputs = []
-    for (low, high), residual in zip(edges, residuals):
+    residuals = jnp.concatenate(residuals, axis=1)
+    for low, high in split_edges(w_out.shape[1], PARTS):
+        residual = residuals[:, low:high]
         produced = 0.0
         for (start, stop), part_rows in zip(ranges, activated):
             produced = produced + jnp.dot(

time: 110 us -> 107 us (0.973)
  waiting for transfers between devices: 54.1 us -> 46.2 us
  starting transfers between devices: 27.6 us -> 31.3 us
    ppermute x2, waiting for transfers between devices: 5.31 us -> 11.4 us  [shards(): others = [lax.ppermute(both, 'ctx', swap) for both in sums]]
    ppermute x14, waiting for transfers between devices: 23.6 us -> 17.8 us  [halved(): got = lax.ppermute(array[half:], 'ep', crossing(count, step))]
    ppermute x1, waiting for transfers between devices: 5.75 us -> 0.01 us  [shards(): token_squares = token_squares + lax.ppermute(token_squares, 'ctx', swap)]
    ppermute x14, starting transfers between devices: 11.9 us -> 14.4 us  [halved(): got = lax.ppermute(array[half:], 'ep', crossing(count, step))]
    ppermute x2, starting transfers between devices: 3.06 us -> 5.31 us  [shards(): got = lax.ppermute(sent, 'ep', crossing(ep_count, bits - 1))]
    ppermute x2, starting transfers between devices: 0.71 us -> 2.15 us  [shards(): others = [lax.ppermute(both, 'ctx', swap) for both in sums]]
    ppermute x1, starting transfers between devices: 1.8 us -> 0.36 us  [shards(): token_squares = token_squares + lax.ppermute(token_squares, 'ctx', swap)]
    ppermute x2, waiting for transfers between devices: 5.63 us -> 4.29 us  [shards(): got = lax.ppermute(sent, 'ep', crossing(ep_count, bits - 1))]
  transfers between devices with their start and end apart: 27 -> 27, of which waited for: 22 -> 20; matrix products, arithmetic and copies ran while one was open for 3% -> 8% of each run, Pallas kernels for 3% -> 3%
where the time goes in v4:
time: 107 us
  waiting for transfers between devices  46.2 us (43%)
  starting transfers between devices  31.3 us (29%)
  matrix products  9.9 us (9%)
  local copies, waits for them, and re-layouts  8.96 us (8%)
  Pallas kernels  5.26 us (5%)
  other arithmetic  4.21 us (4%)
    ppermute x14, waiting for transfers between devices, halved(): got = lax.ppermute(array[half:], 'ep', crossing(count, step))  17.8 us
    ppermute x14, starting transfers between devices, halved(): got = lax.ppermute(array[half:], 'ep', crossing(count, step))  14.4 us
    ppermute x2, waiting for transfers between devices, shards(): others = [lax.ppermute(both, 'ctx', swap) for both in sums]  11.4 us
    ppermute x6, waiting for transfers between devices, doubled(): lax.ppermute(array, 'ep', crossing(count, step))  10.3 us
    unnamed x26, local copies, waits for them, and re-layouts  8.54 us
    ppermute x2, starting transfers between devices, shards(): got = lax.ppermute(sent, 'ep', crossing(ep_count, bits - 1))  5.31 us
    ppermute x1, starting transfers between devices, shards(): blocks = [key_columns, lax.ppermute(key_columns, 'ctx', [(0, 1)])]  4.87 us
    ppermute x2, waiting for transfers between devices, shards(): got = lax.ppermute(sent, 'ep', crossing(ep_count, bits - 1))  4.29 us
  transfers between devices with their start and end apart: 27, of which 20 were waited for; matrix products, arithmetic and copies ran while one was open for 8% of the time, Pallas kernels for 3%

profile of v4, /device:TPU:0, one launch (start us, length us, event | category | flops | bytes accessed | tf_op | source)
XLA Modules:
  0.0 106.6 jit_solution(13091148403940095955)
XLA Ops:
  0.0 4.9 %collective-permute-start = (bf16[576,128]{1,0:T(8,128)(2,1)}, bf16[576,128]{1,0:T(8,128)(2,1)S(1)}, u32[]{:S(2)}, u32[]{:S(2)}) collective-permute-start(bf16[576,128]{1,0:T(8,128)(2,1)} %bitcast.70), channel_id=1, source_target_pairs={{0,16},{1,17},{2,18},{3,19},{4,20},{5,21},{6,22},{7,23},{8,24},{9,... | collective-permute-start | bytes 442376 | tf_op jit(solution)/shard_map/ppermute | solution.py:363
  4.9 1.3 %copy-done.1 = bf16[128,4608]{1,0:T(8,128)(2,1)S(1)} copy-done((bf16[128,4608]{1,0:T(8,128)(2,1)S(1)}, bf16[128,4608]{1,0:T(8,128)(2,1)}, u32[]{:S(2)}) %copy-start.1) | copy-done | bytes 1179672
  6.2 1.2 %copy-done.2 = bf16[8,512,128]{2,1,0:T(8,128)(2,1)S(1)} copy-done((bf16[8,512,128]{2,1,0:T(8,128)(2,1)S(1)}, bf16[8,512,128]{2,1,0:T(8,128)(2,1)}, u32[]{:S(2)}) %copy-start.2) | copy-done | bytes 1048600
  9.9 1.8 %attention.1.after_ref = bf16[128,1024]{1,0:T(8,128)(2,1)S(1)} custom-call(s32[1,256]{1,0:T(1,128)S(1)} %get-tuple-element.32.doc_ref, bf16[1024,640]{1,0:T(8,128)(2,1)S(1)} %get-tuple-element.33.heads_ref, f32[1024,128]{1,0:T(8,128)S(1)} %get-tuple-element.34.scores_ref, bf16[8,512,128]{2,1,0:T(8,128)(2,1)S(1)} %get-tuple-element.35.up_ref, ...), custom_call_target="tpu_custom_call" | custom-call | flops 570425344 | bytes 2228224 | tf_op jit(solution)/shard_map/attention/pallas_call | solution.py:208
  13.4 3.1 %copy-done = bf16[1024,3584]{1,0:T(8,128)(2,1)S(1)} copy-done((bf16[1024,3584]{1,0:T(8,128)(2,1)S(1)}, bf16[1024,3584]{1,0:T(8,128)(2,1)}, u32[]{:S(2)}) %copy-start) | copy-done | bytes 7340056
  17.0 2.4 %collective-permute-done.1 = bf16[128,1024]{1,0:T(8,128)(2,1)S(1)} collective-permute-done((bf16[128,1024]{1,0:T(8,128)(2,1)S(1)}, bf16[128,1024]{1,0:T(8,128)(2,1)S(1)}, u32[]{:S(2)}, u32[]{:S(2)}) %collective-permute-start.1) | collective-permute-done | bytes 262176 | tf_op jit(solution)/shard_map/ppermute | solution.py:374
  21.0 1.3 %fusion.4 = bf16[256,1920]{1,0:T(8,128)(2,1)S(1)} fusion(bf16[256,1024]{1,0:T(8,128)(2,1)S(1)} %convolution_convert_fusion.4, bf16[1024,3584]{1,0:T(8,128)(2,1)S(1)} %fetch_weights.4), kind=kOutput, calls=%fused_computation.4 | convolution fusion | flops 1007124480 | bytes 5439488 | tf_op jit(solution)/shard_map/dot_general | solution.py:408
  24.3 1.6 %collective-permute-start.7 = (bf16[4,16,1664]{2,1,0:T(8,128)(2,1)S(1)}, bf16[4,16,1664]{2,1,0:T(8,128)(2,1)S(1)}, u32[]{:S(2)}, u32[]{:S(2)}) collective-permute-start(bf16[4,16,1664]{2,1,0:T(8,128)(2,1)S(1)} %slice.285), channel_id=1, source_target_pairs={{0,4},{1,3},{2,6},{3,1},{4,0},{5,7},{6,2},{7,5},{8,12},{9,11},{10,... | collective-permute-start | bytes 638984 | tf_op jit(solution)/shard_map/ppermute | solution.py:59
  26.7 3.6 %collective-permute-done.7 = bf16[4,16,1664]{2,1,0:T(8,128)(2,1)S(1)} collective-permute-done((bf16[4,16,1664]{2,1,0:T(8,128)(2,1)S(1)}, bf16[4,16,1664]{2,1,0:T(8,128)(2,1)S(1)}, u32[]{:S(2)}, u32[]{:S(2)}) %collective-permute-start.7) | collective-permute-done | bytes 213024 | tf_op jit(solution)/shard_map/ppermute | solution.py:59
  30.3 1.6 %collective-permute-start.8 = (bf16[2,16,1664]{2,1,0:T(8,128)(2,1)S(1)}, bf16[2,16,1664]{2,1,0:T(8,128)(2,1)S(1)}, u32[]{:S(2)}, u32[]{:S(2)}) collective-permute-start(bf16[2,16,1664]{2,1,0:T(8,128)(2,1)S(1)} %slice.287), channel_id=1, source_target_pairs={{0,2},{1,5},{2,0},{3,7},{4,6},{5,1},{6,4},{7,3},{8,10},{9,13},{10,... | collective-permute-start | bytes 319496 | tf_op jit(solution)/shard_map/ppermute | solution.py:59
  31.9 1.5 %collective-permute-done.3 = bf16[4,16,1920]{2,1,0:T(8,128)(2,1)S(1)} collective-permute-done((bf16[4,16,1920]{2,1,0:T(8,128)(2,1)S(1)}, bf16[4,16,1920]{2,1,0:T(8,128)(2,1)S(1)}, u32[]{:S(2)}, u32[]{:S(2)}) %collective-permute-start.3) | collective-permute-done | bytes 245792 | tf_op jit(solution)/shard_map/ppermute | solution.py:59
  33.5 1.6 %collective-permute-start.4 = (bf16[2,16,1920]{2,1,0:T(8,128)(2,1)S(1)}, bf16[2,16,1920]{2,1,0:T(8,128)(2,1)S(1)}, u32[]{:S(2)}, u32[]{:S(2)}) collective-permute-start(bf16[2,16,1920]{2,1,0:T(8,128)(2,1)S(1)} %slice.278), channel_id=1, source_target_pairs={{0,2},{1,5},{2,0},{3,7},{4,6},{5,1},{6,4},{7,3},{8,10},{9,13},{10,... | collective-permute-start | bytes 368648 | tf_op jit(solution)/shard_map/ppermute | solution.py:59
  35.2 2.7 %collective-permute-start.9 = (bf16[2,16,1792]{2,1,0:T(8,128)(2,1)S(1)}, bf16[2,16,1792]{2,1,0:T(8,128)(2,1)S(1)}, u32[]{:S(2)}, u32[]{:S(2)}) collective-permute-start(bf16[2,16,1792]{2,1,0:T(8,128)(2,1)S(1)} %fusion.78), channel_id=1, source_target_pairs={{0,8},{1,9},{2,10},{3,11},{4,12},{5,13},{6,14},{7,15},{8,0},{9,1},... | collective-permute-start | bytes 344072 | tf_op jit(solution)/shard_map/ppermute | solution.py:421
  38.6 2.7 %collective-permute-start.5 = (bf16[2,16,1920]{2,1,0:T(8,128)(2,1)S(1)}, bf16[2,16,1920]{2,1,0:T(8,128)(2,1)S(1)}, u32[]{:S(2)}, u32[]{:S(2)}) collective-permute-start(bf16[2,16,1920]{2,1,0:T(8,128)(2,1)S(1)} %fusion.104.after_ref), channel_id=1, source_target_pairs={{0,8},{1,9},{2,10},{3,11},{4,12},{5,13},{6,14},{7,15},{8,0},{9,1},... | collective-permute-start | bytes 368648 | tf_op jit(solution)/shard_map/ppermute | solution.py:421
  41.8 1.3 %slice-done.5 = s8[3145728]{0:T(1024)(128)(4,1)S(1)} async-done(((s8[7340032]{0:T(1024)(128)(4,1)}), s8[3145728]{0:T(1024)(128)(4,1)S(1)}, s32[]{:S(2)}) %slice-start.5) | async-done | bytes 3145752
  43.7 4.3 %collective-permute-done.5.got_ref = bf16[2,16,1920]{2,1,0:T(8,128)(2,1)S(1)} collective-permute-done((bf16[2,16,1920]{2,1,0:T(8,128)(2,1)S(1)}, bf16[2,16,1920]{2,1,0:T(8,128)(2,1)S(1)}, u32[]{:S(2)}, u32[]{:S(2)}) %collective-permute-start.5) | collective-permute-done | bytes 122912 | tf_op jit(solution)/shard_map/ppermute | solution.py:421
  48.3 1.6 %collective-permute-start.10 = (bf16[2,16,1792]{2,1,0:T(8,128)(2,1)S(1)}, bf16[2,16,1792]{2,1,0:T(8,128)(2,1)S(1)}, u32[]{:S(2)}, u32[]{:S(2)}) collective-permute-start(bf16[2,16,1792]{2,1,0:T(8,128)(2,1)S(1)} %get-tuple-element.44), channel_id=1, source_target_pairs={{0,2},{1,5},{2,0},{3,7},{4,6},{5,1},{6,4},{7,3},{8,10},{9,13},{10,... | collective-permute-start | bytes 344072 | tf_op jit(solution)/shard_map/ppermute | solution.py:64
  50.4 2.8 %collective-permute-done.10 = bf16[2,16,1792]{2,1,0:T(8,128)(2,1)S(1)} collective-permute-done((bf16[2,16,1792]{2,1,0:T(8,128)(2,1)S(1)}, bf16[2,16,1792]{2,1,0:T(8,128)(2,1)S(1)}, u32[]{:S(2)}, u32[]{:S(2)}) %collective-permute-start.10) | collective-permute-done | bytes 114720 | tf_op jit(solution)/shard_map/ppermute | solution.py:64
  54.0 1.9 %collective-permute-done.13 = bf16[2,16,1920]{2,1,0:T(8,128)(2,1)S(1)} collective-permute-done((bf16[2,16,1920]{2,1,0:T(8,128)(2,1)S(1)}, bf16[2,16,1920]{2,1,0:T(8,128)(2,1)S(1)}, u32[]{:S(2)}, u32[]{:S(2)}) %collective-permute-start.13) | collective-permute-done | bytes 122912 | tf_op jit(solution)/shard_map/ppermute | solution.py:64
  56.4 2.9 %collective-permute-done.11 = bf16[4,16,1792]{2,1,0:T(8,128)(2,1)S(1)} collective-permute-done((bf16[4,16,1792]{2,1,0:T(8,128)(2,1)S(1)}, bf16[4,16,1792]{2,1,0:T(8,128)(2,1)S(1)}, u32[]{:S(2)}, u32[]{:S(2)}) %collective-permute-start.11) | collective-permute-done | bytes 229408 | tf_op jit(solution)/shard_map/ppermute | solution.py:64
  59.4 2.7 %collective-permute-done.14 = bf16[4,16,1920]{2,1,0:T(8,128)(2,1)S(1)} collective-permute-done((bf16[4,16,1920]{2,1,0:T(8,128)(2,1)S(1)}, bf16[4,16,1920]{2,1,0:T(8,128)(2,1)S(1)}, u32[]{:S(2)}, u32[]{:S(2)}) %collective-permute-start.14) | collective-permute-done | bytes 245792 | tf_op jit(solution)/shard_map/ppermute | solution.py:64
  67.0 1.8 %collective-permute-start.16 = (bf16[144,1024]{1,0:T(8,128)(2,1)S(1)}, bf16[144,1024]{1,0:T(8,128)(2,1)S(1)}, u32[]{:S(2)}, u32[]{:S(2)}) collective-permute-start(bf16[144,1024]{1,0:T(8,128)(2,1)S(1)} %pad_maximum_fusion.4), channel_id=1, source_target_pairs={{0,16},{16,0},{1,17},{17,1},{2,18},{18,2},{3,19},{19,3},{4,20},{20... | collective-permute-start | bytes 884744 | tf_op jit(solution)/shard_map/ppermute | solution.py:479
  71.2 5.8 %collective-permute-done.16 = bf16[144,1024]{1,0:T(8,128)(2,1)S(1)} collective-permute-done((bf16[144,1024]{1,0:T(8,128)(2,1)S(1)}, bf16[144,1024]{1,0:T(8,128)(2,1)S(1)}, u32[]{:S(2)}, u32[]{:S(2)}) %collective-permute-start.16) | collective-permute-done | bytes 294944 | tf_op jit(solution)/shard_map/ppermute | solution.py:479
  77.0 5.6 %collective-permute-done.18 = bf16[144,1024]{1,0:T(8,128)(2,1)S(1)} collective-permute-done((bf16[144,1024]{1,0:T(8,128)(2,1)S(1)}, bf16[144,1024]{1,0:T(8,128)(2,1)S(1)}, u32[]{:S(2)}, u32[]{:S(2)}) %collective-permute-start.18) | collective-permute-done | bytes 294944 | tf_op jit(solution)/shard_map/ppermute | solution.py:479
  89.2 3.8 %collective-permute-done.20 = bf16[4,16,1792]{2,1,0:T(8,128)(2,1)S(1)} collective-permute-done((bf16[4,16,1792]{2,1,0:T(8,128)(2,1)S(1)}, bf16[4,16,1792]{2,1,0:T(8,128)(2,1)S(1)}, u32[]{:S(2)}, u32[]{:S(2)}) %collective-permute-start.20) | collective-permute-done | bytes 229408 | tf_op jit(solution)/shard_map/ppermute | solution.py:59
  93.0 1.3 %collective-permute-start.21 = (bf16[2,16,1792]{2,1,0:T(8,128)(2,1)S(1)}, bf16[2,16,1792]{2,1,0:T(8,128)(2,1)S(1)}, u32[]{:S(2)}, u32[]{:S(2)}) collective-permute-start(bf16[2,16,1792]{2,1,0:T(8,128)(2,1)S(1)} %slice.306), channel_id=1, source_target_pairs={{0,2},{1,5},{2,0},{3,7},{4,6},{5,1},{6,4},{7,3},{8,10},{9,13},{10,... | collective-permute-start | bytes 344072 | tf_op jit(solution)/shard_map/ppermute | solution.py:59
  94.4 1.4 %collective-permute-done.24 = bf16[4,16,1792]{2,1,0:T(8,128)(2,1)S(1)} collective-permute-done((bf16[4,16,1792]{2,1,0:T(8,128)(2,1)S(1)}, bf16[4,16,1792]{2,1,0:T(8,128)(2,1)S(1)}, u32[]{:S(2)}, u32[]{:S(2)}) %collective-permute-start.24) | collective-permute-done | bytes 229408 | tf_op jit(solution)/shard_map/ppermute | solution.py:59
  95.9 1.3 %collective-permute-start.25 = (bf16[2,16,1792]{2,1,0:T(8,128)(2,1)S(1)}, bf16[2,16,1792]{2,1,0:T(8,128)(2,1)S(1)}, u32[]{:S(2)}, u32[]{:S(2)}) collective-permute-start(bf16[2,16,1792]{2,1,0:T(8,128)(2,1)S(1)} %slice.314), channel_id=1, source_target_pairs={{0,2},{1,5},{2,0},{3,7},{4,6},{5,1},{6,4},{7,3},{8,10},{9,13},{10,... | collective-permute-start | bytes 344072 | tf_op jit(solution)/shard_map/ppermute | solution.py:59
  98.0 1.9 %collective-permute-start.22 = (bf16[1,16,1792]{2,1,0:T(8,128)(2,1)S(1)}, bf16[1,16,1792]{2,1,0:T(8,128)(2,1)S(1)}, u32[]{:S(2)}, u32[]{:S(2)}) collective-permute-start(bf16[1,16,1792]{2,1,0:T(8,128)(2,1)S(1)} %slice.308), channel_id=1, source_target_pairs={{0,8},{1,9},{2,10},{3,11},{4,12},{5,13},{6,14},{7,15},{8,0},{9,1},... | collective-permute-start | bytes 172040 | tf_op jit(solution)/shard_map/ppermute | solution.py:59
  100.8 1.6 %collective-permute-start.26 = (bf16[1,16,1792]{2,1,0:T(8,128)(2,1)S(1)}, bf16[1,16,1792]{2,1,0:T(8,128)(2,1)S(1)}, u32[]{:S(2)}, u32[]{:S(2)}) collective-permute-start(bf16[1,16,1792]{2,1,0:T(8,128)(2,1)S(1)} %slice.316), channel_id=1, source_target_pairs={{0,8},{1,9},{2,10},{3,11},{4,12},{5,13},{6,14},{7,15},{8,0},{9,1},... | collective-permute-start | bytes 172040 | tf_op jit(solution)/shard_map/ppermute | solution.py:59
  102.4 2.2 %collective-permute-done.22 = bf16[1,16,1792]{2,1,0:T(8,128)(2,1)S(1)} collective-permute-done((bf16[1,16,1792]{2,1,0:T(8,128)(2,1)S(1)}, bf16[1,16,1792]{2,1,0:T(8,128)(2,1)S(1)}, u32[]{:S(2)}, u32[]{:S(2)}) %collective-permute-start.22) | collective-permute-done | bytes 57376 | tf_op jit(solution)/shard_map/ppermute | solution.py:59
  104.6 1.4 %collective-permute-done.26 = bf16[1,16,1792]{2,1,0:T(8,128)(2,1)S(1)} collective-permute-done((bf16[1,16,1792]{2,1,0:T(8,128)(2,1)S(1)}, bf16[1,16,1792]{2,1,0:T(8,128)(2,1)S(1)}, u32[]{:S(2)}, u32[]{:S(2)}) %collective-permute-start.26) | collective-permute-done | bytes 57376 | tf_op jit(solution)/shard_map/ppermute | solution.py:59
  (145 shorter events, 29.2 us)
Async XLA Ops:
  0.0 9.9 %collective-permute-start = (bf16[576,128]{1,0:T(8,128)(2,1)}, bf16[576,128]{1,0:T(8,128)(2,1)S(1)}, u32[]{:S(2)}, u32[]{:S(2)}) collective-permute-start(bf16[576,128]{1,0:T(8,128)(2,1)} %bitcast.70), channel_id=1, source_target_pairs={{0,16},{1,17},{2,18},{3,19},{4,20},{5,21},{6,22},{7,23},{8,24},{9,... | collective-permute-start | bytes 442376 | tf_op jit(solution)/shard_map/ppermute | solution.py:363
  11.6 7.8 %collective-permute-start.1 = (bf16[128,1024]{1,0:T(8,128)(2,1)S(1)}, bf16[128,1024]{1,0:T(8,128)(2,1)S(1)}, u32[]{:S(2)}, u32[]{:S(2)}) collective-permute-start(bf16[128,1024]{1,0:T(8,128)(2,1)S(1)} %attention.1.after_ref), channel_id=1, source_target_pairs={{0,16},{16,0},{1,17},{17,1},{2,18},{18,2},{3,19},{19,3},{4,20},{20... | collective-permute-start | bytes 786440 | tf_op jit(solution)/shard_map/ppermute | solution.py:374
  21.0 14.2 %copy-start.5 = (bf16[16,3584]{1,0:T(8,128)(2,1)S(1)}, bf16[16,3584]{1,0:T(8,128)(2,1)}, u32[]{:S(2)}) copy-start(bf16[16,3584]{1,0:T(8,128)(2,1)} %param.17) | copy-start | bytes 344068
  21.0 20.3 %slice-start.2 = ((s8[7340032]{0:T(1024)(128)(4,1)}), s8[3145728]{0:T(1024)(128)(4,1)S(1)}, s32[]{:S(2)}) async-start(s8[7340032]{0:T(1024)(128)(4,1)} %bitcast.64), calls=%async_computation.2 | async-start | bytes 6291456
  22.3 18.9 %slice-start.3 = ((s8[7340032]{0:T(1024)(128)(4,1)}), s8[4194304]{0:T(1024)(128)(4,1)S(1)}, s32[]{:S(2)}) async-start(s8[7340032]{0:T(1024)(128)(4,1)} %bitcast.64), calls=%async_computation.3 | async-start | bytes 8388608
  22.3 1.8 %collective-permute-start.6 = (bf16[8,16,1664]{2,1,0:T(8,128)(2,1)S(1)}, bf16[8,16,1664]{2,1,0:T(8,128)(2,1)S(1)}, u32[]{:S(2)}, u32[]{:S(2)}) collective-permute-start(bf16[8,16,1664]{2,1,0:T(8,128)(2,1)S(1)} %bitcast.84), channel_id=1, source_target_pairs={{0,1},{1,0},{2,3},{3,2},{4,5},{5,4},{6,7},{7,6},{8,9},{9,8},{10,11... | collective-permute-start | bytes 1277960 | tf_op jit(solution)/shard_map/ppermute | solution.py:59
  22.5 3.5 %collective-permute-start.2 = (bf16[8,16,1920]{2,1,0:T(8,128)(2,1)S(1)}, bf16[8,16,1920]{2,1,0:T(8,128)(2,1)S(1)}, u32[]{:S(2)}, u32[]{:S(2)}) collective-permute-start(bf16[8,16,1920]{2,1,0:T(8,128)(2,1)S(1)} %bitcast.81), channel_id=1, source_target_pairs={{0,1},{1,0},{2,3},{3,2},{4,5},{5,4},{6,7},{7,6},{8,9},{9,8},{10,11... | collective-permute-start | bytes 1474568 | tf_op jit(solution)/shard_map/ppermute | solution.py:59
  24.3 5.9 %collective-permute-start.7 = (bf16[4,16,1664]{2,1,0:T(8,128)(2,1)S(1)}, bf16[4,16,1664]{2,1,0:T(8,128)(2,1)S(1)}, u32[]{:S(2)}, u32[]{:S(2)}) collective-permute-start(bf16[4,16,1664]{2,1,0:T(8,128)(2,1)S(1)} %slice.285), channel_id=1, source_target_pairs={{0,4},{1,3},{2,6},{3,1},{4,0},{5,7},{6,2},{7,5},{8,12},{9,11},{10,... | collective-permute-start | bytes 638984 | tf_op jit(solution)/shard_map/ppermute | solution.py:59
  26.1 7.3 %collective-permute-start.3 = (bf16[4,16,1920]{2,1,0:T(8,128)(2,1)S(1)}, bf16[4,16,1920]{2,1,0:T(8,128)(2,1)S(1)}, u32[]{:S(2)}, u32[]{:S(2)}) collective-permute-start(bf16[4,16,1920]{2,1,0:T(8,128)(2,1)S(1)} %slice.276), channel_id=1, source_target_pairs={{0,4},{1,3},{2,6},{3,1},{4,0},{5,7},{6,2},{7,5},{8,12},{9,11},{10,... | collective-permute-start | bytes 737288 | tf_op jit(solution)/shard_map/ppermute | solution.py:59
  30.3 4.8 %collective-permute-start.8 = (bf16[2,16,1664]{2,1,0:T(8,128)(2,1)S(1)}, bf16[2,16,1664]{2,1,0:T(8,128)(2,1)S(1)}, u32[]{:S(2)}, u32[]{:S(2)}) collective-permute-start(bf16[2,16,1664]{2,1,0:T(8,128)(2,1)S(1)} %slice.287), channel_id=1, source_target_pairs={{0,2},{1,5},{2,0},{3,7},{4,6},{5,1},{6,4},{7,3},{8,10},{9,13},{10,... | collective-permute-start | bytes 319496 | tf_op jit(solution)/shard_map/ppermute | solution.py:59
  33.5 4.9 %collective-permute-start.4 = (bf16[2,16,1920]{2,1,0:T(8,128)(2,1)S(1)}, bf16[2,16,1920]{2,1,0:T(8,128)(2,1)S(1)}, u32[]{:S(2)}, u32[]{:S(2)}) collective-permute-start(bf16[2,16,1920]{2,1,0:T(8,128)(2,1)S(1)} %slice.278), channel_id=1, source_target_pairs={{0,2},{1,5},{2,0},{3,7},{4,6},{5,1},{6,4},{7,3},{8,10},{9,13},{10,... | collective-permute-start | bytes 368648 | tf_op jit(solution)/shard_map/ppermute | solution.py:59
  35.2 12.9 %collective-permute-start.9 = (bf16[2,16,1792]{2,1,0:T(8,128)(2,1)S(1)}, bf16[2,16,1792]{2,1,0:T(8,128)(2,1)S(1)}, u32[]{:S(2)}, u32[]{:S(2)}) collective-permute-start(bf16[2,16,1792]{2,1,0:T(8,128)(2,1)S(1)} %fusion.78), channel_id=1, source_target_pairs={{0,8},{1,9},{2,10},{3,11},{4,12},{5,13},{6,14},{7,15},{8,0},{9,1},... | collective-permute-start | bytes 344072 | tf_op jit(solution)/shard_map/ppermute | solution.py:421
  38.6 9.4 %collective-permute-start.5 = (bf16[2,16,1920]{2,1,0:T(8,128)(2,1)S(1)}, bf16[2,16,1920]{2,1,0:T(8,128)(2,1)S(1)}, u32[]{:S(2)}, u32[]{:S(2)}) collective-permute-start(bf16[2,16,1920]{2,1,0:T(8,128)(2,1)S(1)} %fusion.104.after_ref), channel_id=1, source_target_pairs={{0,8},{1,9},{2,10},{3,11},{4,12},{5,13},{6,14},{7,15},{8,0},{9,1},... | collective-permute-start | bytes 368648 | tf_op jit(solution)/shard_map/ppermute | solution.py:421
  48.3 4.9 %collective-permute-start.10 = (bf16[2,16,1792]{2,1,0:T(8,128)(2,1)S(1)}, bf16[2,16,1792]{2,1,0:T(8,128)(2,1)S(1)}, u32[]{:S(2)}, u32[]{:S(2)}) collective-permute-start(bf16[2,16,1792]{2,1,0:T(8,128)(2,1)S(1)} %get-tuple-element.44), channel_id=1, source_target_pairs={{0,2},{1,5},{2,0},{3,7},{4,6},{5,1},{6,4},{7,3},{8,10},{9,13},{10,... | collective-permute-start | bytes 344072 | tf_op jit(solution)/shard_map/ppermute | solution.py:64
  49.9 6.0 %collective-permute-start.13 = (bf16[2,16,1920]{2,1,0:T(8,128)(2,1)S(1)}, bf16[2,16,1920]{2,1,0:T(8,128)(2,1)S(1)}, u32[]{:S(2)}, u32[]{:S(2)}) collective-permute-start(bf16[2,16,1920]{2,1,0:T(8,128)(2,1)S(1)} %get-tuple-element.45), channel_id=1, source_target_pairs={{0,2},{1,5},{2,0},{3,7},{4,6},{5,1},{6,4},{7,3},{8,10},{9,13},{10,... | collective-permute-start | bytes 368648 | tf_op jit(solution)/shard_map/ppermute | solution.py:64
  53.2 6.1 %collective-permute-start.11 = (bf16[4,16,1792]{2,1,0:T(8,128)(2,1)S(1)}, bf16[4,16,1792]{2,1,0:T(8,128)(2,1)S(1)}, u32[]{:S(2)}, u32[]{:S(2)}) collective-permute-start(bf16[4,16,1792]{2,1,0:T(8,128)(2,1)S(1)} %pad_maximum_fusion.8), channel_id=1, source_target_pairs={{0,4},{1,3},{2,6},{3,1},{4,0},{5,7},{6,2},{7,5},{8,12},{9,11},{10,... | collective-permute-start | bytes 688136 | tf_op jit(solution)/shard_map/ppermute | solution.py:64
  55.9 6.3 %collective-permute-start.14 = (bf16[4,16,1920]{2,1,0:T(8,128)(2,1)S(1)}, bf16[4,16,1920]{2,1,0:T(8,128)(2,1)S(1)}, u32[]{:S(2)}, u32[]{:S(2)}) collective-permute-start(bf16[4,16,1920]{2,1,0:T(8,128)(2,1)S(1)} %pad_maximum_fusion.7), channel_id=1, source_target_pairs={{0,4},{1,3},{2,6},{3,1},{4,0},{5,7},{6,2},{7,5},{8,12},{9,11},{10,... | collective-permute-start | bytes 737288 | tf_op jit(solution)/shard_map/ppermute | solution.py:64
  59.4 2.9 %collective-permute-start.12 = (bf16[8,16,1792]{2,1,0:T(8,128)(2,1)S(1)}, bf16[8,16,1792]{2,1,0:T(8,128)(2,1)S(1)}, u32[]{:S(2)}, u32[]{:S(2)}) collective-permute-start(bf16[8,16,1792]{2,1,0:T(8,128)(2,1)S(1)} %pad_maximum_fusion.3), channel_id=1, source_target_pairs={{0,1},{1,0},{2,3},{3,2},{4,5},{5,4},{6,7},{7,6},{8,9},{9,8},{10,11... | collective-permute-start | bytes 1376264 | tf_op jit(solution)/shard_map/ppermute | solution.py:64
  62.2 3.3 %collective-permute-start.15 = (bf16[8,16,1920]{2,1,0:T(8,128)(2,1)S(1)}, bf16[8,16,1920]{2,1,0:T(8,128)(2,1)S(1)}, u32[]{:S(2)}, u32[]{:S(2)}) collective-permute-start(bf16[8,16,1920]{2,1,0:T(8,128)(2,1)S(1)} %pad_maximum_fusion.2), channel_id=1, source_target_pairs={{0,1},{1,0},{2,3},{3,2},{4,5},{5,4},{6,7},{7,6},{8,9},{9,8},{10,11... | collective-permute-start | bytes 1474568 | tf_op jit(solution)/shard_map/ppermute | solution.py:64
  64.7 5.6 %collective-permute-start.17 = (f32[256]{0:T(256)S(1)}, f32[256]{0:T(256)S(1)}, u32[]{:S(2)}, u32[]{:S(2)}) collective-permute-start(f32[256]{0:T(256)S(1)} %slice_reduce_fusion), channel_id=1, source_target_pairs={{0,16},{16,0},{1,17},{17,1},{2,18},{18,2},{3,19},{19,3},{4,20},{20... | collective-permute-start | bytes 3080 | tf_op jit(solution)/shard_map/ppermute | solution.py:452
  65.7 4.8 %slice-start = ((s8[7340032]{0:T(1024)(128)(4,1)}), s8[4194304]{0:T(1024)(128)(4,1)S(1)}, s32[]{:S(2)}) async-start(s8[7340032]{0:T(1024)(128)(4,1)} %bitcast.61), calls=%async_computation | async-start | bytes 8388608
  66.5 3.9 %slice-start.1 = ((s8[7340032]{0:T(1024)(128)(4,1)}), s8[3145728]{0:T(1024)(128)(4,1)S(1)}, s32[]{:S(2)}) async-start(s8[7340032]{0:T(1024)(128)(4,1)} %bitcast.61), calls=%async_computation.1 | async-start | bytes 6291456
  67.0 9.9 %collective-permute-start.16 = (bf16[144,1024]{1,0:T(8,128)(2,1)S(1)}, bf16[144,1024]{1,0:T(8,128)(2,1)S(1)}, u32[]{:S(2)}, u32[]{:S(2)}) collective-permute-start(bf16[144,1024]{1,0:T(8,128)(2,1)S(1)} %pad_maximum_fusion.4), channel_id=1, source_target_pairs={{0,16},{16,0},{1,17},{17,1},{2,18},{18,2},{3,19},{19,3},{4,20},{20... | collective-permute-start | bytes 884744 | tf_op jit(solution)/shard_map/ppermute | solution.py:479
  69.9 12.7 %collective-permute-start.18 = (bf16[144,1024]{1,0:T(8,128)(2,1)S(1)}, bf16[144,1024]{1,0:T(8,128)(2,1)S(1)}, u32[]{:S(2)}, u32[]{:S(2)}) collective-permute-start(bf16[144,1024]{1,0:T(8,128)(2,1)S(1)} %pad_maximum_fusion.5.after_ref), channel_id=1, source_target_pairs={{0,16},{16,0},{1,17},{17,1},{2,18},{18,2},{3,19},{19,3},{4,20},{20... | collective-permute-start | bytes 884744 | tf_op jit(solution)/shard_map/ppermute | solution.py:479
  84.9 1.9 %collective-permute-start.19 = (bf16[8,16,1792]{2,1,0:T(8,128)(2,1)S(1)}, bf16[8,16,1792]{2,1,0:T(8,128)(2,1)S(1)}, u32[]{:S(2)}, u32[]{:S(2)}) collective-permute-start(bf16[8,16,1792]{2,1,0:T(8,128)(2,1)S(1)} %bitcast.82), channel_id=1, source_target_pairs={{0,1},{1,0},{2,3},{3,2},{4,5},{5,4},{6,7},{7,6},{8,9},{9,8},{10,11... | collective-permute-start | bytes 1376264 | tf_op jit(solution)/shard_map/ppermute | solution.py:59
  85.9 2.0 %collective-permute-start.23 = (bf16[8,16,1792]{2,1,0:T(8,128)(2,1)S(1)}, bf16[8,16,1792]{2,1,0:T(8,128)(2,1)S(1)}, u32[]{:S(2)}, u32[]{:S(2)}) collective-permute-start(bf16[8,16,1792]{2,1,0:T(8,128)(2,1)S(1)} %bitcast.83), channel_id=1, source_target_pairs={{0,1},{1,0},{2,3},{3,2},{4,5},{5,4},{6,7},{7,6},{8,9},{9,8},{10,11... | collective-permute-start | bytes 1376264 | tf_op jit(solution)/shard_map/ppermute | solution.py:59
  86.9 6.1 %collective-permute-start.20 = (bf16[4,16,1792]{2,1,0:T(8,128)(2,1)S(1)}, bf16[4,16,1792]{2,1,0:T(8,128)(2,1)S(1)}, u32[]{:S(2)}, u32[]{:S(2)}) collective-permute-start(bf16[4,16,1792]{2,1,0:T(8,128)(2,1)S(1)} %slice.304), channel_id=1, source_target_pairs={{0,4},{1,3},{2,6},{3,1},{4,0},{5,7},{6,2},{7,5},{8,12},{9,11},{10,... | collective-permute-start | bytes 688136 | tf_op jit(solution)/shard_map/ppermute | solution.py:59
  88.1 7.7 %collective-permute-start.24 = (bf16[4,16,1792]{2,1,0:T(8,128)(2,1)S(1)}, bf16[4,16,1792]{2,1,0:T(8,128)(2,1)S(1)}, u32[]{:S(2)}, u32[]{:S(2)}) collective-permute-start(bf16[4,16,1792]{2,1,0:T(8,128)(2,1)S(1)} %slice.312), channel_id=1, source_target_pairs={{0,4},{1,3},{2,6},{3,1},{4,0},{5,7},{6,2},{7,5},{8,12},{9,11},{10,... | collective-permute-start | bytes 688136 | tf_op jit(solution)/shard_map/ppermute | solution.py:59
  93.0 4.9 %collective-permute-start.21 = (bf16[2,16,1792]{2,1,0:T(8,128)(2,1)S(1)}, bf16[2,16,1792]{2,1,0:T(8,128)(2,1)S(1)}, u32[]{:S(2)}, u32[]{:S(2)}) collective-permute-start(bf16[2,16,1792]{2,1,0:T(8,128)(2,1)S(1)} %slice.306), channel_id=1, source_target_pairs={{0,2},{1,5},{2,0},{3,7},{4,6},{5,1},{6,4},{7,3},{8,10},{9,13},{10,... | collective-permute-start | bytes 344072 | tf_op jit(solution)/shard_map/ppermute | solution.py:59
  95.9 4.9 %collective-permute-start.25 = (bf16[2,16,1792]{2,1,0:T(8,128)(2,1)S(1)}, bf16[2,16,1792]{2,1,0:T(8,128)(2,1)S(1)}, u32[]{:S(2)}, u32[]{:S(2)}) collective-permute-start(bf16[2,16,1792]{2,1,0:T(8,128)(2,1)S(1)} %slice.314), channel_id=1, source_target_pairs={{0,2},{1,5},{2,0},{3,7},{4,6},{5,1},{6,4},{7,3},{8,10},{9,13},{10,... | collective-permute-start | bytes 344072 | tf_op jit(solution)/shard_map/ppermute | solution.py:59
  98.0 6.6 %collective-permute-start.22 = (bf16[1,16,1792]{2,1,0:T(8,128)(2,1)S(1)}, bf16[1,16,1792]{2,1,0:T(8,128)(2,1)S(1)}, u32[]{:S(2)}, u32[]{:S(2)}) collective-permute-start(bf16[1,16,1792]{2,1,0:T(8,128)(2,1)S(1)} %slice.308), channel_id=1, source_target_pairs={{0,8},{1,9},{2,10},{3,11},{4,12},{5,13},{6,14},{7,15},{8,0},{9,1},... | collective-permute-start | bytes 172040 | tf_op jit(solution)/shard_map/ppermute | solution.py:59
  100.8 5.2 %collective-permute-start.26 = (bf16[1,16,1792]{2,1,0:T(8,128)(2,1)S(1)}, bf16[1,16,1792]{2,1,0:T(8,128)(2,1)S(1)}, u32[]{:S(2)}, u32[]{:S(2)}) collective-permute-start(bf16[1,16,1792]{2,1,0:T(8,128)(2,1)S(1)} %slice.316), channel_id=1, source_target_pairs={{0,8},{1,9},{2,10},{3,11},{4,12},{5,13},{6,14},{7,15},{8,0},{9,1},... | collective-permute-start | bytes 172040 | tf_op jit(solution)/shard_map/ppermute | solution.py:59
  (9 other events, 19.0 us)

commit v5 on v4

--- a/solution.py
+++ b/solution.py
@@ -323,6 +323,58 @@
     )(own, got, gain[None], squares, facts)
 
 
+def project_kernel(edge, values_ref, weights_ref, out_ref):
+    low, high = edge
+    out_ref[...] = jnp.dot(
+        values_ref[...], weights_ref[:, low:high], preferred_element_type=jnp.float32
+    ).astype(jnp.bfloat16)
+
+
+def project(values, weights, edge):
+    vmem = pl.BlockSpec(memory_space=pltpu.VMEM)
+    return pl.pallas_call(
+        functools.partial(project_kernel, edge),
+        out_shape=jax.ShapeDtypeStruct((values.shape[0], edge[1] - edge[0]), jnp.bfloat16),
+        in_specs=[vmem] * 2,
+        out_specs=vmem,
+        compiler_params=pltpu.CompilerParams(vmem_limit_bytes=8 << 20),
+        cost_estimate=pl.CostEstimate(flops=0, bytes_accessed=0, transcendentals=0),
+        name="project",
+    )(values, weights)
+
+
+def terms_kernel(edges, hidden_range, *refs):
+    row_refs, (gate_ref, up_ref, *more, out_ref) = refs[: len(edges)], refs[len(edges) :]
+    start, stop = hidden_range
+    for place, weights_ref in enumerate((gate_ref, up_ref)):
+        total = 0.0
+        for (low, high), row_ref in zip(edges, row_refs):
+            total = total + jnp.dot(
+                row_ref[...], weights_ref[low:high, start:stop], preferred_element_type=jnp.float32
+            )
+        width = stop - start
+        out_ref[:, place * width : (place + 1) * width] = total.astype(jnp.bfloat16)
+    if more:
+        placing_ref, facts_ref = more
+        out_ref[:, 2 * width :] = jnp.dot(
+            placing_ref[...], facts_ref[...], preferred_element_type=jnp.float32
+        ).astype(jnp.bfloat16)
+
+
+def hidden_terms(rows, edges, hidden_range, gate_weights, up_weights, *facts):
+    vmem = pl.BlockSpec(memory_space=pltpu.VMEM)
+    width = 2 * (hidden_range[1] - hidden_range[0]) + (facts[1].shape[1] if facts else 0)
+    return pl.pallas_call(
+        functools.partial(terms_kernel, edges, hidden_range),
+        out_shape=jax.ShapeDtypeStruct((rows[0].shape[0], width), jnp.bfloat16),
+        in_specs=[vmem] * (len(rows) + 2 + len(facts)),
+        out_specs=vmem,
+        compiler_params=pltpu.CompilerParams(vmem_limit_bytes=8 << 20),
+        cost_estimate=pl.CostEstimate(flops=0, bytes_accessed=0, transcendentals=0),
+        name="hidden_terms",
+    )(*rows, gate_weights, up_weights, *facts)
+
+
 def three_terms(values):
     first = values.astype(jnp.bfloat16)
     rest = values - first.astype(jnp.float32)
@@ -404,11 +456,10 @@
     residuals, arrived = [], []
     squares = jnp.zeros((2, token_count, 1), jnp.float32)
     for part, (low, high) in enumerate(edges):
-        array = (
-            jnp.dot(all_values, w_out[:, low:high], preferred_element_type=jnp.float32)
-            .astype(jnp.bfloat16)
-            .reshape(ep_count, token_count, -1)
-        )
+        array = project(all_values, w_out, (low, high))
+        if part == 0:
+            all_values, array = lax.optimization_barrier((all_values, array))
+        array = array.reshape(ep_count, token_count, -1)
         for step in range(bits - 1):
             total = halved(array, step, ep_count)
             array = total.astype(jnp.bfloat16)
@@ -435,7 +486,8 @@
         for step in range(bits - 2, -1, -1):
             array = doubled(array, step, ep_count)
         arrived.append(array.reshape(all_tokens, -1))
-    facts = arrived[-1][:, width:].astype(jnp.float32)
+    all_facts = arrived[-1][:, width:]
+    facts = all_facts.astype(jnp.float32)
     arrived[-1] = arrived[-1][:, :width]
 
     capacity = min(token_count, max(2, token_count * top_count * 9 // (8 * ep_count)))
@@ -448,16 +500,10 @@
     token_place = of_expert[0].astype(jnp.int32)
     token_weight = of_expert[1] + of_expert[2] + of_expert[3]
     token_squares = jnp.sum(facts[:, 4 * ep_count : 4 * ep_count + 3], axis=1)
-    if ctx_count == 2:
-        token_squares = token_squares + lax.ppermute(token_squares, "ctx", swap)
-    else:
-        token_squares = lax.psum(token_squares, "ctx")
-    token_scale = lax.rsqrt(token_squares / D + 1e-06)
     token_slot = jnp.where(token_place >= 0, chunk * capacity + token_place, -1)
     placing = jnp.arange(slots, dtype=jnp.int32)[:, None] == token_slot[None, :]
-    slot_scale = jnp.sum(jnp.where(placing, token_scale[None, :], 0.0), axis=1)
     slot_weight = jnp.sum(jnp.where(placing, token_weight[None, :], 0.0), axis=1)
-    placing = placing.astype(jnp.bfloat16)
+    placed, placing = placing, placing.astype(jnp.bfloat16)
     rows = [
         jnp.dot(placing, features, preferred_element_type=jnp.float32).astype(jnp.bfloat16)
         for features in arrived
@@ -465,43 +511,58 @@
     hidden = gate_weights.shape[1]
     ranges = split_edges(hidden, HIDDEN_PARTS)
     sums = []
-    for start, stop in ranges:
-        both = []
-        for weights in (gate_weights, up_weights):
-            total = 0.0
-            for (low, high), part_rows in zip(edges, rows):
-                total = total + jnp.dot(
-                    part_rows, weights[low:high, start:stop], preferred_element_type=jnp.float32
-                )
-            both.append(total.astype(jnp.bfloat16))
-        sums.append(jnp.concatenate(both, axis=1))
+    for hidden_range in ranges:
+        beside = (placing, all_facts) if hidden_range is ranges[0] and ctx_count == 2 else ()
+        sums.append(hidden_terms(rows, edges, hidden_range, gate_weights, up_weights, *beside))
+        if hidden_range is ranges[0]:
+            rows[0], sums[0] = lax.optimization_barrier((rows[0], sums[0]))
     if ctx_count == 2:
         others = [lax.ppermute(both, "ctx", swap) for both in sums]
         down_weights = fetched(w_down[0], sums[-1])
         others[0], down_weights = lax.optimization_barrier((others[0], down_weights))
-        sums = [
-            both.astype(jnp.float32) + other.astype(jnp.float32)
-            for both, other in zip(sums, others)
-        ]
+        squares_at = 2 * ranges[0][1] + facts_width
     else:
         down_weights = w_down[0]
-        sums = [lax.psum(both, "ctx").astype(jnp.float32) for both in sums]
+        others = [
+            lax.psum(both, "ctx").astype(jnp.float32) - both.astype(jnp.float32) for both in sums
+        ]
+        squares = jnp.where(placed, lax.psum(token_squares, "ctx")[None, :], 0.0)
+        slot_squares = jnp.sum(squares, axis=1, keepdims=True)
+    out_edges = split_edges(w_out.shape[1], PARTS)
     activated = []
-    for both in sums:
-        both = both * slot_scale[:, None]
-        half = both.shape[1] // 2
-        activated.append((jax.nn.silu(both[:, :half]) * both[:, half:]).astype(jnp.bfloat16))
+    for place in range(len(ranges)):
+        if place == 1:
+            others[1], first_products = lax.optimization_barrier((others[1], first_products))
+        both = sums[place].astype(jnp.float32) + others[place].astype(jnp.float32)
+        if place == 0:
+            if ctx_count == 2:
+                terms = both[:, squares_at : squares_at + 3]
+                slot_squares = jnp.sum(terms, axis=1, keepdims=True)
+            slot_scale = lax.rsqrt(slot_squares / D + 1e-06)
+        half = ranges[place][1] - ranges[place][0]
+        both = both[:, : 2 * half] * slot_scale
+        weighted = both[:, half:] * slot_weight[:, None]
+        activated.append((jax.nn.silu(both[:, :half]) * weighted).astype(jnp.bfloat16))
+        if place == 0:
+            start, stop = ranges[0]
+            first_products = [
+                jnp.dot(
+                    activated[0],
+                    down_weights[start:stop, low:high],
+                    preferred_element_type=jnp.float32,
+                )
+                for low, high in out_edges
+            ]
     spread = placing.T
     outputs = []
     residuals = jnp.concatenate(residuals, axis=1)
-    for low, high in split_edges(w_out.shape[1], PARTS):
+    for (low, high), produced in zip(out_edges, first_products):
         residual = residuals[:, low:high]
-        produced = 0.0
-        for (start, stop), part_rows in zip(ranges, activated):
+        for (start, stop), part_rows in zip(ranges[1:], activated[1:]):
             produced = produced + jnp.dot(
                 part_rows, down_weights[start:stop, low:high], preferred_element_type=jnp.float32
             )
-        produced = (produced * slot_weight[:, None]).astype(jnp.bfloat16)
+        produced = produced.astype(jnp.bfloat16)
         produced = lax.optimization_barrier(produced)
         array = (
             jnp.dot(spread, produced, preferred_element_type=jnp.float32)

time: 107 us -> 106 us (level)
  matrix products: 9.9 us -> 3.91 us
  Pallas kernels: 5.26 us -> 10.3 us
    dot_general x10 -> x2, matrix products: 6.2 us -> 0.99 us  [shards(): jnp.dot(activated[0], down_weights[start:stop, low:high], preferred_eleme...]
    pallas_call x0 -> x4, Pallas kernels: none -> 5.07 us  [the longest x2 2.71 us: hidden_terms(): pl.pallas_call(functools.partial(terms_kernel, edges, hidden_range), out_...]
  transfers between devices with their start and end apart: 27 -> 26, of which waited for: 20 -> 21; matrix products, arithmetic and copies ran while one was open for 8% -> 5% of each run, Pallas kernels for 3% -> 4%
where the time goes in v5:
time: 106 us
  waiting for transfers between devices  46.2 us (44%)
  starting transfers between devices  31.3 us (30%)
  Pallas kernels  10.3 us (10%)
  local copies, waits for them, and re-layouts  9.26 us (9%)
  other arithmetic  4.27 us (4%)
  matrix products  3.91 us (4%)
    ppermute x14, waiting for transfers between devices, halved(): got = lax.ppermute(array[half:], 'ep', crossing(count, step))  17.9 us
    ppermute x14, starting transfers between devices, halved(): got = lax.ppermute(array[half:], 'ep', crossing(count, step))  14.7 us
    ppermute x6, waiting for transfers between devices, doubled(): lax.ppermute(array, 'ep', crossing(count, step))  11.4 us
    ppermute x2, waiting for transfers between devices, shards(): others = [lax.ppermute(both, 'ctx', swap) for both in sums]  10.5 us
    unnamed x26, local copies, waits for them, and re-layouts  8.84 us
    ppermute x2, starting transfers between devices, shards(): got = lax.ppermute(sent, 'ep', crossing(ep_count, bits - 1))  5.29 us
    ppermute x1, starting transfers between devices, shards(): blocks = [key_columns, lax.ppermute(key_columns, 'ctx', [(0, 1)])]  4.87 us
    ppermute x2, waiting for transfers between devices, shards(): got = lax.ppermute(sent, 'ep', crossing(ep_count, bits - 1))  4 us
  transfers between devices with their start and end apart: 26, of which 21 were waited for; matrix products, arithmetic and copies ran while one was open for 5% of the time, Pallas kernels for 4%

profile of v5, /device:TPU:0, one launch (start us, length us, event | category | flops | bytes accessed | tf_op | source)
XLA Modules:
  0.0 105.9 jit_solution(2879572846581537178)
XLA Ops:
  0.0 4.9 %collective-permute-start = (bf16[576,128]{1,0:T(8,128)(2,1)}, bf16[576,128]{1,0:T(8,128)(2,1)S(1)}, u32[]{:S(2)}, u32[]{:S(2)}) collective-permute-start(bf16[576,128]{1,0:T(8,128)(2,1)} %bitcast.56), channel_id=1, source_target_pairs={{0,16},{1,17},{2,18},{3,19},{4,20},{5,21},{6,22},{7,23},{8,24},{9,... | collective-permute-start | bytes 442376 | tf_op jit(solution)/shard_map/ppermute | solution.py:415
  9.9 1.7 %attention.1.after_ref = bf16[128,1024]{1,0:T(8,128)(2,1)S(1)} custom-call(s32[1,256]{1,0:T(1,128)S(1)} %get-tuple-element.39.doc_ref, bf16[1024,640]{1,0:T(8,128)(2,1)S(1)} %get-tuple-element.40.heads_ref, f32[1024,128]{1,0:T(8,128)S(1)} %get-tuple-element.41.scores_ref, bf16[8,512,128]{2,1,0:T(8,128)(2,1)S(1)} %get-tuple-element.42.up_ref, ...), custom_call_target="tpu_custom_call" | custom-call | flops 570425344 | bytes 2228224 | tf_op jit(solution)/shard_map/attention/pallas_call | solution.py:208
  13.4 3.1 %copy-done = bf16[1024,3584]{1,0:T(8,128)(2,1)S(1)} copy-done((bf16[1024,3584]{1,0:T(8,128)(2,1)S(1)}, bf16[1024,3584]{1,0:T(8,128)(2,1)}, u32[]{:S(2)}) %copy-start) | copy-done | bytes 7340056
  17.0 2.4 %collective-permute-done.1 = bf16[128,1024]{1,0:T(8,128)(2,1)S(1)} collective-permute-done((bf16[128,1024]{1,0:T(8,128)(2,1)S(1)}, bf16[128,1024]{1,0:T(8,128)(2,1)S(1)}, u32[]{:S(2)}, u32[]{:S(2)}) %collective-permute-start.1) | collective-permute-done | bytes 262176 | tf_op jit(solution)/shard_map/ppermute | solution.py:426
  24.3 1.6 %collective-permute-start.7 = (bf16[4,16,1664]{2,1,0:T(8,128)(2,1)S(1)}, bf16[4,16,1664]{2,1,0:T(8,128)(2,1)S(1)}, u32[]{:S(2)}, u32[]{:S(2)}) collective-permute-start(bf16[4,16,1664]{2,1,0:T(8,128)(2,1)S(1)} %slice.245), channel_id=1, source_target_pairs={{0,4},{1,3},{2,6},{3,1},{4,0},{5,7},{6,2},{7,5},{8,12},{9,11},{10,... | collective-permute-start | bytes 638984 | tf_op jit(solution)/shard_map/ppermute | solution.py:59
  26.6 3.5 %collective-permute-done.7 = bf16[4,16,1664]{2,1,0:T(8,128)(2,1)S(1)} collective-permute-done((bf16[4,16,1664]{2,1,0:T(8,128)(2,1)S(1)}, bf16[4,16,1664]{2,1,0:T(8,128)(2,1)S(1)}, u32[]{:S(2)}, u32[]{:S(2)}) %collective-permute-start.7) | collective-permute-done | bytes 213024 | tf_op jit(solution)/shard_map/ppermute | solution.py:59
  30.3 1.6 %collective-permute-start.8 = (bf16[2,16,1664]{2,1,0:T(8,128)(2,1)S(1)}, bf16[2,16,1664]{2,1,0:T(8,128)(2,1)S(1)}, u32[]{:S(2)}, u32[]{:S(2)}) collective-permute-start(bf16[2,16,1664]{2,1,0:T(8,128)(2,1)S(1)} %slice.247), channel_id=1, source_target_pairs={{0,2},{1,5},{2,0},{3,7},{4,6},{5,1},{6,4},{7,3},{8,10},{9,13},{10,... | collective-permute-start | bytes 319496 | tf_op jit(solution)/shard_map/ppermute | solution.py:59
  31.8 1.5 %collective-permute-done.3 = bf16[4,16,1920]{2,1,0:T(8,128)(2,1)S(1)} collective-permute-done((bf16[4,16,1920]{2,1,0:T(8,128)(2,1)S(1)}, bf16[4,16,1920]{2,1,0:T(8,128)(2,1)S(1)}, u32[]{:S(2)}, u32[]{:S(2)}) %collective-permute-start.3) | collective-permute-done | bytes 245792 | tf_op jit(solution)/shard_map/ppermute | solution.py:59
  33.5 1.6 %collective-permute-start.4 = (bf16[2,16,1920]{2,1,0:T(8,128)(2,1)S(1)}, bf16[2,16,1920]{2,1,0:T(8,128)(2,1)S(1)}, u32[]{:S(2)}, u32[]{:S(2)}) collective-permute-start(bf16[2,16,1920]{2,1,0:T(8,128)(2,1)S(1)} %slice.239), channel_id=1, source_target_pairs={{0,2},{1,5},{2,0},{3,7},{4,6},{5,1},{6,4},{7,3},{8,10},{9,13},{10,... | collective-permute-start | bytes 368648 | tf_op jit(solution)/shard_map/ppermute | solution.py:59
  35.2 2.6 %collective-permute-start.9 = (bf16[2,16,1792]{2,1,0:T(8,128)(2,1)S(1)}, bf16[2,16,1792]{2,1,0:T(8,128)(2,1)S(1)}, u32[]{:S(2)}, u32[]{:S(2)}) collective-permute-start(bf16[2,16,1792]{2,1,0:T(8,128)(2,1)S(1)} %fusion.29), channel_id=1, source_target_pairs={{0,8},{1,9},{2,10},{3,11},{4,12},{5,13},{6,14},{7,15},{8,0},{9,1},... | collective-permute-start | bytes 344072 | tf_op jit(solution)/shard_map/ppermute | solution.py:472
  38.5 2.6 %collective-permute-start.5 = (bf16[2,16,1920]{2,1,0:T(8,128)(2,1)S(1)}, bf16[2,16,1920]{2,1,0:T(8,128)(2,1)S(1)}, u32[]{:S(2)}, u32[]{:S(2)}) collective-permute-start(bf16[2,16,1920]{2,1,0:T(8,128)(2,1)S(1)} %fusion.55.after_ref), channel_id=1, source_target_pairs={{0,8},{1,9},{2,10},{3,11},{4,12},{5,13},{6,14},{7,15},{8,0},{9,1},... | collective-permute-start | bytes 368648 | tf_op jit(solution)/shard_map/ppermute | solution.py:472
  41.8 1.6 %slice-done.5 = s8[4194304]{0:T(1024)(128)(4,1)S(1)} async-done(((s8[7340032]{0:T(1024)(128)(4,1)}), s8[4194304]{0:T(1024)(128)(4,1)S(1)}, s32[]{:S(2)}) %slice-start.5) | async-done | bytes 4194328
  43.9 4.0 %collective-permute-done.5.got_ref = bf16[2,16,1920]{2,1,0:T(8,128)(2,1)S(1)} collective-permute-done((bf16[2,16,1920]{2,1,0:T(8,128)(2,1)S(1)}, bf16[2,16,1920]{2,1,0:T(8,128)(2,1)S(1)}, u32[]{:S(2)}, u32[]{:S(2)}) %collective-permute-start.5) | collective-permute-done | bytes 122912 | tf_op jit(solution)/shard_map/ppermute | solution.py:472
  48.3 1.6 %collective-permute-start.10 = (bf16[2,16,1792]{2,1,0:T(8,128)(2,1)S(1)}, bf16[2,16,1792]{2,1,0:T(8,128)(2,1)S(1)}, u32[]{:S(2)}, u32[]{:S(2)}) collective-permute-start(bf16[2,16,1792]{2,1,0:T(8,128)(2,1)S(1)} %get-tuple-element.53), channel_id=1, source_target_pairs={{0,2},{1,5},{2,0},{3,7},{4,6},{5,1},{6,4},{7,3},{8,10},{9,13},{10,... | collective-permute-start | bytes 344072 | tf_op jit(solution)/shard_map/ppermute | solution.py:64
  50.4 2.8 %collective-permute-done.10 = bf16[2,16,1792]{2,1,0:T(8,128)(2,1)S(1)} collective-permute-done((bf16[2,16,1792]{2,1,0:T(8,128)(2,1)S(1)}, bf16[2,16,1792]{2,1,0:T(8,128)(2,1)S(1)}, u32[]{:S(2)}, u32[]{:S(2)}) %collective-permute-start.10) | collective-permute-done | bytes 114720 | tf_op jit(solution)/shard_map/ppermute | solution.py:64
  53.9 1.9 %collective-permute-done.13 = bf16[2,16,1920]{2,1,0:T(8,128)(2,1)S(1)} collective-permute-done((bf16[2,16,1920]{2,1,0:T(8,128)(2,1)S(1)}, bf16[2,16,1920]{2,1,0:T(8,128)(2,1)S(1)}, u32[]{:S(2)}, u32[]{:S(2)}) %collective-permute-start.13) | collective-permute-done | bytes 122912 | tf_op jit(solution)/shard_map/ppermute | solution.py:64
  56.3 2.9 %collective-permute-done.11 = bf16[4,16,1792]{2,1,0:T(8,128)(2,1)S(1)} collective-permute-done((bf16[4,16,1792]{2,1,0:T(8,128)(2,1)S(1)}, bf16[4,16,1792]{2,1,0:T(8,128)(2,1)S(1)}, u32[]{:S(2)}, u32[]{:S(2)}) %collective-permute-start.11) | collective-permute-done | bytes 229408 | tf_op jit(solution)/shard_map/ppermute | solution.py:64
  59.4 2.7 %collective-permute-done.14 = bf16[4,16,1920]{2,1,0:T(8,128)(2,1)S(1)} collective-permute-done((bf16[4,16,1920]{2,1,0:T(8,128)(2,1)S(1)}, bf16[4,16,1920]{2,1,0:T(8,128)(2,1)S(1)}, u32[]{:S(2)}, u32[]{:S(2)}) %collective-permute-start.14) | collective-permute-done | bytes 245792 | tf_op jit(solution)/shard_map/ppermute | solution.py:64
  64.6 1.4 %hidden_terms.2 = bf16[144,1152]{1,0:T(8,128)(2,1)S(1)} custom-call(bf16[144,1920]{1,0:T(8,128)(2,1)S(1)} %convolution_convert_fusion.3.refs_0_, bf16[144,1664]{1,0:T(8,128)(2,1)S(1)} %convolution_convert_fusion.2.refs_1_, bf16[3584,1024]{1,0:T(8,128)(2,1)S(1)} %fetch_weights.5.refs_2_, bf16[3584,1024]{1,0:T(8,128)(2,1)S(1)} %fetch_weights.6.refs_3_, ...), custom_call_target="tpu_custom_call" | custom-call | tf_op jit(solution)/shard_map/hidden_terms/pallas_call | solution.py:367
  66.5 1.3 %hidden_terms.3.after_ref = bf16[144,1024]{1,0:T(8,128)(2,1)S(1)} custom-call(bf16[144,1920]{1,0:T(8,128)(2,1)S(1)} %convolution_convert_fusion.3.refs_0_, bf16[144,1664]{1,0:T(8,128)(2,1)S(1)} %convolution_convert_fusion.2.refs_1_, bf16[3584,1024]{1,0:T(8,128)(2,1)S(1)} %fetch_weights.5.refs_2_, bf16[3584,1024]{1,0:T(8,128)(2,1)S(1)} %fetch_weights.6.refs_3_), custom_call_target="tpu_custom_call" | custom-call | tf_op jit(solution)/shard_map/hidden_terms/pallas_call | solution.py:367
  67.8 1.8 %collective-permute-start.16 = (bf16[144,1024]{1,0:T(8,128)(2,1)S(1)}, bf16[144,1024]{1,0:T(8,128)(2,1)S(1)}, u32[]{:S(2)}, u32[]{:S(2)}) collective-permute-start(bf16[144,1024]{1,0:T(8,128)(2,1)S(1)} %hidden_terms.3.after_ref), channel_id=1, source_target_pairs={{0,16},{16,0},{1,17},{17,1},{2,18},{18,2},{3,19},{19,3},{4,20},{20... | collective-permute-start | bytes 884744 | tf_op jit(solution)/shard_map/ppermute | solution.py:520
  70.3 6.4 %collective-permute-done.17 = bf16[144,1152]{1,0:T(8,128)(2,1)S(1)} collective-permute-done((bf16[144,1152]{1,0:T(8,128)(2,1)S(1)}, bf16[144,1152]{1,0:T(8,128)(2,1)S(1)}, u32[]{:S(2)}, u32[]{:S(2)}) %collective-permute-start.17) | collective-permute-done | bytes 331808 | tf_op jit(solution)/shard_map/ppermute | solution.py:520
  78.1 4.1 %collective-permute-done.16 = bf16[144,1024]{1,0:T(8,128)(2,1)S(1)} collective-permute-done((bf16[144,1024]{1,0:T(8,128)(2,1)S(1)}, bf16[144,1024]{1,0:T(8,128)(2,1)S(1)}, u32[]{:S(2)}, u32[]{:S(2)}) %collective-permute-start.16) | collective-permute-done | bytes 294944 | tf_op jit(solution)/shard_map/ppermute | solution.py:520
  86.9 1.5 %collective-permute-start.19 = (bf16[4,16,1792]{2,1,0:T(8,128)(2,1)S(1)}, bf16[4,16,1792]{2,1,0:T(8,128)(2,1)S(1)}, u32[]{:S(2)}, u32[]{:S(2)}) collective-permute-start(bf16[4,16,1792]{2,1,0:T(8,128)(2,1)S(1)} %slice.265), channel_id=1, source_target_pairs={{0,4},{1,3},{2,6},{3,1},{4,0},{5,7},{6,2},{7,5},{8,12},{9,11},{10,... | collective-permute-start | bytes 688136 | tf_op jit(solution)/shard_map/ppermute | solution.py:59
  88.4 3.8 %collective-permute-done.23 = bf16[4,16,1792]{2,1,0:T(8,128)(2,1)S(1)} collective-permute-done((bf16[4,16,1792]{2,1,0:T(8,128)(2,1)S(1)}, bf16[4,16,1792]{2,1,0:T(8,128)(2,1)S(1)}, u32[]{:S(2)}, u32[]{:S(2)}) %collective-permute-start.23) | collective-permute-done | bytes 229408 | tf_op jit(solution)/shard_map/ppermute | solution.py:59
  92.3 1.3 %collective-permute-start.24 = (bf16[2,16,1792]{2,1,0:T(8,128)(2,1)S(1)}, bf16[2,16,1792]{2,1,0:T(8,128)(2,1)S(1)}, u32[]{:S(2)}, u32[]{:S(2)}) collective-permute-start(bf16[2,16,1792]{2,1,0:T(8,128)(2,1)S(1)} %slice.275), channel_id=1, source_target_pairs={{0,2},{1,5},{2,0},{3,7},{4,6},{5,1},{6,4},{7,3},{8,10},{9,13},{10,... | collective-permute-start | bytes 344072 | tf_op jit(solution)/shard_map/ppermute | solution.py:59
  93.6 1.4 %collective-permute-done.19 = bf16[4,16,1792]{2,1,0:T(8,128)(2,1)S(1)} collective-permute-done((bf16[4,16,1792]{2,1,0:T(8,128)(2,1)S(1)}, bf16[4,16,1792]{2,1,0:T(8,128)(2,1)S(1)}, u32[]{:S(2)}, u32[]{:S(2)}) %collective-permute-start.19) | collective-permute-done | bytes 229408 | tf_op jit(solution)/shard_map/ppermute | solution.py:59
  95.1 1.3 %collective-permute-start.20 = (bf16[2,16,1792]{2,1,0:T(8,128)(2,1)S(1)}, bf16[2,16,1792]{2,1,0:T(8,128)(2,1)S(1)}, u32[]{:S(2)}, u32[]{:S(2)}) collective-permute-start(bf16[2,16,1792]{2,1,0:T(8,128)(2,1)S(1)} %slice.267), channel_id=1, source_target_pairs={{0,2},{1,5},{2,0},{3,7},{4,6},{5,1},{6,4},{7,3},{8,10},{9,13},{10,... | collective-permute-start | bytes 344072 | tf_op jit(solution)/shard_map/ppermute | solution.py:59
  97.2 1.9 %collective-permute-start.25 = (bf16[1,16,1792]{2,1,0:T(8,128)(2,1)S(1)}, bf16[1,16,1792]{2,1,0:T(8,128)(2,1)S(1)}, u32[]{:S(2)}, u32[]{:S(2)}) collective-permute-start(bf16[1,16,1792]{2,1,0:T(8,128)(2,1)S(1)} %slice.277), channel_id=1, source_target_pairs={{0,8},{1,9},{2,10},{3,11},{4,12},{5,13},{6,14},{7,15},{8,0},{9,1},... | collective-permute-start | bytes 172040 | tf_op jit(solution)/shard_map/ppermute | solution.py:59
  100.0 1.6 %collective-permute-start.21 = (bf16[1,16,1792]{2,1,0:T(8,128)(2,1)S(1)}, bf16[1,16,1792]{2,1,0:T(8,128)(2,1)S(1)}, u32[]{:S(2)}, u32[]{:S(2)}) collective-permute-start(bf16[1,16,1792]{2,1,0:T(8,128)(2,1)S(1)} %slice.269), channel_id=1, source_target_pairs={{0,8},{1,9},{2,10},{3,11},{4,12},{5,13},{6,14},{7,15},{8,0},{9,1},... | collective-permute-start | bytes 172040 | tf_op jit(solution)/shard_map/ppermute | solution.py:59
  101.6 2.2 %collective-permute-done.25 = bf16[1,16,1792]{2,1,0:T(8,128)(2,1)S(1)} collective-permute-done((bf16[1,16,1792]{2,1,0:T(8,128)(2,1)S(1)}, bf16[1,16,1792]{2,1,0:T(8,128)(2,1)S(1)}, u32[]{:S(2)}, u32[]{:S(2)}) %collective-permute-start.25) | collective-permute-done | bytes 57376 | tf_op jit(solution)/shard_map/ppermute | solution.py:59
  103.8 1.4 %collective-permute-done.21 = bf16[1,16,1792]{2,1,0:T(8,128)(2,1)S(1)} collective-permute-done((bf16[1,16,1792]{2,1,0:T(8,128)(2,1)S(1)}, bf16[1,16,1792]{2,1,0:T(8,128)(2,1)S(1)}, u32[]{:S(2)}, u32[]{:S(2)}) %collective-permute-start.21) | collective-permute-done | bytes 57376 | tf_op jit(solution)/shard_map/ppermute | solution.py:59
  (138 shorter events, 29.0 us)
Async XLA Ops:
  0.0 9.9 %collective-permute-start = (bf16[576,128]{1,0:T(8,128)(2,1)}, bf16[576,128]{1,0:T(8,128)(2,1)S(1)}, u32[]{:S(2)}, u32[]{:S(2)}) collective-permute-start(bf16[576,128]{1,0:T(8,128)(2,1)} %bitcast.56), channel_id=1, source_target_pairs={{0,16},{1,17},{2,18},{3,19},{4,20},{5,21},{6,22},{7,23},{8,24},{9,... | collective-permute-start | bytes 442376 | tf_op jit(solution)/shard_map/ppermute | solution.py:415
  11.6 7.8 %collective-permute-start.1 = (bf16[128,1024]{1,0:T(8,128)(2,1)S(1)}, bf16[128,1024]{1,0:T(8,128)(2,1)S(1)}, u32[]{:S(2)}, u32[]{:S(2)}) collective-permute-start(bf16[128,1024]{1,0:T(8,128)(2,1)S(1)} %attention.1.after_ref), channel_id=1, source_target_pairs={{0,16},{16,0},{1,17},{17,1},{2,18},{18,2},{3,19},{19,3},{4,20},{20... | collective-permute-start | bytes 786440 | tf_op jit(solution)/shard_map/ppermute | solution.py:426
  21.1 14.0 %copy-start.5 = (bf16[16,3584]{1,0:T(8,128)(2,1)S(1)}, bf16[16,3584]{1,0:T(8,128)(2,1)}, u32[]{:S(2)}) copy-start(bf16[16,3584]{1,0:T(8,128)(2,1)} %param.17) | copy-start | bytes 344068
  21.1 20.1 %slice-start.2 = ((s8[7340032]{0:T(1024)(128)(4,1)}), s8[4194304]{0:T(1024)(128)(4,1)S(1)}, s32[]{:S(2)}) async-start(s8[7340032]{0:T(1024)(128)(4,1)} %bitcast.50), calls=%async_computation.2 | async-start | bytes 8388608
  22.3 18.9 %slice-start.3 = ((s8[7340032]{0:T(1024)(128)(4,1)}), s8[3145728]{0:T(1024)(128)(4,1)S(1)}, s32[]{:S(2)}) async-start(s8[7340032]{0:T(1024)(128)(4,1)} %bitcast.50), calls=%async_computation.3 | async-start | bytes 6291456
  22.3 1.8 %collective-permute-start.6 = (bf16[8,16,1664]{2,1,0:T(8,128)(2,1)S(1)}, bf16[8,16,1664]{2,1,0:T(8,128)(2,1)S(1)}, u32[]{:S(2)}, u32[]{:S(2)}) collective-permute-start(bf16[8,16,1664]{2,1,0:T(8,128)(2,1)S(1)} %bitcast.70), channel_id=1, source_target_pairs={{0,1},{1,0},{2,3},{3,2},{4,5},{5,4},{6,7},{7,6},{8,9},{9,8},{10,11... | collective-permute-start | bytes 1277960 | tf_op jit(solution)/shard_map/ppermute | solution.py:59
  22.5 3.5 %collective-permute-start.2 = (bf16[8,16,1920]{2,1,0:T(8,128)(2,1)S(1)}, bf16[8,16,1920]{2,1,0:T(8,128)(2,1)S(1)}, u32[]{:S(2)}, u32[]{:S(2)}) collective-permute-start(bf16[8,16,1920]{2,1,0:T(8,128)(2,1)S(1)} %bitcast.67), channel_id=1, source_target_pairs={{0,1},{1,0},{2,3},{3,2},{4,5},{5,4},{6,7},{7,6},{8,9},{9,8},{10,11... | collective-permute-start | bytes 1474568 | tf_op jit(solution)/shard_map/ppermute | solution.py:59
  24.3 5.9 %collective-permute-start.7 = (bf16[4,16,1664]{2,1,0:T(8,128)(2,1)S(1)}, bf16[4,16,1664]{2,1,0:T(8,128)(2,1)S(1)}, u32[]{:S(2)}, u32[]{:S(2)}) collective-permute-start(bf16[4,16,1664]{2,1,0:T(8,128)(2,1)S(1)} %slice.245), channel_id=1, source_target_pairs={{0,4},{1,3},{2,6},{3,1},{4,0},{5,7},{6,2},{7,5},{8,12},{9,11},{10,... | collective-permute-start | bytes 638984 | tf_op jit(solution)/shard_map/ppermute | solution.py:59
  26.1 7.3 %collective-permute-start.3 = (bf16[4,16,1920]{2,1,0:T(8,128)(2,1)S(1)}, bf16[4,16,1920]{2,1,0:T(8,128)(2,1)S(1)}, u32[]{:S(2)}, u32[]{:S(2)}) collective-permute-start(bf16[4,16,1920]{2,1,0:T(8,128)(2,1)S(1)} %slice.237), channel_id=1, source_target_pairs={{0,4},{1,3},{2,6},{3,1},{4,0},{5,7},{6,2},{7,5},{8,12},{9,11},{10,... | collective-permute-start | bytes 737288 | tf_op jit(solution)/shard_map/ppermute | solution.py:59
  30.3 4.8 %collective-permute-start.8 = (bf16[2,16,1664]{2,1,0:T(8,128)(2,1)S(1)}, bf16[2,16,1664]{2,1,0:T(8,128)(2,1)S(1)}, u32[]{:S(2)}, u32[]{:S(2)}) collective-permute-start(bf16[2,16,1664]{2,1,0:T(8,128)(2,1)S(1)} %slice.247), channel_id=1, source_target_pairs={{0,2},{1,5},{2,0},{3,7},{4,6},{5,1},{6,4},{7,3},{8,10},{9,13},{10,... | collective-permute-start | bytes 319496 | tf_op jit(solution)/shard_map/ppermute | solution.py:59
  33.5 4.9 %collective-permute-start.4 = (bf16[2,16,1920]{2,1,0:T(8,128)(2,1)S(1)}, bf16[2,16,1920]{2,1,0:T(8,128)(2,1)S(1)}, u32[]{:S(2)}, u32[]{:S(2)}) collective-permute-start(bf16[2,16,1920]{2,1,0:T(8,128)(2,1)S(1)} %slice.239), channel_id=1, source_target_pairs={{0,2},{1,5},{2,0},{3,7},{4,6},{5,1},{6,4},{7,3},{8,10},{9,13},{10,... | collective-permute-start | bytes 368648 | tf_op jit(solution)/shard_map/ppermute | solution.py:59
  35.2 12.9 %collective-permute-start.9 = (bf16[2,16,1792]{2,1,0:T(8,128)(2,1)S(1)}, bf16[2,16,1792]{2,1,0:T(8,128)(2,1)S(1)}, u32[]{:S(2)}, u32[]{:S(2)}) collective-permute-start(bf16[2,16,1792]{2,1,0:T(8,128)(2,1)S(1)} %fusion.29), channel_id=1, source_target_pairs={{0,8},{1,9},{2,10},{3,11},{4,12},{5,13},{6,14},{7,15},{8,0},{9,1},... | collective-permute-start | bytes 344072 | tf_op jit(solution)/shard_map/ppermute | solution.py:472
  38.5 3.3 %slice-start.4 = ((s8[7340032]{0:T(1024)(128)(4,1)}), s8[3145728]{0:T(1024)(128)(4,1)S(1)}, s32[]{:S(2)}) async-start(s8[7340032]{0:T(1024)(128)(4,1)} %bitcast.53), calls=%async_computation.4 | async-start | bytes 6291456
  38.5 9.4 %collective-permute-start.5 = (bf16[2,16,1920]{2,1,0:T(8,128)(2,1)S(1)}, bf16[2,16,1920]{2,1,0:T(8,128)(2,1)S(1)}, u32[]{:S(2)}, u32[]{:S(2)}) collective-permute-start(bf16[2,16,1920]{2,1,0:T(8,128)(2,1)S(1)} %fusion.55.after_ref), channel_id=1, source_target_pairs={{0,8},{1,9},{2,10},{3,11},{4,12},{5,13},{6,14},{7,15},{8,0},{9,1},... | collective-permute-start | bytes 368648 | tf_op jit(solution)/shard_map/ppermute | solution.py:472
  48.3 4.9 %collective-permute-start.10 = (bf16[2,16,1792]{2,1,0:T(8,128)(2,1)S(1)}, bf16[2,16,1792]{2,1,0:T(8,128)(2,1)S(1)}, u32[]{:S(2)}, u32[]{:S(2)}) collective-permute-start(bf16[2,16,1792]{2,1,0:T(8,128)(2,1)S(1)} %get-tuple-element.53), channel_id=1, source_target_pairs={{0,2},{1,5},{2,0},{3,7},{4,6},{5,1},{6,4},{7,3},{8,10},{9,13},{10,... | collective-permute-start | bytes 344072 | tf_op jit(solution)/shard_map/ppermute | solution.py:64
  49.9 6.0 %collective-permute-start.13 = (bf16[2,16,1920]{2,1,0:T(8,128)(2,1)S(1)}, bf16[2,16,1920]{2,1,0:T(8,128)(2,1)S(1)}, u32[]{:S(2)}, u32[]{:S(2)}) collective-permute-start(bf16[2,16,1920]{2,1,0:T(8,128)(2,1)S(1)} %get-tuple-element.54), channel_id=1, source_target_pairs={{0,2},{1,5},{2,0},{3,7},{4,6},{5,1},{6,4},{7,3},{8,10},{9,13},{10,... | collective-permute-start | bytes 368648 | tf_op jit(solution)/shard_map/ppermute | solution.py:64
  53.2 6.1 %collective-permute-start.11 = (bf16[4,16,1792]{2,1,0:T(8,128)(2,1)S(1)}, bf16[4,16,1792]{2,1,0:T(8,128)(2,1)S(1)}, u32[]{:S(2)}, u32[]{:S(2)}) collective-permute-start(bf16[4,16,1792]{2,1,0:T(8,128)(2,1)S(1)} %pad_maximum_fusion.6), channel_id=1, source_target_pairs={{0,4},{1,3},{2,6},{3,1},{4,0},{5,7},{6,2},{7,5},{8,12},{9,11},{10,... | collective-permute-start | bytes 688136 | tf_op jit(solution)/shard_map/ppermute | solution.py:64
  55.9 6.3 %collective-permute-start.14 = (bf16[4,16,1920]{2,1,0:T(8,128)(2,1)S(1)}, bf16[4,16,1920]{2,1,0:T(8,128)(2,1)S(1)}, u32[]{:S(2)}, u32[]{:S(2)}) collective-permute-start(bf16[4,16,1920]{2,1,0:T(8,128)(2,1)S(1)} %pad_maximum_fusion.5), channel_id=1, source_target_pairs={{0,4},{1,3},{2,6},{3,1},{4,0},{5,7},{6,2},{7,5},{8,12},{9,11},{10,... | collective-permute-start | bytes 737288 | tf_op jit(solution)/shard_map/ppermute | solution.py:64
  59.3 3.0 %collective-permute-start.12 = (bf16[8,16,1792]{2,1,0:T(8,128)(2,1)S(1)}, bf16[8,16,1792]{2,1,0:T(8,128)(2,1)S(1)}, u32[]{:S(2)}, u32[]{:S(2)}) collective-permute-start(bf16[8,16,1792]{2,1,0:T(8,128)(2,1)S(1)} %pad_maximum_fusion.3), channel_id=1, source_target_pairs={{0,1},{1,0},{2,3},{3,2},{4,5},{5,4},{6,7},{7,6},{8,9},{9,8},{10,11... | collective-permute-start | bytes 1376264 | tf_op jit(solution)/shard_map/ppermute | solution.py:64
  62.2 1.9 %collective-permute-start.15 = (bf16[8,16,1920]{2,1,0:T(8,128)(2,1)S(1)}, bf16[8,16,1920]{2,1,0:T(8,128)(2,1)S(1)}, u32[]{:S(2)}, u32[]{:S(2)}) collective-permute-start(bf16[8,16,1920]{2,1,0:T(8,128)(2,1)S(1)} %pad_maximum_fusion.2), channel_id=1, source_target_pairs={{0,1},{1,0},{2,3},{3,2},{4,5},{5,4},{6,7},{7,6},{8,9},{9,8},{10,11... | collective-permute-start | bytes 1474568 | tf_op jit(solution)/shard_map/ppermute | solution.py:64
  64.3 5.4 %slice-start = ((s8[7340032]{0:T(1024)(128)(4,1)}), s8[4194304]{0:T(1024)(128)(4,1)S(1)}, s32[]{:S(2)}) async-start(s8[7340032]{0:T(1024)(128)(4,1)} %bitcast.47), calls=%async_computation | async-start | bytes 8388608
  64.6 5.0 %slice-start.1 = ((s8[7340032]{0:T(1024)(128)(4,1)}), s8[3145728]{0:T(1024)(128)(4,1)S(1)}, s32[]{:S(2)}) async-start(s8[7340032]{0:T(1024)(128)(4,1)} %bitcast.47), calls=%async_computation.1 | async-start | bytes 6291456
  66.0 10.7 %collective-permute-start.17 = (bf16[144,1152]{1,0:T(8,128)(2,1)S(1)}, bf16[144,1152]{1,0:T(8,128)(2,1)S(1)}, u32[]{:S(2)}, u32[]{:S(2)}) collective-permute-start(bf16[144,1152]{1,0:T(8,128)(2,1)S(1)} %hidden_terms.2), channel_id=1, source_target_pairs={{0,16},{16,0},{1,17},{17,1},{2,18},{18,2},{3,19},{19,3},{4,20},{20... | collective-permute-start | bytes 995336 | tf_op jit(solution)/shard_map/ppermute | solution.py:520
  67.8 14.4 %collective-permute-start.16 = (bf16[144,1024]{1,0:T(8,128)(2,1)S(1)}, bf16[144,1024]{1,0:T(8,128)(2,1)S(1)}, u32[]{:S(2)}, u32[]{:S(2)}) collective-permute-start(bf16[144,1024]{1,0:T(8,128)(2,1)S(1)} %hidden_terms.3.after_ref), channel_id=1, source_target_pairs={{0,16},{16,0},{1,17},{17,1},{2,18},{18,2},{3,19},{19,3},{4,20},{20... | collective-permute-start | bytes 884744 | tf_op jit(solution)/shard_map/ppermute | solution.py:520
  84.1 1.9 %collective-permute-start.22 = (bf16[8,16,1792]{2,1,0:T(8,128)(2,1)S(1)}, bf16[8,16,1792]{2,1,0:T(8,128)(2,1)S(1)}, u32[]{:S(2)}, u32[]{:S(2)}) collective-permute-start(bf16[8,16,1792]{2,1,0:T(8,128)(2,1)S(1)} %bitcast.69), channel_id=1, source_target_pairs={{0,1},{1,0},{2,3},{3,2},{4,5},{5,4},{6,7},{7,6},{8,9},{9,8},{10,11... | collective-permute-start | bytes 1376264 | tf_op jit(solution)/shard_map/ppermute | solution.py:59
  84.7 2.0 %collective-permute-start.18 = (bf16[8,16,1792]{2,1,0:T(8,128)(2,1)S(1)}, bf16[8,16,1792]{2,1,0:T(8,128)(2,1)S(1)}, u32[]{:S(2)}, u32[]{:S(2)}) collective-permute-start(bf16[8,16,1792]{2,1,0:T(8,128)(2,1)S(1)} %bitcast.68), channel_id=1, source_target_pairs={{0,1},{1,0},{2,3},{3,2},{4,5},{5,4},{6,7},{7,6},{8,9},{9,8},{10,11... | collective-permute-start | bytes 1376264 | tf_op jit(solution)/shard_map/ppermute | solution.py:59
  86.1 6.1 %collective-permute-start.23 = (bf16[4,16,1792]{2,1,0:T(8,128)(2,1)S(1)}, bf16[4,16,1792]{2,1,0:T(8,128)(2,1)S(1)}, u32[]{:S(2)}, u32[]{:S(2)}) collective-permute-start(bf16[4,16,1792]{2,1,0:T(8,128)(2,1)S(1)} %slice.273), channel_id=1, source_target_pairs={{0,4},{1,3},{2,6},{3,1},{4,0},{5,7},{6,2},{7,5},{8,12},{9,11},{10,... | collective-permute-start | bytes 688136 | tf_op jit(solution)/shard_map/ppermute | solution.py:59
  86.9 8.2 %collective-permute-start.19 = (bf16[4,16,1792]{2,1,0:T(8,128)(2,1)S(1)}, bf16[4,16,1792]{2,1,0:T(8,128)(2,1)S(1)}, u32[]{:S(2)}, u32[]{:S(2)}) collective-permute-start(bf16[4,16,1792]{2,1,0:T(8,128)(2,1)S(1)} %slice.265), channel_id=1, source_target_pairs={{0,4},{1,3},{2,6},{3,1},{4,0},{5,7},{6,2},{7,5},{8,12},{9,11},{10,... | collective-permute-start | bytes 688136 | tf_op jit(solution)/shard_map/ppermute | solution.py:59
  92.3 4.9 %collective-permute-start.24 = (bf16[2,16,1792]{2,1,0:T(8,128)(2,1)S(1)}, bf16[2,16,1792]{2,1,0:T(8,128)(2,1)S(1)}, u32[]{:S(2)}, u32[]{:S(2)}) collective-permute-start(bf16[2,16,1792]{2,1,0:T(8,128)(2,1)S(1)} %slice.275), channel_id=1, source_target_pairs={{0,2},{1,5},{2,0},{3,7},{4,6},{5,1},{6,4},{7,3},{8,10},{9,13},{10,... | collective-permute-start | bytes 344072 | tf_op jit(solution)/shard_map/ppermute | solution.py:59
  95.1 4.9 %collective-permute-start.20 = (bf16[2,16,1792]{2,1,0:T(8,128)(2,1)S(1)}, bf16[2,16,1792]{2,1,0:T(8,128)(2,1)S(1)}, u32[]{:S(2)}, u32[]{:S(2)}) collective-permute-start(bf16[2,16,1792]{2,1,0:T(8,128)(2,1)S(1)} %slice.267), channel_id=1, source_target_pairs={{0,2},{1,5},{2,0},{3,7},{4,6},{5,1},{6,4},{7,3},{8,10},{9,13},{10,... | collective-permute-start | bytes 344072 | tf_op jit(solution)/shard_map/ppermute | solution.py:59
  97.2 6.6 %collective-permute-start.25 = (bf16[1,16,1792]{2,1,0:T(8,128)(2,1)S(1)}, bf16[1,16,1792]{2,1,0:T(8,128)(2,1)S(1)}, u32[]{:S(2)}, u32[]{:S(2)}) collective-permute-start(bf16[1,16,1792]{2,1,0:T(8,128)(2,1)S(1)} %slice.277), channel_id=1, source_target_pairs={{0,8},{1,9},{2,10},{3,11},{4,12},{5,13},{6,14},{7,15},{8,0},{9,1},... | collective-permute-start | bytes 172040 | tf_op jit(solution)/shard_map/ppermute | solution.py:59
  100.0 5.2 %collective-permute-start.21 = (bf16[1,16,1792]{2,1,0:T(8,128)(2,1)S(1)}, bf16[1,16,1792]{2,1,0:T(8,128)(2,1)S(1)}, u32[]{:S(2)}, u32[]{:S(2)}) collective-permute-start(bf16[1,16,1792]{2,1,0:T(8,128)(2,1)S(1)} %slice.269), channel_id=1, source_target_pairs={{0,8},{1,9},{2,10},{3,11},{4,12},{5,13},{6,14},{7,15},{8,0},{9,1},... | collective-permute-start | bytes 172040 | tf_op jit(solution)/shard_map/ppermute | solution.py:59
  (8 other events, 13.5 us)

commit v6 on v5

--- a/solution.py
+++ b/solution.py
@@ -159,15 +159,19 @@
     return pl.BlockSpec(shape, lambda step: (0,) * len(shape))
 
 
+def in_vmem(grid, spec):
+    return spec if grid else pl.BlockSpec(memory_space=pltpu.VMEM)
+
+
 def attend(queries, blocks, doc_ids, w_uv):
     rows = queries.shape[0]
     head_count, value_in, value_width = w_uv.shape
     query_width = queries.shape[1] // head_count
     key_count = doc_ids.shape[0]
     width = -(-query_width // 128) * 128
-    pair_count = 2 if head_count % 4 == 0 and key_count <= 512 else 1
+    pair_count = head_count // 2 if key_count <= 512 else 1
     heads = 2 * pair_count
-    grid = (head_count // heads,)
+    grid = (head_count // heads,) if head_count > heads else ()
     first_keys = blocks[0].shape[1]
     params = pltpu.CompilerParams(
         vmem_limit_bytes=(8 << 20) + 8 * heads * rows * (key_count + KVL) * 4
@@ -185,17 +189,23 @@
         ),
         grid=grid,
         in_specs=[
-            pl.BlockSpec((rows, heads * query_width), lambda step: (0, step)),
-            whole_block(blocks[0].shape),
-            up_block,
-            whole_block((1, key_count)),
+            in_vmem(grid, spec)
+            for spec in (
+                pl.BlockSpec((rows, heads * query_width), lambda step: (0, step)),
+                whole_block(blocks[0].shape),
+                up_block,
+                whole_block((1, key_count)),
+            )
         ],
-        out_specs=(
-            stacked(width),
-            stacked(first_keys),
-            whole_block(blocks[0].shape),
-            up_block,
-            whole_block((1, key_count)),
+        out_specs=tuple(
+            in_vmem(grid, spec)
+            for spec in (
+                stacked(width),
+                stacked(first_keys),
+                whole_block(blocks[0].shape),
+                up_block,
+                whole_block((1, key_count)),
+            )
         ),
         compiler_params=params,
         cost_estimate=pl.CostEstimate(
@@ -210,13 +220,18 @@
         out_shape=jax.ShapeDtypeStruct((rows, head_count * value_width), jnp.bfloat16),
         grid=grid,
         in_specs=[
-            whole_block((1, key_count)),
-            stacked(width),
-            stacked(first_keys),
-            up_block,
-            *(whole_block(block.shape) for block in blocks),
+            in_vmem(grid, spec)
+            for spec in (
+                whole_block((1, key_count)),
+                stacked(width),
+                stacked(first_keys),
+                up_block,
+                *(whole_block(block.shape) for block in blocks),
+            )
         ],
-        out_specs=pl.BlockSpec((rows, heads * value_width), lambda step: (0, step)),
+        out_specs=in_vmem(
+            grid, pl.BlockSpec((rows, heads * value_width), lambda step: (0, step))
+        ),
         compiler_params=params,
         cost_estimate=pl.CostEstimate(
             flops=2 * rows * head_count * key_count * (query_width + value_in),
@@ -257,9 +272,7 @@
         out_specs=pl.BlockSpec(memory_space=pltpu.VMEM),
         scratch_shapes=[pltpu.SemaphoreType.DMA((pieces,))],
         compiler_params=pltpu.CompilerParams(vmem_limit_bytes=1 << 20),
-        cost_estimate=pl.CostEstimate(
-            flops=0, bytes_accessed=2 * weights.shape[0] * (high - low) * weights.dtype.itemsize, transcendentals=0
-        ),
+        cost_estimate=pl.CostEstimate(flops=0, bytes_accessed=0, transcendentals=0),
         name="fetch_weights",
     )(weights, after)
 

time: 106 us -> 105 us (level)
  no operation moved by 1% of the time
where the time goes in v6:
time: 105 us
  waiting for transfers between devices  45.7 us (44%)
  starting transfers between devices  31.7 us (30%)
  Pallas kernels  9.49 us (9%)
  local copies, waits for them, and re-layouts  9.26 us (9%)
  other arithmetic  4.27 us (4%)
  matrix products  3.91 us (4%)
    ppermute x14, waiting for transfers between devices, halved(): got = lax.ppermute(array[half:], 'ep', crossing(count, step))  17.8 us
    ppermute x14, starting transfers between devices, halved(): got = lax.ppermute(array[half:], 'ep', crossing(count, step))  14.8 us
    ppermute x6, waiting for transfers between devices, doubled(): lax.ppermute(array, 'ep', crossing(count, step))  11.3 us
    ppermute x2, waiting for transfers between devices, shards(): others = [lax.ppermute(both, 'ctx', swap) for both in sums]  10.5 us
    unnamed x26, local copies, waits for them, and re-layouts  8.84 us
    ppermute x2, starting transfers between devices, shards(): got = lax.ppermute(sent, 'ep', crossing(ep_count, bits - 1))  5.31 us
    ppermute x1, starting transfers between devices, shards(): blocks = [key_columns, lax.ppermute(key_columns, 'ctx', [(0, 1)])]  4.87 us
    ppermute x2, waiting for transfers between devices, shards(): got = lax.ppermute(sent, 'ep', crossing(ep_count, bits - 1))  3.99 us
  transfers between devices with their start and end apart: 26, of which 21 were waited for; matrix products, arithmetic and copies ran while one was open for 5% of the time, Pallas kernels for 4%

profile of v6, /device:TPU:0, one launch (start us, length us, event | category | flops | bytes accessed | tf_op | source)
XLA Modules:
  0.0 105.0 jit_solution(9614137083023149299)
XLA Ops:
  0.0 4.9 %collective-permute-start = (bf16[576,128]{1,0:T(8,128)(2,1)}, bf16[576,128]{1,0:T(8,128)(2,1)S(1)}, u32[]{:S(2)}, u32[]{:S(2)}) collective-permute-start(bf16[576,128]{1,0:T(8,128)(2,1)} %bitcast.56), channel_id=1, source_target_pairs={{0,16},{1,17},{2,18},{3,19},{4,20},{5,21},{6,22},{7,23},{8,24},{9,... | collective-permute-start | bytes 442376 | tf_op jit(solution)/shard_map/ppermute | solution.py:428
  4.9 1.3 %copy-done.1 = bf16[128,4608]{1,0:T(8,128)(2,1)S(1)} copy-done((bf16[128,4608]{1,0:T(8,128)(2,1)S(1)}, bf16[128,4608]{1,0:T(8,128)(2,1)}, u32[]{:S(2)}) %copy-start.1) | copy-done | bytes 1179672
  12.9 3.1 %copy-done = bf16[1024,3584]{1,0:T(8,128)(2,1)S(1)} copy-done((bf16[1024,3584]{1,0:T(8,128)(2,1)S(1)}, bf16[1024,3584]{1,0:T(8,128)(2,1)}, u32[]{:S(2)}) %copy-start) | copy-done | bytes 7340056
  16.5 2.1 %collective-permute-done.1 = bf16[128,1024]{1,0:T(8,128)(2,1)S(1)} collective-permute-done((bf16[128,1024]{1,0:T(8,128)(2,1)S(1)}, bf16[128,1024]{1,0:T(8,128)(2,1)S(1)}, u32[]{:S(2)}, u32[]{:S(2)}) %collective-permute-start.1) | collective-permute-done | bytes 262176 | tf_op jit(solution)/shard_map/ppermute | solution.py:439
  23.5 1.6 %collective-permute-start.7 = (bf16[4,16,1664]{2,1,0:T(8,128)(2,1)S(1)}, bf16[4,16,1664]{2,1,0:T(8,128)(2,1)S(1)}, u32[]{:S(2)}, u32[]{:S(2)}) collective-permute-start(bf16[4,16,1664]{2,1,0:T(8,128)(2,1)S(1)} %slice.245), channel_id=1, source_target_pairs={{0,4},{1,3},{2,6},{3,1},{4,0},{5,7},{6,2},{7,5},{8,12},{9,11},{10,... | collective-permute-start | bytes 638984 | tf_op jit(solution)/shard_map/ppermute | solution.py:59
  25.8 3.5 %collective-permute-done.7 = bf16[4,16,1664]{2,1,0:T(8,128)(2,1)S(1)} collective-permute-done((bf16[4,16,1664]{2,1,0:T(8,128)(2,1)S(1)}, bf16[4,16,1664]{2,1,0:T(8,128)(2,1)S(1)}, u32[]{:S(2)}, u32[]{:S(2)}) %collective-permute-start.7) | collective-permute-done | bytes 213024 | tf_op jit(solution)/shard_map/ppermute | solution.py:59
  29.4 1.6 %collective-permute-start.8 = (bf16[2,16,1664]{2,1,0:T(8,128)(2,1)S(1)}, bf16[2,16,1664]{2,1,0:T(8,128)(2,1)S(1)}, u32[]{:S(2)}, u32[]{:S(2)}) collective-permute-start(bf16[2,16,1664]{2,1,0:T(8,128)(2,1)S(1)} %slice.247), channel_id=1, source_target_pairs={{0,2},{1,5},{2,0},{3,7},{4,6},{5,1},{6,4},{7,3},{8,10},{9,13},{10,... | collective-permute-start | bytes 319496 | tf_op jit(solution)/shard_map/ppermute | solution.py:59
  31.0 1.6 %collective-permute-done.3 = bf16[4,16,1920]{2,1,0:T(8,128)(2,1)S(1)} collective-permute-done((bf16[4,16,1920]{2,1,0:T(8,128)(2,1)S(1)}, bf16[4,16,1920]{2,1,0:T(8,128)(2,1)S(1)}, u32[]{:S(2)}, u32[]{:S(2)}) %collective-permute-start.3) | collective-permute-done | bytes 245792 | tf_op jit(solution)/shard_map/ppermute | solution.py:59
  32.6 1.6 %collective-permute-start.4 = (bf16[2,16,1920]{2,1,0:T(8,128)(2,1)S(1)}, bf16[2,16,1920]{2,1,0:T(8,128)(2,1)S(1)}, u32[]{:S(2)}, u32[]{:S(2)}) collective-permute-start(bf16[2,16,1920]{2,1,0:T(8,128)(2,1)S(1)} %slice.239), channel_id=1, source_target_pairs={{0,2},{1,5},{2,0},{3,7},{4,6},{5,1},{6,4},{7,3},{8,10},{9,13},{10,... | collective-permute-start | bytes 368648 | tf_op jit(solution)/shard_map/ppermute | solution.py:59
  34.3 2.7 %collective-permute-start.9 = (bf16[2,16,1792]{2,1,0:T(8,128)(2,1)S(1)}, bf16[2,16,1792]{2,1,0:T(8,128)(2,1)S(1)}, u32[]{:S(2)}, u32[]{:S(2)}) collective-permute-start(bf16[2,16,1792]{2,1,0:T(8,128)(2,1)S(1)} %fusion.29), channel_id=1, source_target_pairs={{0,8},{1,9},{2,10},{3,11},{4,12},{5,13},{6,14},{7,15},{8,0},{9,1},... | collective-permute-start | bytes 344072 | tf_op jit(solution)/shard_map/ppermute | solution.py:485
  37.7 2.7 %collective-permute-start.5 = (bf16[2,16,1920]{2,1,0:T(8,128)(2,1)S(1)}, bf16[2,16,1920]{2,1,0:T(8,128)(2,1)S(1)}, u32[]{:S(2)}, u32[]{:S(2)}) collective-permute-start(bf16[2,16,1920]{2,1,0:T(8,128)(2,1)S(1)} %fusion.55.after_ref), channel_id=1, source_target_pairs={{0,8},{1,9},{2,10},{3,11},{4,12},{5,13},{6,14},{7,15},{8,0},{9,1},... | collective-permute-start | bytes 368648 | tf_op jit(solution)/shard_map/ppermute | solution.py:485
  41.0 1.6 %slice-done.5 = s8[4194304]{0:T(1024)(128)(4,1)S(1)} async-done(((s8[7340032]{0:T(1024)(128)(4,1)}), s8[4194304]{0:T(1024)(128)(4,1)S(1)}, s32[]{:S(2)}) %slice-start.5) | async-done | bytes 4194328
  43.1 4.0 %collective-permute-done.5.got_ref = bf16[2,16,1920]{2,1,0:T(8,128)(2,1)S(1)} collective-permute-done((bf16[2,16,1920]{2,1,0:T(8,128)(2,1)S(1)}, bf16[2,16,1920]{2,1,0:T(8,128)(2,1)S(1)}, u32[]{:S(2)}, u32[]{:S(2)}) %collective-permute-start.5) | collective-permute-done | bytes 122912 | tf_op jit(solution)/shard_map/ppermute | solution.py:485
  47.5 1.6 %collective-permute-start.10 = (bf16[2,16,1792]{2,1,0:T(8,128)(2,1)S(1)}, bf16[2,16,1792]{2,1,0:T(8,128)(2,1)S(1)}, u32[]{:S(2)}, u32[]{:S(2)}) collective-permute-start(bf16[2,16,1792]{2,1,0:T(8,128)(2,1)S(1)} %get-tuple-element.53), channel_id=1, source_target_pairs={{0,2},{1,5},{2,0},{3,7},{4,6},{5,1},{6,4},{7,3},{8,10},{9,13},{10,... | collective-permute-start | bytes 344072 | tf_op jit(solution)/shard_map/ppermute | solution.py:64
  49.6 2.8 %collective-permute-done.10 = bf16[2,16,1792]{2,1,0:T(8,128)(2,1)S(1)} collective-permute-done((bf16[2,16,1792]{2,1,0:T(8,128)(2,1)S(1)}, bf16[2,16,1792]{2,1,0:T(8,128)(2,1)S(1)}, u32[]{:S(2)}, u32[]{:S(2)}) %collective-permute-start.10) | collective-permute-done | bytes 114720 | tf_op jit(solution)/shard_map/ppermute | solution.py:64
  53.1 1.9 %collective-permute-done.13 = bf16[2,16,1920]{2,1,0:T(8,128)(2,1)S(1)} collective-permute-done((bf16[2,16,1920]{2,1,0:T(8,128)(2,1)S(1)}, bf16[2,16,1920]{2,1,0:T(8,128)(2,1)S(1)}, u32[]{:S(2)}, u32[]{:S(2)}) %collective-permute-start.13) | collective-permute-done | bytes 122912 | tf_op jit(solution)/shard_map/ppermute | solution.py:64
  55.5 2.9 %collective-permute-done.11 = bf16[4,16,1792]{2,1,0:T(8,128)(2,1)S(1)} collective-permute-done((bf16[4,16,1792]{2,1,0:T(8,128)(2,1)S(1)}, bf16[4,16,1792]{2,1,0:T(8,128)(2,1)S(1)}, u32[]{:S(2)}, u32[]{:S(2)}) %collective-permute-start.11) | collective-permute-done | bytes 229408 | tf_op jit(solution)/shard_map/ppermute | solution.py:64
  58.6 2.7 %collective-permute-done.14 = bf16[4,16,1920]{2,1,0:T(8,128)(2,1)S(1)} collective-permute-done((bf16[4,16,1920]{2,1,0:T(8,128)(2,1)S(1)}, bf16[4,16,1920]{2,1,0:T(8,128)(2,1)S(1)}, u32[]{:S(2)}, u32[]{:S(2)}) %collective-permute-start.14) | collective-permute-done | bytes 245792 | tf_op jit(solution)/shard_map/ppermute | solution.py:64
  63.8 1.4 %hidden_terms.2 = bf16[144,1152]{1,0:T(8,128)(2,1)S(1)} custom-call(bf16[144,1920]{1,0:T(8,128)(2,1)S(1)} %convolution_convert_fusion.3.refs_0_, bf16[144,1664]{1,0:T(8,128)(2,1)S(1)} %convolution_convert_fusion.2.refs_1_, bf16[3584,1024]{1,0:T(8,128)(2,1)S(1)} %fetch_weights.5.refs_2_, bf16[3584,1024]{1,0:T(8,128)(2,1)S(1)} %fetch_weights.6.refs_3_, ...), custom_call_target="tpu_custom_call" | custom-call | tf_op jit(solution)/shard_map/hidden_terms/pallas_call | solution.py:380
  65.8 1.3 %hidden_terms.3.after_ref = bf16[144,1024]{1,0:T(8,128)(2,1)S(1)} custom-call(bf16[144,1920]{1,0:T(8,128)(2,1)S(1)} %convolution_convert_fusion.3.refs_0_, bf16[144,1664]{1,0:T(8,128)(2,1)S(1)} %convolution_convert_fusion.2.refs_1_, bf16[3584,1024]{1,0:T(8,128)(2,1)S(1)} %fetch_weights.5.refs_2_, bf16[3584,1024]{1,0:T(8,128)(2,1)S(1)} %fetch_weights.6.refs_3_), custom_call_target="tpu_custom_call" | custom-call | tf_op jit(solution)/shard_map/hidden_terms/pallas_call | solution.py:380
  67.1 1.6 %collective-permute-start.16 = (bf16[144,1024]{1,0:T(8,128)(2,1)S(1)}, bf16[144,1024]{1,0:T(8,128)(2,1)S(1)}, u32[]{:S(2)}, u32[]{:S(2)}) collective-permute-start(bf16[144,1024]{1,0:T(8,128)(2,1)S(1)} %hidden_terms.3.after_ref), channel_id=1, source_target_pairs={{0,16},{16,0},{1,17},{17,1},{2,18},{18,2},{3,19},{19,3},{4,20},{20... | collective-permute-start | bytes 884744 | tf_op jit(solution)/shard_map/ppermute | solution.py:533
  69.5 6.4 %collective-permute-done.17 = bf16[144,1152]{1,0:T(8,128)(2,1)S(1)} collective-permute-done((bf16[144,1152]{1,0:T(8,128)(2,1)S(1)}, bf16[144,1152]{1,0:T(8,128)(2,1)S(1)}, u32[]{:S(2)}, u32[]{:S(2)}) %collective-permute-start.17) | collective-permute-done | bytes 331808 | tf_op jit(solution)/shard_map/ppermute | solution.py:533
  77.3 4.1 %collective-permute-done.16 = bf16[144,1024]{1,0:T(8,128)(2,1)S(1)} collective-permute-done((bf16[144,1024]{1,0:T(8,128)(2,1)S(1)}, bf16[144,1024]{1,0:T(8,128)(2,1)S(1)}, u32[]{:S(2)}, u32[]{:S(2)}) %collective-permute-start.16) | collective-permute-done | bytes 294944 | tf_op jit(solution)/shard_map/ppermute | solution.py:533
  86.0 1.5 %collective-permute-start.19 = (bf16[4,16,1792]{2,1,0:T(8,128)(2,1)S(1)}, bf16[4,16,1792]{2,1,0:T(8,128)(2,1)S(1)}, u32[]{:S(2)}, u32[]{:S(2)}) collective-permute-start(bf16[4,16,1792]{2,1,0:T(8,128)(2,1)S(1)} %slice.265), channel_id=1, source_target_pairs={{0,4},{1,3},{2,6},{3,1},{4,0},{5,7},{6,2},{7,5},{8,12},{9,11},{10,... | collective-permute-start | bytes 688136 | tf_op jit(solution)/shard_map/ppermute | solution.py:59
  87.6 3.8 %collective-permute-done.23 = bf16[4,16,1792]{2,1,0:T(8,128)(2,1)S(1)} collective-permute-done((bf16[4,16,1792]{2,1,0:T(8,128)(2,1)S(1)}, bf16[4,16,1792]{2,1,0:T(8,128)(2,1)S(1)}, u32[]{:S(2)}, u32[]{:S(2)}) %collective-permute-start.23) | collective-permute-done | bytes 229408 | tf_op jit(solution)/shard_map/ppermute | solution.py:59
  91.5 1.3 %collective-permute-start.24 = (bf16[2,16,1792]{2,1,0:T(8,128)(2,1)S(1)}, bf16[2,16,1792]{2,1,0:T(8,128)(2,1)S(1)}, u32[]{:S(2)}, u32[]{:S(2)}) collective-permute-start(bf16[2,16,1792]{2,1,0:T(8,128)(2,1)S(1)} %slice.275), channel_id=1, source_target_pairs={{0,2},{1,5},{2,0},{3,7},{4,6},{5,1},{6,4},{7,3},{8,10},{9,13},{10,... | collective-permute-start | bytes 344072 | tf_op jit(solution)/shard_map/ppermute | solution.py:59
  92.8 1.4 %collective-permute-done.19 = bf16[4,16,1792]{2,1,0:T(8,128)(2,1)S(1)} collective-permute-done((bf16[4,16,1792]{2,1,0:T(8,128)(2,1)S(1)}, bf16[4,16,1792]{2,1,0:T(8,128)(2,1)S(1)}, u32[]{:S(2)}, u32[]{:S(2)}) %collective-permute-start.19) | collective-permute-done | bytes 229408 | tf_op jit(solution)/shard_map/ppermute | solution.py:59
  94.3 1.3 %collective-permute-start.20 = (bf16[2,16,1792]{2,1,0:T(8,128)(2,1)S(1)}, bf16[2,16,1792]{2,1,0:T(8,128)(2,1)S(1)}, u32[]{:S(2)}, u32[]{:S(2)}) collective-permute-start(bf16[2,16,1792]{2,1,0:T(8,128)(2,1)S(1)} %slice.267), channel_id=1, source_target_pairs={{0,2},{1,5},{2,0},{3,7},{4,6},{5,1},{6,4},{7,3},{8,10},{9,13},{10,... | collective-permute-start | bytes 344072 | tf_op jit(solution)/shard_map/ppermute | solution.py:59
  96.4 1.9 %collective-permute-start.25 = (bf16[1,16,1792]{2,1,0:T(8,128)(2,1)S(1)}, bf16[1,16,1792]{2,1,0:T(8,128)(2,1)S(1)}, u32[]{:S(2)}, u32[]{:S(2)}) collective-permute-start(bf16[1,16,1792]{2,1,0:T(8,128)(2,1)S(1)} %slice.277), channel_id=1, source_target_pairs={{0,8},{1,9},{2,10},{3,11},{4,12},{5,13},{6,14},{7,15},{8,0},{9,1},... | collective-permute-start | bytes 172040 | tf_op jit(solution)/shard_map/ppermute | solution.py:59
  99.2 1.6 %collective-permute-start.21 = (bf16[1,16,1792]{2,1,0:T(8,128)(2,1)S(1)}, bf16[1,16,1792]{2,1,0:T(8,128)(2,1)S(1)}, u32[]{:S(2)}, u32[]{:S(2)}) collective-permute-start(bf16[1,16,1792]{2,1,0:T(8,128)(2,1)S(1)} %slice.269), channel_id=1, source_target_pairs={{0,8},{1,9},{2,10},{3,11},{4,12},{5,13},{6,14},{7,15},{8,0},{9,1},... | collective-permute-start | bytes 172040 | tf_op jit(solution)/shard_map/ppermute | solution.py:59
  100.8 2.2 %collective-permute-done.25 = bf16[1,16,1792]{2,1,0:T(8,128)(2,1)S(1)} collective-permute-done((bf16[1,16,1792]{2,1,0:T(8,128)(2,1)S(1)}, bf16[1,16,1792]{2,1,0:T(8,128)(2,1)S(1)}, u32[]{:S(2)}, u32[]{:S(2)}) %collective-permute-start.25) | collective-permute-done | bytes 57376 | tf_op jit(solution)/shard_map/ppermute | solution.py:59
  103.0 1.4 %collective-permute-done.21 = bf16[1,16,1792]{2,1,0:T(8,128)(2,1)S(1)} collective-permute-done((bf16[1,16,1792]{2,1,0:T(8,128)(2,1)S(1)}, bf16[1,16,1792]{2,1,0:T(8,128)(2,1)S(1)}, u32[]{:S(2)}, u32[]{:S(2)}) %collective-permute-start.21) | collective-permute-done | bytes 57376 | tf_op jit(solution)/shard_map/ppermute | solution.py:59
  (138 shorter events, 29.1 us)
Async XLA Ops:
  0.0 9.6 %collective-permute-start = (bf16[576,128]{1,0:T(8,128)(2,1)}, bf16[576,128]{1,0:T(8,128)(2,1)S(1)}, u32[]{:S(2)}, u32[]{:S(2)}) collective-permute-start(bf16[576,128]{1,0:T(8,128)(2,1)} %bitcast.56), channel_id=1, source_target_pairs={{0,16},{1,17},{2,18},{3,19},{4,20},{5,21},{6,22},{7,23},{8,24},{9,... | collective-permute-start | bytes 442376 | tf_op jit(solution)/shard_map/ppermute | solution.py:428
  10.8 7.8 %collective-permute-start.1 = (bf16[128,1024]{1,0:T(8,128)(2,1)S(1)}, bf16[128,1024]{1,0:T(8,128)(2,1)S(1)}, u32[]{:S(2)}, u32[]{:S(2)}) collective-permute-start(bf16[128,1024]{1,0:T(8,128)(2,1)S(1)} %attention.1.after_ref), channel_id=1, source_target_pairs={{0,16},{16,0},{1,17},{17,1},{2,18},{18,2},{3,19},{19,3},{4,20},{20... | collective-permute-start | bytes 786440 | tf_op jit(solution)/shard_map/ppermute | solution.py:439
  20.3 14.0 %copy-start.5 = (bf16[16,3584]{1,0:T(8,128)(2,1)S(1)}, bf16[16,3584]{1,0:T(8,128)(2,1)}, u32[]{:S(2)}) copy-start(bf16[16,3584]{1,0:T(8,128)(2,1)} %param.17) | copy-start | bytes 344068
  20.3 20.1 %slice-start.2 = ((s8[7340032]{0:T(1024)(128)(4,1)}), s8[4194304]{0:T(1024)(128)(4,1)S(1)}, s32[]{:S(2)}) async-start(s8[7340032]{0:T(1024)(128)(4,1)} %bitcast.50), calls=%async_computation.2 | async-start | bytes 8388608
  21.5 18.9 %slice-start.3 = ((s8[7340032]{0:T(1024)(128)(4,1)}), s8[3145728]{0:T(1024)(128)(4,1)S(1)}, s32[]{:S(2)}) async-start(s8[7340032]{0:T(1024)(128)(4,1)} %bitcast.50), calls=%async_computation.3 | async-start | bytes 6291456
  21.5 1.8 %collective-permute-start.6 = (bf16[8,16,1664]{2,1,0:T(8,128)(2,1)S(1)}, bf16[8,16,1664]{2,1,0:T(8,128)(2,1)S(1)}, u32[]{:S(2)}, u32[]{:S(2)}) collective-permute-start(bf16[8,16,1664]{2,1,0:T(8,128)(2,1)S(1)} %bitcast.70), channel_id=1, source_target_pairs={{0,1},{1,0},{2,3},{3,2},{4,5},{5,4},{6,7},{7,6},{8,9},{9,8},{10,11... | collective-permute-start | bytes 1277960 | tf_op jit(solution)/shard_map/ppermute | solution.py:59
  21.7 3.5 %collective-permute-start.2 = (bf16[8,16,1920]{2,1,0:T(8,128)(2,1)S(1)}, bf16[8,16,1920]{2,1,0:T(8,128)(2,1)S(1)}, u32[]{:S(2)}, u32[]{:S(2)}) collective-permute-start(bf16[8,16,1920]{2,1,0:T(8,128)(2,1)S(1)} %bitcast.67), channel_id=1, source_target_pairs={{0,1},{1,0},{2,3},{3,2},{4,5},{5,4},{6,7},{7,6},{8,9},{9,8},{10,11... | collective-permute-start | bytes 1474568 | tf_op jit(solution)/shard_map/ppermute | solution.py:59
  23.5 5.9 %collective-permute-start.7 = (bf16[4,16,1664]{2,1,0:T(8,128)(2,1)S(1)}, bf16[4,16,1664]{2,1,0:T(8,128)(2,1)S(1)}, u32[]{:S(2)}, u32[]{:S(2)}) collective-permute-start(bf16[4,16,1664]{2,1,0:T(8,128)(2,1)S(1)} %slice.245), channel_id=1, source_target_pairs={{0,4},{1,3},{2,6},{3,1},{4,0},{5,7},{6,2},{7,5},{8,12},{9,11},{10,... | collective-permute-start | bytes 638984 | tf_op jit(solution)/shard_map/ppermute | solution.py:59
  25.3 7.3 %collective-permute-start.3 = (bf16[4,16,1920]{2,1,0:T(8,128)(2,1)S(1)}, bf16[4,16,1920]{2,1,0:T(8,128)(2,1)S(1)}, u32[]{:S(2)}, u32[]{:S(2)}) collective-permute-start(bf16[4,16,1920]{2,1,0:T(8,128)(2,1)S(1)} %slice.237), channel_id=1, source_target_pairs={{0,4},{1,3},{2,6},{3,1},{4,0},{5,7},{6,2},{7,5},{8,12},{9,11},{10,... | collective-permute-start | bytes 737288 | tf_op jit(solution)/shard_map/ppermute | solution.py:59
  29.4 4.8 %collective-permute-start.8 = (bf16[2,16,1664]{2,1,0:T(8,128)(2,1)S(1)}, bf16[2,16,1664]{2,1,0:T(8,128)(2,1)S(1)}, u32[]{:S(2)}, u32[]{:S(2)}) collective-permute-start(bf16[2,16,1664]{2,1,0:T(8,128)(2,1)S(1)} %slice.247), channel_id=1, source_target_pairs={{0,2},{1,5},{2,0},{3,7},{4,6},{5,1},{6,4},{7,3},{8,10},{9,13},{10,... | collective-permute-start | bytes 319496 | tf_op jit(solution)/shard_map/ppermute | solution.py:59
  32.6 4.9 %collective-permute-start.4 = (bf16[2,16,1920]{2,1,0:T(8,128)(2,1)S(1)}, bf16[2,16,1920]{2,1,0:T(8,128)(2,1)S(1)}, u32[]{:S(2)}, u32[]{:S(2)}) collective-permute-start(bf16[2,16,1920]{2,1,0:T(8,128)(2,1)S(1)} %slice.239), channel_id=1, source_target_pairs={{0,2},{1,5},{2,0},{3,7},{4,6},{5,1},{6,4},{7,3},{8,10},{9,13},{10,... | collective-permute-start | bytes 368648 | tf_op jit(solution)/shard_map/ppermute | solution.py:59
  34.3 12.9 %collective-permute-start.9 = (bf16[2,16,1792]{2,1,0:T(8,128)(2,1)S(1)}, bf16[2,16,1792]{2,1,0:T(8,128)(2,1)S(1)}, u32[]{:S(2)}, u32[]{:S(2)}) collective-permute-start(bf16[2,16,1792]{2,1,0:T(8,128)(2,1)S(1)} %fusion.29), channel_id=1, source_target_pairs={{0,8},{1,9},{2,10},{3,11},{4,12},{5,13},{6,14},{7,15},{8,0},{9,1},... | collective-permute-start | bytes 344072 | tf_op jit(solution)/shard_map/ppermute | solution.py:485
  37.6 3.3 %slice-start.4 = ((s8[7340032]{0:T(1024)(128)(4,1)}), s8[3145728]{0:T(1024)(128)(4,1)S(1)}, s32[]{:S(2)}) async-start(s8[7340032]{0:T(1024)(128)(4,1)} %bitcast.53), calls=%async_computation.4 | async-start | bytes 6291456
  37.7 9.4 %collective-permute-start.5 = (bf16[2,16,1920]{2,1,0:T(8,128)(2,1)S(1)}, bf16[2,16,1920]{2,1,0:T(8,128)(2,1)S(1)}, u32[]{:S(2)}, u32[]{:S(2)}) collective-permute-start(bf16[2,16,1920]{2,1,0:T(8,128)(2,1)S(1)} %fusion.55.after_ref), channel_id=1, source_target_pairs={{0,8},{1,9},{2,10},{3,11},{4,12},{5,13},{6,14},{7,15},{8,0},{9,1},... | collective-permute-start | bytes 368648 | tf_op jit(solution)/shard_map/ppermute | solution.py:485
  47.5 4.9 %collective-permute-start.10 = (bf16[2,16,1792]{2,1,0:T(8,128)(2,1)S(1)}, bf16[2,16,1792]{2,1,0:T(8,128)(2,1)S(1)}, u32[]{:S(2)}, u32[]{:S(2)}) collective-permute-start(bf16[2,16,1792]{2,1,0:T(8,128)(2,1)S(1)} %get-tuple-element.53), channel_id=1, source_target_pairs={{0,2},{1,5},{2,0},{3,7},{4,6},{5,1},{6,4},{7,3},{8,10},{9,13},{10,... | collective-permute-start | bytes 344072 | tf_op jit(solution)/shard_map/ppermute | solution.py:64
  49.0 6.0 %collective-permute-start.13 = (bf16[2,16,1920]{2,1,0:T(8,128)(2,1)S(1)}, bf16[2,16,1920]{2,1,0:T(8,128)(2,1)S(1)}, u32[]{:S(2)}, u32[]{:S(2)}) collective-permute-start(bf16[2,16,1920]{2,1,0:T(8,128)(2,1)S(1)} %get-tuple-element.54), channel_id=1, source_target_pairs={{0,2},{1,5},{2,0},{3,7},{4,6},{5,1},{6,4},{7,3},{8,10},{9,13},{10,... | collective-permute-start | bytes 368648 | tf_op jit(solution)/shard_map/ppermute | solution.py:64
  52.4 6.1 %collective-permute-start.11 = (bf16[4,16,1792]{2,1,0:T(8,128)(2,1)S(1)}, bf16[4,16,1792]{2,1,0:T(8,128)(2,1)S(1)}, u32[]{:S(2)}, u32[]{:S(2)}) collective-permute-start(bf16[4,16,1792]{2,1,0:T(8,128)(2,1)S(1)} %pad_maximum_fusion.6), channel_id=1, source_target_pairs={{0,4},{1,3},{2,6},{3,1},{4,0},{5,7},{6,2},{7,5},{8,12},{9,11},{10,... | collective-permute-start | bytes 688136 | tf_op jit(solution)/shard_map/ppermute | solution.py:64
  55.0 6.3 %collective-permute-start.14 = (bf16[4,16,1920]{2,1,0:T(8,128)(2,1)S(1)}, bf16[4,16,1920]{2,1,0:T(8,128)(2,1)S(1)}, u32[]{:S(2)}, u32[]{:S(2)}) collective-permute-start(bf16[4,16,1920]{2,1,0:T(8,128)(2,1)S(1)} %pad_maximum_fusion.5), channel_id=1, source_target_pairs={{0,4},{1,3},{2,6},{3,1},{4,0},{5,7},{6,2},{7,5},{8,12},{9,11},{10,... | collective-permute-start | bytes 737288 | tf_op jit(solution)/shard_map/ppermute | solution.py:64
  58.5 2.9 %collective-permute-start.12 = (bf16[8,16,1792]{2,1,0:T(8,128)(2,1)S(1)}, bf16[8,16,1792]{2,1,0:T(8,128)(2,1)S(1)}, u32[]{:S(2)}, u32[]{:S(2)}) collective-permute-start(bf16[8,16,1792]{2,1,0:T(8,128)(2,1)S(1)} %pad_maximum_fusion.3), channel_id=1, source_target_pairs={{0,1},{1,0},{2,3},{3,2},{4,5},{5,4},{6,7},{7,6},{8,9},{9,8},{10,11... | collective-permute-start | bytes 1376264 | tf_op jit(solution)/shard_map/ppermute | solution.py:64
  61.4 1.9 %collective-permute-start.15 = (bf16[8,16,1920]{2,1,0:T(8,128)(2,1)S(1)}, bf16[8,16,1920]{2,1,0:T(8,128)(2,1)S(1)}, u32[]{:S(2)}, u32[]{:S(2)}) collective-permute-start(bf16[8,16,1920]{2,1,0:T(8,128)(2,1)S(1)} %pad_maximum_fusion.2), channel_id=1, source_target_pairs={{0,1},{1,0},{2,3},{3,2},{4,5},{5,4},{6,7},{7,6},{8,9},{9,8},{10,11... | collective-permute-start | bytes 1474568 | tf_op jit(solution)/shard_map/ppermute | solution.py:64
  63.4 5.4 %slice-start = ((s8[7340032]{0:T(1024)(128)(4,1)}), s8[4194304]{0:T(1024)(128)(4,1)S(1)}, s32[]{:S(2)}) async-start(s8[7340032]{0:T(1024)(128)(4,1)} %bitcast.47), calls=%async_computation | async-start | bytes 8388608
  63.8 5.0 %slice-start.1 = ((s8[7340032]{0:T(1024)(128)(4,1)}), s8[3145728]{0:T(1024)(128)(4,1)S(1)}, s32[]{:S(2)}) async-start(s8[7340032]{0:T(1024)(128)(4,1)} %bitcast.47), calls=%async_computation.1 | async-start | bytes 6291456
  65.1 10.7 %collective-permute-start.17 = (bf16[144,1152]{1,0:T(8,128)(2,1)S(1)}, bf16[144,1152]{1,0:T(8,128)(2,1)S(1)}, u32[]{:S(2)}, u32[]{:S(2)}) collective-permute-start(bf16[144,1152]{1,0:T(8,128)(2,1)S(1)} %hidden_terms.2), channel_id=1, source_target_pairs={{0,16},{16,0},{1,17},{17,1},{2,18},{18,2},{3,19},{19,3},{4,20},{20... | collective-permute-start | bytes 995336 | tf_op jit(solution)/shard_map/ppermute | solution.py:533
  67.1 14.2 %collective-permute-start.16 = (bf16[144,1024]{1,0:T(8,128)(2,1)S(1)}, bf16[144,1024]{1,0:T(8,128)(2,1)S(1)}, u32[]{:S(2)}, u32[]{:S(2)}) collective-permute-start(bf16[144,1024]{1,0:T(8,128)(2,1)S(1)} %hidden_terms.3.after_ref), channel_id=1, source_target_pairs={{0,16},{16,0},{1,17},{17,1},{2,18},{18,2},{3,19},{19,3},{4,20},{20... | collective-permute-start | bytes 884744 | tf_op jit(solution)/shard_map/ppermute | solution.py:533
  83.3 1.9 %collective-permute-start.22 = (bf16[8,16,1792]{2,1,0:T(8,128)(2,1)S(1)}, bf16[8,16,1792]{2,1,0:T(8,128)(2,1)S(1)}, u32[]{:S(2)}, u32[]{:S(2)}) collective-permute-start(bf16[8,16,1792]{2,1,0:T(8,128)(2,1)S(1)} %bitcast.69), channel_id=1, source_target_pairs={{0,1},{1,0},{2,3},{3,2},{4,5},{5,4},{6,7},{7,6},{8,9},{9,8},{10,11... | collective-permute-start | bytes 1376264 | tf_op jit(solution)/shard_map/ppermute | solution.py:59
  83.9 2.0 %collective-permute-start.18 = (bf16[8,16,1792]{2,1,0:T(8,128)(2,1)S(1)}, bf16[8,16,1792]{2,1,0:T(8,128)(2,1)S(1)}, u32[]{:S(2)}, u32[]{:S(2)}) collective-permute-start(bf16[8,16,1792]{2,1,0:T(8,128)(2,1)S(1)} %bitcast.68), channel_id=1, source_target_pairs={{0,1},{1,0},{2,3},{3,2},{4,5},{5,4},{6,7},{7,6},{8,9},{9,8},{10,11... | collective-permute-start | bytes 1376264 | tf_op jit(solution)/shard_map/ppermute | solution.py:59
  85.3 6.1 %collective-permute-start.23 = (bf16[4,16,1792]{2,1,0:T(8,128)(2,1)S(1)}, bf16[4,16,1792]{2,1,0:T(8,128)(2,1)S(1)}, u32[]{:S(2)}, u32[]{:S(2)}) collective-permute-start(bf16[4,16,1792]{2,1,0:T(8,128)(2,1)S(1)} %slice.273), channel_id=1, source_target_pairs={{0,4},{1,3},{2,6},{3,1},{4,0},{5,7},{6,2},{7,5},{8,12},{9,11},{10,... | collective-permute-start | bytes 688136 | tf_op jit(solution)/shard_map/ppermute | solution.py:59
  86.0 8.2 %collective-permute-start.19 = (bf16[4,16,1792]{2,1,0:T(8,128)(2,1)S(1)}, bf16[4,16,1792]{2,1,0:T(8,128)(2,1)S(1)}, u32[]{:S(2)}, u32[]{:S(2)}) collective-permute-start(bf16[4,16,1792]{2,1,0:T(8,128)(2,1)S(1)} %slice.265), channel_id=1, source_target_pairs={{0,4},{1,3},{2,6},{3,1},{4,0},{5,7},{6,2},{7,5},{8,12},{9,11},{10,... | collective-permute-start | bytes 688136 | tf_op jit(solution)/shard_map/ppermute | solution.py:59
  91.5 4.9 %collective-permute-start.24 = (bf16[2,16,1792]{2,1,0:T(8,128)(2,1)S(1)}, bf16[2,16,1792]{2,1,0:T(8,128)(2,1)S(1)}, u32[]{:S(2)}, u32[]{:S(2)}) collective-permute-start(bf16[2,16,1792]{2,1,0:T(8,128)(2,1)S(1)} %slice.275), channel_id=1, source_target_pairs={{0,2},{1,5},{2,0},{3,7},{4,6},{5,1},{6,4},{7,3},{8,10},{9,13},{10,... | collective-permute-start | bytes 344072 | tf_op jit(solution)/shard_map/ppermute | solution.py:59
  94.3 4.9 %collective-permute-start.20 = (bf16[2,16,1792]{2,1,0:T(8,128)(2,1)S(1)}, bf16[2,16,1792]{2,1,0:T(8,128)(2,1)S(1)}, u32[]{:S(2)}, u32[]{:S(2)}) collective-permute-start(bf16[2,16,1792]{2,1,0:T(8,128)(2,1)S(1)} %slice.267), channel_id=1, source_target_pairs={{0,2},{1,5},{2,0},{3,7},{4,6},{5,1},{6,4},{7,3},{8,10},{9,13},{10,... | collective-permute-start | bytes 344072 | tf_op jit(solution)/shard_map/ppermute | solution.py:59
  96.4 6.6 %collective-permute-start.25 = (bf16[1,16,1792]{2,1,0:T(8,128)(2,1)S(1)}, bf16[1,16,1792]{2,1,0:T(8,128)(2,1)S(1)}, u32[]{:S(2)}, u32[]{:S(2)}) collective-permute-start(bf16[1,16,1792]{2,1,0:T(8,128)(2,1)S(1)} %slice.277), channel_id=1, source_target_pairs={{0,8},{1,9},{2,10},{3,11},{4,12},{5,13},{6,14},{7,15},{8,0},{9,1},... | collective-permute-start | bytes 172040 | tf_op jit(solution)/shard_map/ppermute | solution.py:59
  99.2 5.2 %collective-permute-start.21 = (bf16[1,16,1792]{2,1,0:T(8,128)(2,1)S(1)}, bf16[1,16,1792]{2,1,0:T(8,128)(2,1)S(1)}, u32[]{:S(2)}, u32[]{:S(2)}) collective-permute-start(bf16[1,16,1792]{2,1,0:T(8,128)(2,1)S(1)} %slice.269), channel_id=1, source_target_pairs={{0,8},{1,9},{2,10},{3,11},{4,12},{5,13},{6,14},{7,15},{8,0},{9,1},... | collective-permute-start | bytes 172040 | tf_op jit(solution)/shard_map/ppermute | solution.py:59
  (8 other events, 13.5 us)

commit v7 on v6

--- a/solution.py
+++ b/solution.py
@@ -356,6 +356,19 @@
     )(values, weights)
 
 
+def output_kernel(edges, out_edges, *refs):
+    out_ref = refs[-1]
+    residual_refs, sums = refs[: len(edges)], refs[len(edges) : -1]
+    for place, (start, stop) in enumerate(out_edges):
+        kept_ref, got_ref = sums[2 * place], sums[2 * place + 1]
+        for (low, high), residual_ref in zip(edges, residual_refs):
+            first, last = max(low, start), min(high, stop)
+            if first < last:
+                own, at = slice(first - low, last - low), slice(first - start, last - start)
+                total = kept_ref[0, :, at].astype(jnp.float32) + got_ref[0, :, at].astype(jnp.float32)
+                out_ref[:, first:last] = (residual_ref[:, own] + total).astype(jnp.bfloat16)
+
+
 def terms_kernel(edges, hidden_range, *refs):
     row_refs, (gate_ref, up_ref, *more, out_ref) = refs[: len(edges)], refs[len(edges) :]
     start, stop = hidden_range
@@ -568,9 +581,7 @@
             ]
     spread = placing.T
     outputs = []
-    residuals = jnp.concatenate(residuals, axis=1)
     for (low, high), produced in zip(out_edges, first_products):
-        residual = residuals[:, low:high]
         for (start, stop), part_rows in zip(ranges[1:], activated[1:]):
             produced = produced + jnp.dot(
                 part_rows, down_weights[start:stop, low:high], preferred_element_type=jnp.float32
@@ -582,11 +593,19 @@
             .astype(jnp.bfloat16)
             .reshape(ep_count, token_count, -1)
         )
-        for step in range(bits):
-            total = halved(array, step, ep_count)
-            array = total.astype(jnp.bfloat16)
-        outputs.append((residual + total[0]).astype(jnp.bfloat16))
-    return jnp.concatenate(outputs, axis=1)
+        for step in range(bits - 1):
+            array = halved(array, step, ep_count).astype(jnp.bfloat16)
+        got = lax.ppermute(array[1:], "ep", crossing(ep_count, bits - 1))
+        outputs.extend([array[:1], got])
+    vmem = pl.BlockSpec(memory_space=pltpu.VMEM)
+    return pl.pallas_call(
+        functools.partial(output_kernel, edges, out_edges),
+        out_shape=jax.ShapeDtypeStruct(hidden_in.shape, jnp.bfloat16),
+        in_specs=[vmem] * (len(residuals) + len(outputs)),
+        out_specs=vmem,
+        compiler_params=pltpu.CompilerParams(vmem_limit_bytes=4 << 20),
+        name="output",
+    )(*residuals, *outputs)
 
 
 def solution(mesh):

time: 105 us -> 105 us (level)
    ppermute x0 -> x2, waiting for transfers between devices: none -> 3.55 us  [shards(): got = lax.ppermute(array[1:], 'ep', crossing(ep_count, bits - 1))]
    ppermute x14 -> x12, waiting for transfers between devices: 17.8 us -> 14.2 us  [halved(): got = lax.ppermute(array[half:], 'ep', crossing(count, step))]
    ppermute x14 -> x12, starting transfers between devices: 14.8 us -> 11.3 us  [halved(): got = lax.ppermute(array[half:], 'ep', crossing(count, step))]
    ppermute x0 -> x2, starting transfers between devices: none -> 3.49 us  [shards(): got = lax.ppermute(array[1:], 'ep', crossing(ep_count, bits - 1))]
where the time goes in v7:
time: 105 us
  waiting for transfers between devices  45.7 us (44%)
  starting transfers between devices  31.7 us (30%)
  Pallas kernels  10.2 us (10%)
  local copies, waits for them, and re-layouts  9.28 us (9%)
  matrix products  3.9 us (4%)
  other arithmetic  3.57 us (3%)
    ppermute x12, waiting for transfers between devices, halved(): got = lax.ppermute(array[half:], 'ep', crossing(count, step))  14.2 us
    ppermute x12, starting transfers between devices, halved(): got = lax.ppermute(array[half:], 'ep', crossing(count, step))  11.3 us
    ppermute x6, waiting for transfers between devices, doubled(): lax.ppermute(array, 'ep', crossing(count, step))  11.3 us
    ppermute x2, waiting for transfers between devices, shards(): others = [lax.ppermute(both, 'ctx', swap) for both in sums]  10.5 us
    unnamed x26, local copies, waits for them, and re-layouts  8.84 us
    ppermute x2, starting transfers between devices, shards(): got = lax.ppermute(sent, 'ep', crossing(ep_count, bits - 1))  5.31 us
    ppermute x1, starting transfers between devices, shards(): blocks = [key_columns, lax.ppermute(key_columns, 'ctx', [(0, 1)])]  4.87 us
    ppermute x2, waiting for transfers between devices, shards(): got = lax.ppermute(sent, 'ep', crossing(ep_count, bits - 1))  3.99 us
  transfers between devices with their start and end apart: 26, of which 21 were waited for; matrix products, arithmetic and copies ran while one was open for 5% of the time, Pallas kernels for 4%

profile of v7, /device:TPU:0, one launch (start us, length us, event | category | flops | bytes accessed | tf_op | source)
XLA Modules:
  0.0 105.0 jit_solution(8605762536198136075)
XLA Ops:
  0.0 4.9 %collective-permute-start = (bf16[576,128]{1,0:T(8,128)(2,1)}, bf16[576,128]{1,0:T(8,128)(2,1)S(1)}, u32[]{:S(2)}, u32[]{:S(2)}) collective-permute-start(bf16[576,128]{1,0:T(8,128)(2,1)} %bitcast.50), channel_id=1, source_target_pairs={{0,16},{1,17},{2,18},{3,19},{4,20},{5,21},{6,22},{7,23},{8,24},{9,... | collective-permute-start | bytes 442376 | tf_op jit(solution)/shard_map/ppermute | solution.py:441
  4.9 1.3 %copy-done.1 = bf16[128,4608]{1,0:T(8,128)(2,1)S(1)} copy-done((bf16[128,4608]{1,0:T(8,128)(2,1)S(1)}, bf16[128,4608]{1,0:T(8,128)(2,1)}, u32[]{:S(2)}) %copy-start.1) | copy-done | bytes 1179672
  12.9 3.1 %copy-done = bf16[1024,3584]{1,0:T(8,128)(2,1)S(1)} copy-done((bf16[1024,3584]{1,0:T(8,128)(2,1)S(1)}, bf16[1024,3584]{1,0:T(8,128)(2,1)}, u32[]{:S(2)}) %copy-start) | copy-done | bytes 7340056
  16.5 2.1 %collective-permute-done.1 = bf16[128,1024]{1,0:T(8,128)(2,1)S(1)} collective-permute-done((bf16[128,1024]{1,0:T(8,128)(2,1)S(1)}, bf16[128,1024]{1,0:T(8,128)(2,1)S(1)}, u32[]{:S(2)}, u32[]{:S(2)}) %collective-permute-start.1) | collective-permute-done | bytes 262176 | tf_op jit(solution)/shard_map/ppermute | solution.py:452
  23.5 1.6 %collective-permute-start.7 = (bf16[4,16,1664]{2,1,0:T(8,128)(2,1)S(1)}, bf16[4,16,1664]{2,1,0:T(8,128)(2,1)S(1)}, u32[]{:S(2)}, u32[]{:S(2)}) collective-permute-start(bf16[4,16,1664]{2,1,0:T(8,128)(2,1)S(1)} %slice.237), channel_id=1, source_target_pairs={{0,4},{1,3},{2,6},{3,1},{4,0},{5,7},{6,2},{7,5},{8,12},{9,11},{10,... | collective-permute-start | bytes 638984 | tf_op jit(solution)/shard_map/ppermute | solution.py:59
  25.8 3.5 %collective-permute-done.7 = bf16[4,16,1664]{2,1,0:T(8,128)(2,1)S(1)} collective-permute-done((bf16[4,16,1664]{2,1,0:T(8,128)(2,1)S(1)}, bf16[4,16,1664]{2,1,0:T(8,128)(2,1)S(1)}, u32[]{:S(2)}, u32[]{:S(2)}) %collective-permute-start.7) | collective-permute-done | bytes 213024 | tf_op jit(solution)/shard_map/ppermute | solution.py:59
  29.4 1.6 %collective-permute-start.8 = (bf16[2,16,1664]{2,1,0:T(8,128)(2,1)S(1)}, bf16[2,16,1664]{2,1,0:T(8,128)(2,1)S(1)}, u32[]{:S(2)}, u32[]{:S(2)}) collective-permute-start(bf16[2,16,1664]{2,1,0:T(8,128)(2,1)S(1)} %slice.239), channel_id=1, source_target_pairs={{0,2},{1,5},{2,0},{3,7},{4,6},{5,1},{6,4},{7,3},{8,10},{9,13},{10,... | collective-permute-start | bytes 319496 | tf_op jit(solution)/shard_map/ppermute | solution.py:59
  31.0 1.6 %collective-permute-done.3 = bf16[4,16,1920]{2,1,0:T(8,128)(2,1)S(1)} collective-permute-done((bf16[4,16,1920]{2,1,0:T(8,128)(2,1)S(1)}, bf16[4,16,1920]{2,1,0:T(8,128)(2,1)S(1)}, u32[]{:S(2)}, u32[]{:S(2)}) %collective-permute-start.3) | collective-permute-done | bytes 245792 | tf_op jit(solution)/shard_map/ppermute | solution.py:59
  32.6 1.6 %collective-permute-start.4 = (bf16[2,16,1920]{2,1,0:T(8,128)(2,1)S(1)}, bf16[2,16,1920]{2,1,0:T(8,128)(2,1)S(1)}, u32[]{:S(2)}, u32[]{:S(2)}) collective-permute-start(bf16[2,16,1920]{2,1,0:T(8,128)(2,1)S(1)} %slice.231), channel_id=1, source_target_pairs={{0,2},{1,5},{2,0},{3,7},{4,6},{5,1},{6,4},{7,3},{8,10},{9,13},{10,... | collective-permute-start | bytes 368648 | tf_op jit(solution)/shard_map/ppermute | solution.py:59
  34.3 2.7 %collective-permute-start.9 = (bf16[2,16,1792]{2,1,0:T(8,128)(2,1)S(1)}, bf16[2,16,1792]{2,1,0:T(8,128)(2,1)S(1)}, u32[]{:S(2)}, u32[]{:S(2)}) collective-permute-start(bf16[2,16,1792]{2,1,0:T(8,128)(2,1)S(1)} %fusion.29), channel_id=1, source_target_pairs={{0,8},{1,9},{2,10},{3,11},{4,12},{5,13},{6,14},{7,15},{8,0},{9,1},... | collective-permute-start | bytes 344072 | tf_op jit(solution)/shard_map/ppermute | solution.py:498
  37.7 2.7 %collective-permute-start.5 = (bf16[2,16,1920]{2,1,0:T(8,128)(2,1)S(1)}, bf16[2,16,1920]{2,1,0:T(8,128)(2,1)S(1)}, u32[]{:S(2)}, u32[]{:S(2)}) collective-permute-start(bf16[2,16,1920]{2,1,0:T(8,128)(2,1)S(1)} %fusion.52.after_ref), channel_id=1, source_target_pairs={{0,8},{1,9},{2,10},{3,11},{4,12},{5,13},{6,14},{7,15},{8,0},{9,1},... | collective-permute-start | bytes 368648 | tf_op jit(solution)/shard_map/ppermute | solution.py:498
  41.0 1.6 %slice-done.5 = s8[4194304]{0:T(1024)(128)(4,1)S(1)} async-done(((s8[7340032]{0:T(1024)(128)(4,1)}), s8[4194304]{0:T(1024)(128)(4,1)S(1)}, s32[]{:S(2)}) %slice-start.5) | async-done | bytes 4194328
  43.1 4.0 %collective-permute-done.5.got_ref = bf16[2,16,1920]{2,1,0:T(8,128)(2,1)S(1)} collective-permute-done((bf16[2,16,1920]{2,1,0:T(8,128)(2,1)S(1)}, bf16[2,16,1920]{2,1,0:T(8,128)(2,1)S(1)}, u32[]{:S(2)}, u32[]{:S(2)}) %collective-permute-start.5) | collective-permute-done | bytes 122912 | tf_op jit(solution)/shard_map/ppermute | solution.py:498
  47.5 1.6 %collective-permute-start.10 = (bf16[2,16,1792]{2,1,0:T(8,128)(2,1)S(1)}, bf16[2,16,1792]{2,1,0:T(8,128)(2,1)S(1)}, u32[]{:S(2)}, u32[]{:S(2)}) collective-permute-start(bf16[2,16,1792]{2,1,0:T(8,128)(2,1)S(1)} %get-tuple-element.54), channel_id=1, source_target_pairs={{0,2},{1,5},{2,0},{3,7},{4,6},{5,1},{6,4},{7,3},{8,10},{9,13},{10,... | collective-permute-start | bytes 344072 | tf_op jit(solution)/shard_map/ppermute | solution.py:64
  49.6 2.8 %collective-permute-done.10 = bf16[2,16,1792]{2,1,0:T(8,128)(2,1)S(1)} collective-permute-done((bf16[2,16,1792]{2,1,0:T(8,128)(2,1)S(1)}, bf16[2,16,1792]{2,1,0:T(8,128)(2,1)S(1)}, u32[]{:S(2)}, u32[]{:S(2)}) %collective-permute-start.10) | collective-permute-done | bytes 114720 | tf_op jit(solution)/shard_map/ppermute | solution.py:64
  53.1 1.9 %collective-permute-done.13 = bf16[2,16,1920]{2,1,0:T(8,128)(2,1)S(1)} collective-permute-done((bf16[2,16,1920]{2,1,0:T(8,128)(2,1)S(1)}, bf16[2,16,1920]{2,1,0:T(8,128)(2,1)S(1)}, u32[]{:S(2)}, u32[]{:S(2)}) %collective-permute-start.13) | collective-permute-done | bytes 122912 | tf_op jit(solution)/shard_map/ppermute | solution.py:64
  55.5 2.9 %collective-permute-done.11 = bf16[4,16,1792]{2,1,0:T(8,128)(2,1)S(1)} collective-permute-done((bf16[4,16,1792]{2,1,0:T(8,128)(2,1)S(1)}, bf16[4,16,1792]{2,1,0:T(8,128)(2,1)S(1)}, u32[]{:S(2)}, u32[]{:S(2)}) %collective-permute-start.11) | collective-permute-done | bytes 229408 | tf_op jit(solution)/shard_map/ppermute | solution.py:64
  58.6 2.7 %collective-permute-done.14 = bf16[4,16,1920]{2,1,0:T(8,128)(2,1)S(1)} collective-permute-done((bf16[4,16,1920]{2,1,0:T(8,128)(2,1)S(1)}, bf16[4,16,1920]{2,1,0:T(8,128)(2,1)S(1)}, u32[]{:S(2)}, u32[]{:S(2)}) %collective-permute-start.14) | collective-permute-done | bytes 245792 | tf_op jit(solution)/shard_map/ppermute | solution.py:64
  63.8 1.4 %hidden_terms.2 = bf16[144,1152]{1,0:T(8,128)(2,1)S(1)} custom-call(bf16[144,1920]{1,0:T(8,128)(2,1)S(1)} %convolution_convert_fusion.3.refs_0_, bf16[144,1664]{1,0:T(8,128)(2,1)S(1)} %convolution_convert_fusion.2.refs_1_, bf16[3584,1024]{1,0:T(8,128)(2,1)S(1)} %fetch_weights.5.refs_2_, bf16[3584,1024]{1,0:T(8,128)(2,1)S(1)} %fetch_weights.6.refs_3_, ...), custom_call_target="tpu_custom_call" | custom-call | tf_op jit(solution)/shard_map/hidden_terms/pallas_call | solution.py:393
  65.8 1.3 %hidden_terms.3.after_ref = bf16[144,1024]{1,0:T(8,128)(2,1)S(1)} custom-call(bf16[144,1920]{1,0:T(8,128)(2,1)S(1)} %convolution_convert_fusion.3.refs_0_, bf16[144,1664]{1,0:T(8,128)(2,1)S(1)} %convolution_convert_fusion.2.refs_1_, bf16[3584,1024]{1,0:T(8,128)(2,1)S(1)} %fetch_weights.5.refs_2_, bf16[3584,1024]{1,0:T(8,128)(2,1)S(1)} %fetch_weights.6.refs_3_), custom_call_target="tpu_custom_call" | custom-call | tf_op jit(solution)/shard_map/hidden_terms/pallas_call | solution.py:393
  67.1 1.6 %collective-permute-start.16 = (bf16[144,1024]{1,0:T(8,128)(2,1)S(1)}, bf16[144,1024]{1,0:T(8,128)(2,1)S(1)}, u32[]{:S(2)}, u32[]{:S(2)}) collective-permute-start(bf16[144,1024]{1,0:T(8,128)(2,1)S(1)} %hidden_terms.3.after_ref), channel_id=1, source_target_pairs={{0,16},{16,0},{1,17},{17,1},{2,18},{18,2},{3,19},{19,3},{4,20},{20... | collective-permute-start | bytes 884744 | tf_op jit(solution)/shard_map/ppermute | solution.py:546
  69.5 6.4 %collective-permute-done.17 = bf16[144,1152]{1,0:T(8,128)(2,1)S(1)} collective-permute-done((bf16[144,1152]{1,0:T(8,128)(2,1)S(1)}, bf16[144,1152]{1,0:T(8,128)(2,1)S(1)}, u32[]{:S(2)}, u32[]{:S(2)}) %collective-permute-start.17) | collective-permute-done | bytes 331808 | tf_op jit(solution)/shard_map/ppermute | solution.py:546
  77.2 4.1 %collective-permute-done.16 = bf16[144,1024]{1,0:T(8,128)(2,1)S(1)} collective-permute-done((bf16[144,1024]{1,0:T(8,128)(2,1)S(1)}, bf16[144,1024]{1,0:T(8,128)(2,1)S(1)}, u32[]{:S(2)}, u32[]{:S(2)}) %collective-permute-start.16) | collective-permute-done | bytes 294944 | tf_op jit(solution)/shard_map/ppermute | solution.py:546
  86.0 1.5 %collective-permute-start.19 = (bf16[4,16,1792]{2,1,0:T(8,128)(2,1)S(1)}, bf16[4,16,1792]{2,1,0:T(8,128)(2,1)S(1)}, u32[]{:S(2)}, u32[]{:S(2)}) collective-permute-start(bf16[4,16,1792]{2,1,0:T(8,128)(2,1)S(1)} %slice.257), channel_id=1, source_target_pairs={{0,4},{1,3},{2,6},{3,1},{4,0},{5,7},{6,2},{7,5},{8,12},{9,11},{10,... | collective-permute-start | bytes 688136 | tf_op jit(solution)/shard_map/ppermute | solution.py:59
  87.6 3.8 %collective-permute-done.23 = bf16[4,16,1792]{2,1,0:T(8,128)(2,1)S(1)} collective-permute-done((bf16[4,16,1792]{2,1,0:T(8,128)(2,1)S(1)}, bf16[4,16,1792]{2,1,0:T(8,128)(2,1)S(1)}, u32[]{:S(2)}, u32[]{:S(2)}) %collective-permute-start.23) | collective-permute-done | bytes 229408 | tf_op jit(solution)/shard_map/ppermute | solution.py:59
  91.4 1.3 %collective-permute-start.24 = (bf16[2,16,1792]{2,1,0:T(8,128)(2,1)S(1)}, bf16[2,16,1792]{2,1,0:T(8,128)(2,1)S(1)}, u32[]{:S(2)}, u32[]{:S(2)}) collective-permute-start(bf16[2,16,1792]{2,1,0:T(8,128)(2,1)S(1)} %slice.267), channel_id=1, source_target_pairs={{0,2},{1,5},{2,0},{3,7},{4,6},{5,1},{6,4},{7,3},{8,10},{9,13},{10,... | collective-permute-start | bytes 344072 | tf_op jit(solution)/shard_map/ppermute | solution.py:59
  92.8 1.4 %collective-permute-done.19 = bf16[4,16,1792]{2,1,0:T(8,128)(2,1)S(1)} collective-permute-done((bf16[4,16,1792]{2,1,0:T(8,128)(2,1)S(1)}, bf16[4,16,1792]{2,1,0:T(8,128)(2,1)S(1)}, u32[]{:S(2)}, u32[]{:S(2)}) %collective-permute-start.19) | collective-permute-done | bytes 229408 | tf_op jit(solution)/shard_map/ppermute | solution.py:59
  94.3 1.3 %collective-permute-start.20 = (bf16[2,16,1792]{2,1,0:T(8,128)(2,1)S(1)}, bf16[2,16,1792]{2,1,0:T(8,128)(2,1)S(1)}, u32[]{:S(2)}, u32[]{:S(2)}) collective-permute-start(bf16[2,16,1792]{2,1,0:T(8,128)(2,1)S(1)} %slice.259), channel_id=1, source_target_pairs={{0,2},{1,5},{2,0},{3,7},{4,6},{5,1},{6,4},{7,3},{8,10},{9,13},{10,... | collective-permute-start | bytes 344072 | tf_op jit(solution)/shard_map/ppermute | solution.py:59
  96.4 1.9 %collective-permute-start.25 = (bf16[1,16,1792]{2,1,0:T(8,128)(2,1)S(1)}, bf16[1,16,1792]{2,1,0:T(8,128)(2,1)S(1)}, u32[]{:S(2)}, u32[]{:S(2)}) collective-permute-start(bf16[1,16,1792]{2,1,0:T(8,128)(2,1)S(1)} %get-tuple-element.81), channel_id=1, source_target_pairs={{0,8},{1,9},{2,10},{3,11},{4,12},{5,13},{6,14},{7,15},{8,0},{9,1},... | collective-permute-start | bytes 172040 | tf_op jit(solution)/shard_map/ppermute | solution.py:598
  99.2 1.6 %collective-permute-start.21 = (bf16[1,16,1792]{2,1,0:T(8,128)(2,1)S(1)}, bf16[1,16,1792]{2,1,0:T(8,128)(2,1)S(1)}, u32[]{:S(2)}, u32[]{:S(2)}) collective-permute-start(bf16[1,16,1792]{2,1,0:T(8,128)(2,1)S(1)} %get-tuple-element.83), channel_id=1, source_target_pairs={{0,8},{1,9},{2,10},{3,11},{4,12},{5,13},{6,14},{7,15},{8,0},{9,1},... | collective-permute-start | bytes 172040 | tf_op jit(solution)/shard_map/ppermute | solution.py:598
  100.8 2.2 %collective-permute-done.25.refs_5_ = bf16[1,16,1792]{2,1,0:T(8,128)(2,1)S(1)} collective-permute-done((bf16[1,16,1792]{2,1,0:T(8,128)(2,1)S(1)}, bf16[1,16,1792]{2,1,0:T(8,128)(2,1)S(1)}, u32[]{:S(2)}, u32[]{:S(2)}) %collective-permute-start.25) | collective-permute-done | bytes 57376 | tf_op jit(solution)/shard_map/ppermute | solution.py:598
  103.0 1.4 %collective-permute-done.21.refs_3_ = bf16[1,16,1792]{2,1,0:T(8,128)(2,1)S(1)} collective-permute-done((bf16[1,16,1792]{2,1,0:T(8,128)(2,1)S(1)}, bf16[1,16,1792]{2,1,0:T(8,128)(2,1)S(1)}, u32[]{:S(2)}, u32[]{:S(2)}) %collective-permute-start.21) | collective-permute-done | bytes 57376 | tf_op jit(solution)/shard_map/ppermute | solution.py:598
  (137 shorter events, 29.1 us)
Async XLA Ops:
  0.0 9.6 %collective-permute-start = (bf16[576,128]{1,0:T(8,128)(2,1)}, bf16[576,128]{1,0:T(8,128)(2,1)S(1)}, u32[]{:S(2)}, u32[]{:S(2)}) collective-permute-start(bf16[576,128]{1,0:T(8,128)(2,1)} %bitcast.50), channel_id=1, source_target_pairs={{0,16},{1,17},{2,18},{3,19},{4,20},{5,21},{6,22},{7,23},{8,24},{9,... | collective-permute-start | bytes 442376 | tf_op jit(solution)/shard_map/ppermute | solution.py:441
  10.8 7.8 %collective-permute-start.1 = (bf16[128,1024]{1,0:T(8,128)(2,1)S(1)}, bf16[128,1024]{1,0:T(8,128)(2,1)S(1)}, u32[]{:S(2)}, u32[]{:S(2)}) collective-permute-start(bf16[128,1024]{1,0:T(8,128)(2,1)S(1)} %attention.1.after_ref), channel_id=1, source_target_pairs={{0,16},{16,0},{1,17},{17,1},{2,18},{18,2},{3,19},{19,3},{4,20},{20... | collective-permute-start | bytes 786440 | tf_op jit(solution)/shard_map/ppermute | solution.py:452
  20.3 14.0 %copy-start.5 = (bf16[16,3584]{1,0:T(8,128)(2,1)S(1)}, bf16[16,3584]{1,0:T(8,128)(2,1)}, u32[]{:S(2)}) copy-start(bf16[16,3584]{1,0:T(8,128)(2,1)} %param.17) | copy-start | bytes 344068
  20.3 20.1 %slice-start.2 = ((s8[7340032]{0:T(1024)(128)(4,1)}), s8[4194304]{0:T(1024)(128)(4,1)S(1)}, s32[]{:S(2)}) async-start(s8[7340032]{0:T(1024)(128)(4,1)} %bitcast.44), calls=%async_computation.2 | async-start | bytes 8388608
  21.5 18.9 %slice-start.3 = ((s8[7340032]{0:T(1024)(128)(4,1)}), s8[3145728]{0:T(1024)(128)(4,1)S(1)}, s32[]{:S(2)}) async-start(s8[7340032]{0:T(1024)(128)(4,1)} %bitcast.44), calls=%async_computation.3 | async-start | bytes 6291456
  21.5 1.8 %collective-permute-start.6 = (bf16[8,16,1664]{2,1,0:T(8,128)(2,1)S(1)}, bf16[8,16,1664]{2,1,0:T(8,128)(2,1)S(1)}, u32[]{:S(2)}, u32[]{:S(2)}) collective-permute-start(bf16[8,16,1664]{2,1,0:T(8,128)(2,1)S(1)} %bitcast.64), channel_id=1, source_target_pairs={{0,1},{1,0},{2,3},{3,2},{4,5},{5,4},{6,7},{7,6},{8,9},{9,8},{10,11... | collective-permute-start | bytes 1277960 | tf_op jit(solution)/shard_map/ppermute | solution.py:59
  21.7 3.4 %collective-permute-start.2 = (bf16[8,16,1920]{2,1,0:T(8,128)(2,1)S(1)}, bf16[8,16,1920]{2,1,0:T(8,128)(2,1)S(1)}, u32[]{:S(2)}, u32[]{:S(2)}) collective-permute-start(bf16[8,16,1920]{2,1,0:T(8,128)(2,1)S(1)} %bitcast.61), channel_id=1, source_target_pairs={{0,1},{1,0},{2,3},{3,2},{4,5},{5,4},{6,7},{7,6},{8,9},{9,8},{10,11... | collective-permute-start | bytes 1474568 | tf_op jit(solution)/shard_map/ppermute | solution.py:59
  23.5 5.9 %collective-permute-start.7 = (bf16[4,16,1664]{2,1,0:T(8,128)(2,1)S(1)}, bf16[4,16,1664]{2,1,0:T(8,128)(2,1)S(1)}, u32[]{:S(2)}, u32[]{:S(2)}) collective-permute-start(bf16[4,16,1664]{2,1,0:T(8,128)(2,1)S(1)} %slice.237), channel_id=1, source_target_pairs={{0,4},{1,3},{2,6},{3,1},{4,0},{5,7},{6,2},{7,5},{8,12},{9,11},{10,... | collective-permute-start | bytes 638984 | tf_op jit(solution)/shard_map/ppermute | solution.py:59
  25.3 7.3 %collective-permute-start.3 = (bf16[4,16,1920]{2,1,0:T(8,128)(2,1)S(1)}, bf16[4,16,1920]{2,1,0:T(8,128)(2,1)S(1)}, u32[]{:S(2)}, u32[]{:S(2)}) collective-permute-start(bf16[4,16,1920]{2,1,0:T(8,128)(2,1)S(1)} %slice.229), channel_id=1, source_target_pairs={{0,4},{1,3},{2,6},{3,1},{4,0},{5,7},{6,2},{7,5},{8,12},{9,11},{10,... | collective-permute-start | bytes 737288 | tf_op jit(solution)/shard_map/ppermute | solution.py:59
  29.4 4.8 %collective-permute-start.8 = (bf16[2,16,1664]{2,1,0:T(8,128)(2,1)S(1)}, bf16[2,16,1664]{2,1,0:T(8,128)(2,1)S(1)}, u32[]{:S(2)}, u32[]{:S(2)}) collective-permute-start(bf16[2,16,1664]{2,1,0:T(8,128)(2,1)S(1)} %slice.239), channel_id=1, source_target_pairs={{0,2},{1,5},{2,0},{3,7},{4,6},{5,1},{6,4},{7,3},{8,10},{9,13},{10,... | collective-permute-start | bytes 319496 | tf_op jit(solution)/shard_map/ppermute | solution.py:59
  32.6 4.9 %collective-permute-start.4 = (bf16[2,16,1920]{2,1,0:T(8,128)(2,1)S(1)}, bf16[2,16,1920]{2,1,0:T(8,128)(2,1)S(1)}, u32[]{:S(2)}, u32[]{:S(2)}) collective-permute-start(bf16[2,16,1920]{2,1,0:T(8,128)(2,1)S(1)} %slice.231), channel_id=1, source_target_pairs={{0,2},{1,5},{2,0},{3,7},{4,6},{5,1},{6,4},{7,3},{8,10},{9,13},{10,... | collective-permute-start | bytes 368648 | tf_op jit(solution)/shard_map/ppermute | solution.py:59
  34.3 12.9 %collective-permute-start.9 = (bf16[2,16,1792]{2,1,0:T(8,128)(2,1)S(1)}, bf16[2,16,1792]{2,1,0:T(8,128)(2,1)S(1)}, u32[]{:S(2)}, u32[]{:S(2)}) collective-permute-start(bf16[2,16,1792]{2,1,0:T(8,128)(2,1)S(1)} %fusion.29), channel_id=1, source_target_pairs={{0,8},{1,9},{2,10},{3,11},{4,12},{5,13},{6,14},{7,15},{8,0},{9,1},... | collective-permute-start | bytes 344072 | tf_op jit(solution)/shard_map/ppermute | solution.py:498
  37.6 3.3 %slice-start.4 = ((s8[7340032]{0:T(1024)(128)(4,1)}), s8[3145728]{0:T(1024)(128)(4,1)S(1)}, s32[]{:S(2)}) async-start(s8[7340032]{0:T(1024)(128)(4,1)} %bitcast.47), calls=%async_computation.4 | async-start | bytes 6291456
  37.7 9.4 %collective-permute-start.5 = (bf16[2,16,1920]{2,1,0:T(8,128)(2,1)S(1)}, bf16[2,16,1920]{2,1,0:T(8,128)(2,1)S(1)}, u32[]{:S(2)}, u32[]{:S(2)}) collective-permute-start(bf16[2,16,1920]{2,1,0:T(8,128)(2,1)S(1)} %fusion.52.after_ref), channel_id=1, source_target_pairs={{0,8},{1,9},{2,10},{3,11},{4,12},{5,13},{6,14},{7,15},{8,0},{9,1},... | collective-permute-start | bytes 368648 | tf_op jit(solution)/shard_map/ppermute | solution.py:498
  47.5 4.9 %collective-permute-start.10 = (bf16[2,16,1792]{2,1,0:T(8,128)(2,1)S(1)}, bf16[2,16,1792]{2,1,0:T(8,128)(2,1)S(1)}, u32[]{:S(2)}, u32[]{:S(2)}) collective-permute-start(bf16[2,16,1792]{2,1,0:T(8,128)(2,1)S(1)} %get-tuple-element.54), channel_id=1, source_target_pairs={{0,2},{1,5},{2,0},{3,7},{4,6},{5,1},{6,4},{7,3},{8,10},{9,13},{10,... | collective-permute-start | bytes 344072 | tf_op jit(solution)/shard_map/ppermute | solution.py:64
  49.0 6.0 %collective-permute-start.13 = (bf16[2,16,1920]{2,1,0:T(8,128)(2,1)S(1)}, bf16[2,16,1920]{2,1,0:T(8,128)(2,1)S(1)}, u32[]{:S(2)}, u32[]{:S(2)}) collective-permute-start(bf16[2,16,1920]{2,1,0:T(8,128)(2,1)S(1)} %get-tuple-element.55), channel_id=1, source_target_pairs={{0,2},{1,5},{2,0},{3,7},{4,6},{5,1},{6,4},{7,3},{8,10},{9,13},{10,... | collective-permute-start | bytes 368648 | tf_op jit(solution)/shard_map/ppermute | solution.py:64
  52.4 6.1 %collective-permute-start.11 = (bf16[4,16,1792]{2,1,0:T(8,128)(2,1)S(1)}, bf16[4,16,1792]{2,1,0:T(8,128)(2,1)S(1)}, u32[]{:S(2)}, u32[]{:S(2)}) collective-permute-start(bf16[4,16,1792]{2,1,0:T(8,128)(2,1)S(1)} %pad_maximum_fusion.6), channel_id=1, source_target_pairs={{0,4},{1,3},{2,6},{3,1},{4,0},{5,7},{6,2},{7,5},{8,12},{9,11},{10,... | collective-permute-start | bytes 688136 | tf_op jit(solution)/shard_map/ppermute | solution.py:64
  55.0 6.3 %collective-permute-start.14 = (bf16[4,16,1920]{2,1,0:T(8,128)(2,1)S(1)}, bf16[4,16,1920]{2,1,0:T(8,128)(2,1)S(1)}, u32[]{:S(2)}, u32[]{:S(2)}) collective-permute-start(bf16[4,16,1920]{2,1,0:T(8,128)(2,1)S(1)} %pad_maximum_fusion.5), channel_id=1, source_target_pairs={{0,4},{1,3},{2,6},{3,1},{4,0},{5,7},{6,2},{7,5},{8,12},{9,11},{10,... | collective-permute-start | bytes 737288 | tf_op jit(solution)/shard_map/ppermute | solution.py:64
  58.5 2.9 %collective-permute-start.12 = (bf16[8,16,1792]{2,1,0:T(8,128)(2,1)S(1)}, bf16[8,16,1792]{2,1,0:T(8,128)(2,1)S(1)}, u32[]{:S(2)}, u32[]{:S(2)}) collective-permute-start(bf16[8,16,1792]{2,1,0:T(8,128)(2,1)S(1)} %pad_maximum_fusion.3), channel_id=1, source_target_pairs={{0,1},{1,0},{2,3},{3,2},{4,5},{5,4},{6,7},{7,6},{8,9},{9,8},{10,11... | collective-permute-start | bytes 1376264 | tf_op jit(solution)/shard_map/ppermute | solution.py:64
  61.4 1.9 %collective-permute-start.15 = (bf16[8,16,1920]{2,1,0:T(8,128)(2,1)S(1)}, bf16[8,16,1920]{2,1,0:T(8,128)(2,1)S(1)}, u32[]{:S(2)}, u32[]{:S(2)}) collective-permute-start(bf16[8,16,1920]{2,1,0:T(8,128)(2,1)S(1)} %pad_maximum_fusion.2), channel_id=1, source_target_pairs={{0,1},{1,0},{2,3},{3,2},{4,5},{5,4},{6,7},{7,6},{8,9},{9,8},{10,11... | collective-permute-start | bytes 1474568 | tf_op jit(solution)/shard_map/ppermute | solution.py:64
  63.4 5.3 %slice-start = ((s8[7340032]{0:T(1024)(128)(4,1)}), s8[4194304]{0:T(1024)(128)(4,1)S(1)}, s32[]{:S(2)}) async-start(s8[7340032]{0:T(1024)(128)(4,1)} %bitcast.41), calls=%async_computation | async-start | bytes 8388608
  63.8 5.0 %slice-start.1 = ((s8[7340032]{0:T(1024)(128)(4,1)}), s8[3145728]{0:T(1024)(128)(4,1)S(1)}, s32[]{:S(2)}) async-start(s8[7340032]{0:T(1024)(128)(4,1)} %bitcast.41), calls=%async_computation.1 | async-start | bytes 6291456
  65.1 10.7 %collective-permute-start.17 = (bf16[144,1152]{1,0:T(8,128)(2,1)S(1)}, bf16[144,1152]{1,0:T(8,128)(2,1)S(1)}, u32[]{:S(2)}, u32[]{:S(2)}) collective-permute-start(bf16[144,1152]{1,0:T(8,128)(2,1)S(1)} %hidden_terms.2), channel_id=1, source_target_pairs={{0,16},{16,0},{1,17},{17,1},{2,18},{18,2},{3,19},{19,3},{4,20},{20... | collective-permute-start | bytes 995336 | tf_op jit(solution)/shard_map/ppermute | solution.py:546
  67.1 14.2 %collective-permute-start.16 = (bf16[144,1024]{1,0:T(8,128)(2,1)S(1)}, bf16[144,1024]{1,0:T(8,128)(2,1)S(1)}, u32[]{:S(2)}, u32[]{:S(2)}) collective-permute-start(bf16[144,1024]{1,0:T(8,128)(2,1)S(1)} %hidden_terms.3.after_ref), channel_id=1, source_target_pairs={{0,16},{16,0},{1,17},{17,1},{2,18},{18,2},{3,19},{19,3},{4,20},{20... | collective-permute-start | bytes 884744 | tf_op jit(solution)/shard_map/ppermute | solution.py:546
  83.3 1.9 %collective-permute-start.22 = (bf16[8,16,1792]{2,1,0:T(8,128)(2,1)S(1)}, bf16[8,16,1792]{2,1,0:T(8,128)(2,1)S(1)}, u32[]{:S(2)}, u32[]{:S(2)}) collective-permute-start(bf16[8,16,1792]{2,1,0:T(8,128)(2,1)S(1)} %bitcast.63), channel_id=1, source_target_pairs={{0,1},{1,0},{2,3},{3,2},{4,5},{5,4},{6,7},{7,6},{8,9},{9,8},{10,11... | collective-permute-start | bytes 1376264 | tf_op jit(solution)/shard_map/ppermute | solution.py:59
  83.9 2.0 %collective-permute-start.18 = (bf16[8,16,1792]{2,1,0:T(8,128)(2,1)S(1)}, bf16[8,16,1792]{2,1,0:T(8,128)(2,1)S(1)}, u32[]{:S(2)}, u32[]{:S(2)}) collective-permute-start(bf16[8,16,1792]{2,1,0:T(8,128)(2,1)S(1)} %bitcast.62), channel_id=1, source_target_pairs={{0,1},{1,0},{2,3},{3,2},{4,5},{5,4},{6,7},{7,6},{8,9},{9,8},{10,11... | collective-permute-start | bytes 1376264 | tf_op jit(solution)/shard_map/ppermute | solution.py:59
  85.3 6.1 %collective-permute-start.23 = (bf16[4,16,1792]{2,1,0:T(8,128)(2,1)S(1)}, bf16[4,16,1792]{2,1,0:T(8,128)(2,1)S(1)}, u32[]{:S(2)}, u32[]{:S(2)}) collective-permute-start(bf16[4,16,1792]{2,1,0:T(8,128)(2,1)S(1)} %slice.265), channel_id=1, source_target_pairs={{0,4},{1,3},{2,6},{3,1},{4,0},{5,7},{6,2},{7,5},{8,12},{9,11},{10,... | collective-permute-start | bytes 688136 | tf_op jit(solution)/shard_map/ppermute | solution.py:59
  86.0 8.2 %collective-permute-start.19 = (bf16[4,16,1792]{2,1,0:T(8,128)(2,1)S(1)}, bf16[4,16,1792]{2,1,0:T(8,128)(2,1)S(1)}, u32[]{:S(2)}, u32[]{:S(2)}) collective-permute-start(bf16[4,16,1792]{2,1,0:T(8,128)(2,1)S(1)} %slice.257), channel_id=1, source_target_pairs={{0,4},{1,3},{2,6},{3,1},{4,0},{5,7},{6,2},{7,5},{8,12},{9,11},{10,... | collective-permute-start | bytes 688136 | tf_op jit(solution)/shard_map/ppermute | solution.py:59
  91.4 4.9 %collective-permute-start.24 = (bf16[2,16,1792]{2,1,0:T(8,128)(2,1)S(1)}, bf16[2,16,1792]{2,1,0:T(8,128)(2,1)S(1)}, u32[]{:S(2)}, u32[]{:S(2)}) collective-permute-start(bf16[2,16,1792]{2,1,0:T(8,128)(2,1)S(1)} %slice.267), channel_id=1, source_target_pairs={{0,2},{1,5},{2,0},{3,7},{4,6},{5,1},{6,4},{7,3},{8,10},{9,13},{10,... | collective-permute-start | bytes 344072 | tf_op jit(solution)/shard_map/ppermute | solution.py:59
  94.3 4.9 %collective-permute-start.20 = (bf16[2,16,1792]{2,1,0:T(8,128)(2,1)S(1)}, bf16[2,16,1792]{2,1,0:T(8,128)(2,1)S(1)}, u32[]{:S(2)}, u32[]{:S(2)}) collective-permute-start(bf16[2,16,1792]{2,1,0:T(8,128)(2,1)S(1)} %slice.259), channel_id=1, source_target_pairs={{0,2},{1,5},{2,0},{3,7},{4,6},{5,1},{6,4},{7,3},{8,10},{9,13},{10,... | collective-permute-start | bytes 344072 | tf_op jit(solution)/shard_map/ppermute | solution.py:59
  96.4 6.6 %collective-permute-start.25 = (bf16[1,16,1792]{2,1,0:T(8,128)(2,1)S(1)}, bf16[1,16,1792]{2,1,0:T(8,128)(2,1)S(1)}, u32[]{:S(2)}, u32[]{:S(2)}) collective-permute-start(bf16[1,16,1792]{2,1,0:T(8,128)(2,1)S(1)} %get-tuple-element.81), channel_id=1, source_target_pairs={{0,8},{1,9},{2,10},{3,11},{4,12},{5,13},{6,14},{7,15},{8,0},{9,1},... | collective-permute-start | bytes 172040 | tf_op jit(solution)/shard_map/ppermute | solution.py:598
  99.2 5.2 %collective-permute-start.21 = (bf16[1,16,1792]{2,1,0:T(8,128)(2,1)S(1)}, bf16[1,16,1792]{2,1,0:T(8,128)(2,1)S(1)}, u32[]{:S(2)}, u32[]{:S(2)}) collective-permute-start(bf16[1,16,1792]{2,1,0:T(8,128)(2,1)S(1)} %get-tuple-element.83), channel_id=1, source_target_pairs={{0,8},{1,9},{2,10},{3,11},{4,12},{5,13},{6,14},{7,15},{8,0},{9,1},... | collective-permute-start | bytes 172040 | tf_op jit(solution)/shard_map/ppermute | solution.py:598
  (8 other events, 13.5 us)
